TPU v7x, 32 devices: a whole 2x2x4 slice. The times are simulated.
32 devices in a mesh: order: 4 (over z), heads: 2 (over core), seq: 4 (over y, x).
Axes of the slice: x: 2, y: 2, z: 4, core: 2. Of those that a mesh axis runs over, the one named last changes fastest.
Arguments:
- tokens: bfloat16 [4, 2048, 1024], P('seq', 'order'), may hold values from -6 to 6
- cotangent: bfloat16 [4, 2048, 1024], P('seq', 'order'), may hold values from -1 to 1
- node_order: int32 [4, 2048], P('seq', 'order'), may hold values from 0 to 2047, as said below
- decays: float32 [4, 2048, 32], P('seq', 'order', 'heads'), may hold values from 0.4 to 1, as said below
- w_inner: bfloat16 [1024, 2048], P(None, 'heads'), may hold values from -0.1875 to 0.1875
- w_state: bfloat16 [1024, 256], replicated, may hold values from -0.015625 to 0.015625
- w_out: bfloat16 [1024, 2048], P(None, 'heads'), may hold values from -0.125 to 0.125
Outputs:
- d_tokens: bfloat16 [4, 2048, 1024], P('seq', 'order', 'heads')
- d_w_inner: float32 [1024, 2048], P(('order', 'seq'), 'heads')
- d_w_state: float32 [1024, 256], P(('order', 'heads', 'seq'))
- d_w_out: float32 [1024, 2048], P(('order', 'seq'), 'heads')
Inputs may be any that keep to these rules, and one draw needn't show every extreme that they name: `node_order`: within each aligned block of 512 positions of a sequence, the entries are a permutation of that block's positions. `decays`: decay factors of each position and head.
All inputs are finite; a program needn't handle non-finite values.
Results may differ from a plain program's by a relative error of at most 0.0057.
Values sent between devices are 32-bit elements; how exact they have to be, the bound alone decides.
No kernel may reach another device: no remote copies, remote signals or barrier semaphores. Data moves between devices by JAX's collectives and lax.ppermute only.
A program may use at most 128 MiB of HBM per device.

v0:
```python
import jax
import jax.numpy as jnp
from jax import lax
from jax.sharding import PartitionSpec as P

Q = 256


highest = lax.Precision.HIGHEST


def carried_in(value, axis, join, neutral, backward):
    count, mine = (lax.axis_size(axis), lax.axis_index(axis))
    pieces = jax.tree.map(lambda part: lax.all_gather(part, axis), value)
    if backward:
        pieces = jax.tree.map(lambda part: part[::-1], pieces)
        mine = count - 1 - mine
    subtotal = jax.tree.map(
        lambda part, zero: jnp.full_like(part, 0) + jnp.asarray(zero, part.dtype), value, neutral
    )

    def lap(position, subtotal):
        longer = join(subtotal, jax.tree.map(lambda part: part[position], pieces))
        return jax.tree.map(lambda new, old: jnp.where(position < mine, new, old), longer, subtotal)

    return lax.fori_loop(0, count - 1, lap, subtotal)


def decay_table(log_rates):
    cumulative = jnp.cumsum(log_rates, axis=0).T
    length = log_rates.shape[0]
    causal = (jnp.arange(length)[:, None] >= jnp.arange(length)[None, :])[None]
    spread = cumulative[:, :, None] - cumulative[:, None, :]
    decay_mask = jnp.where(causal, jnp.exp(jnp.where(causal, spread, 0.0)), 0.0)
    return (cumulative, decay_mask)


def block_states(inner_x, b_mat, c_mat, inner_dy, log_rates):
    cumulative = jnp.cumsum(log_rates, axis=0).T
    last_sum = cumulative[:, -1]
    to_end = jnp.exp(last_sum[:, None] - cumulative).T
    from_start = jnp.exp(cumulative).T
    forward_part = jnp.einsum("shp,sn->hpn", inner_x * to_end[:, :, None], b_mat, precision=highest)
    backward_part = jnp.einsum(
        "shp,sn->hpn", inner_dy * from_start[:, :, None], c_mat, precision=highest
    )
    return (last_sum, forward_part, backward_part)


def block_outputs(inner_x, b_mat, c_mat, inner_dy, log_rates, state_in, adjoint_in):
    cumulative, decay_mask = decay_table(log_rates)
    last_sum = cumulative[:, -1:]
    grow_in = jnp.exp(cumulative).T[:, :, None]
    decay_out = jnp.exp(last_sum - cumulative).T[:, :, None]
    scores = jnp.dot(c_mat, b_mat.T, precision=highest)
    weights = decay_mask * scores[None]
    out_y = jnp.einsum("hts,shp->thp", weights, inner_x, precision=highest)
    out_y = out_y + jnp.einsum("hpn,tn->thp", state_in, c_mat, precision=highest) * grow_in
    out_dx = jnp.einsum("hst,shp->thp", weights, inner_dy, precision=highest)
    out_dx = out_dx + jnp.einsum("hpn,tn->thp", adjoint_in, b_mat, precision=highest) * decay_out
    pair_dots = jnp.einsum("thp,shp->hts", inner_dy, inner_x, precision=highest)
    masked = decay_mask * pair_dots
    out_dc = jnp.einsum("hts,sn->tn", masked, b_mat, precision=highest)
    out_dc = out_dc + jnp.einsum("hpn,thp->tn", state_in, inner_dy * grow_in, precision=highest)
    out_db = jnp.einsum("hst,sn->tn", masked, c_mat, precision=highest)
    out_db = out_db + jnp.einsum("hpn,thp->tn", adjoint_in, inner_x * decay_out, precision=highest)
    return (out_y, out_dx, out_db, out_dc)


def combine_pairs(earlier, later):
    return (earlier[0] * later[0], later[0][:, :, None, None] * earlier[1] + later[1])


def per_device(tokens, cotangent, node_order, decays, w_inner, w_state, w_out):
    seq_count, row_count, model_width = tokens.shape
    head_count = decays.shape[2]
    inner_dev = w_inner.shape[1]
    head_size = inner_dev // head_count
    state_size = w_state.shape[1] // 2
    block_count = row_count // Q
    total_blocks = seq_count * block_count
    offsets = node_order - lax.axis_index("order") * row_count
    ordered = jnp.take_along_axis(tokens, offsets[:, :, None], axis=1)
    ordered_grad = jnp.take_along_axis(cotangent, offsets[:, :, None], axis=1)
    flat_in = ordered.reshape(seq_count * row_count, model_width)
    flat_grad = ordered_grad.reshape(seq_count * row_count, model_width)
    inner_x = jnp.dot(flat_in, w_inner, preferred_element_type=jnp.float32).astype(jnp.bfloat16)
    proj_bc = jnp.dot(flat_in, w_state, preferred_element_type=jnp.float32).astype(jnp.bfloat16)
    inner_dy = jnp.dot(flat_grad, w_out, preferred_element_type=jnp.float32).astype(jnp.bfloat16)
    log_rates = jnp.log(decays)
    x_blocks = inner_x.astype(jnp.float32).reshape(total_blocks, Q, head_count, head_size)
    b_blocks = proj_bc[:, :state_size].astype(jnp.float32).reshape(total_blocks, Q, state_size)
    c_blocks = proj_bc[:, state_size:].astype(jnp.float32).reshape(total_blocks, Q, state_size)
    dy_blocks = inner_dy.astype(jnp.float32).reshape(total_blocks, Q, head_count, head_size)
    rate_blocks = log_rates.reshape(total_blocks, Q, head_count)
    block_sums, forward_parts, backward_parts = jax.vmap(block_states)(
        x_blocks, b_blocks, c_blocks, dy_blocks, rate_blocks
    )
    block_sums = block_sums.reshape(seq_count, block_count, head_count)
    forward_parts = forward_parts.reshape(seq_count, block_count, head_count, head_size, state_size)
    backward_parts = backward_parts.reshape(
        seq_count, block_count, head_count, head_size, state_size
    )
    empty_state = jnp.zeros((seq_count, head_count, head_size, state_size), jnp.float32)
    running = empty_state
    factor = jnp.ones((seq_count, head_count), jnp.float32)
    start_parts = []
    start_factors = []
    for position in range(block_count):
        start_parts.append(running)
        start_factors.append(factor)
        step_decay = jnp.exp(block_sums[:, position])
        running = step_decay[:, :, None, None] * running + forward_parts[:, position]
        factor = factor * step_decay
    back_running = empty_state
    back_factor = jnp.ones((seq_count, head_count), jnp.float32)
    after_parts = []
    after_factors = []
    for position in reversed(range(block_count)):
        after_parts.insert(0, back_running)
        after_factors.insert(0, back_factor)
        step_decay = jnp.exp(block_sums[:, position])
        back_running = step_decay[:, :, None, None] * back_running + backward_parts[:, position]
        back_factor = back_factor * step_decay
    identity = (jnp.ones_like(factor), jnp.zeros_like(running))
    incoming = carried_in((factor, running), "order", combine_pairs, identity, False)[1]
    returning = carried_in((factor, back_running), "order", combine_pairs, identity, True)[1]
    starts = (
        jnp.stack(start_parts, axis=1)
        + jnp.stack(start_factors, axis=1)[:, :, :, None, None] * incoming[:, None]
    )
    afters = (
        jnp.stack(after_parts, axis=1)
        + jnp.stack(after_factors, axis=1)[:, :, :, None, None] * returning[:, None]
    )
    starts = starts.reshape(total_blocks, head_count, head_size, state_size)
    afters = afters.reshape(total_blocks, head_count, head_size, state_size)
    out_y, out_dx, out_db, out_dc = jax.vmap(block_outputs)(
        x_blocks, b_blocks, c_blocks, dy_blocks, rate_blocks, starts, afters
    )
    token_rows = seq_count * row_count
    recomputed = out_y.reshape(token_rows, inner_dev).astype(jnp.bfloat16)
    grad_x = out_dx.reshape(token_rows, inner_dev).astype(jnp.bfloat16)
    grad_bc = jnp.concatenate([out_db, out_dc], axis=-1).reshape(token_rows, 2 * state_size)
    contract_rows = (((0,), (0,)), ((), ()))
    contract_cols = (((1,), (1,)), ((), ()))
    partial_sums = lax.psum_scatter(
        jnp.concatenate(
            [
                lax.dot_general(flat_in, grad_x, contract_rows, preferred_element_type=jnp.float32),
                lax.dot_general(
                    flat_grad, recomputed, contract_rows, preferred_element_type=jnp.float32
                ),
            ],
            axis=1,
        ),
        "order",
        scatter_dimension=0,
        tiled=True,
    )
    summed = lax.psum_scatter(partial_sums, "seq", scatter_dimension=0, tiled=True)
    d_w_inner = summed[:, :inner_dev]
    d_w_out = summed[:, inner_dev:]
    bc_term = lax.dot_general(
        flat_in.astype(jnp.float32), grad_bc, contract_rows, precision=highest
    )
    d_w_state = lax.psum_scatter(
        bc_term, ("order", "heads", "seq"), scatter_dimension=0, tiled=True
    )
    dx_term = lax.dot_general(grad_x, w_inner, contract_cols, preferred_element_type=jnp.float32)
    dx_term = dx_term + lax.dot_general(
        grad_bc, w_state.astype(jnp.float32), contract_cols, precision=highest
    )
    ordered_back = lax.psum_scatter(dx_term, "heads", scatter_dimension=1, tiled=True).astype(
        jnp.bfloat16
    )
    ordered_back = ordered_back.reshape(seq_count, row_count, -1)
    d_tokens = jax.vmap(
        lambda target_rows, values: jnp.zeros_like(values).at[target_rows].set(values)
    )(offsets, ordered_back)
    return (d_tokens, d_w_inner, d_w_state, d_w_out)


def solution(mesh):
    in_specs = (
        P("seq", "order", None),
        P("seq", "order", None),
        P("seq", "order"),
        P("seq", "order", "heads"),
        P(None, "heads"),
        P(),
        P(None, "heads"),
    )
    out_specs = (
        P("seq", "order", "heads"),
        P(("order", "seq"), "heads"),
        P(("order", "heads", "seq"), None),
        P(("order", "seq"), "heads"),
    )
    return jax.shard_map(
        per_device, mesh=mesh, in_specs=in_specs, out_specs=out_specs, check_vma=False
    )
```

profile of v0, /device:TPU:0, one launch (start us, length us, event | category | flops | bytes accessed | tf_op | source)
XLA Modules:
  0.0 488.8 jit_solution(4851031095743908612)
XLA Ops:
  10.6 4.9 gather_fusion.1
  17.5 2.8 gather_fusion
  20.2 3.2 convolution_convert_fusion.1
  23.5 2.3 reshape.284
  25.8 3.5 copy.62
  29.3 2.5 fusion.27
  33.0 2.3 convolution_convert_fusion
  35.3 4.0 reshape.285
  39.4 2.8 copy.67
  44.6 12.8 %all_gather.6 = f32[4,1,16]{2,1,0:T(1,128)S(1)} all-gather(f32[1,1,16]{2,1,0:T(1,128)S(1)} %get-tuple-element.282), channel_id=1, replica_groups=mesh['order'=4,'heads'=2,'seq'=4] {'order'}, dimensions={0}, use_global_device_ids=true | all-gather | bytes 320 | tf_op jit(solution)/shard_map/all_gather | solution.py:14
  59.1 22.6 %all-gather.3.cloned.1.call-done = f32[4,1,16,64,128]{4,3,2,1,0:T(8,128)} async-done(((f32[1,1,16,64,128]{4,3,2,1,0:T(8,128)}), f32[4,1,16,64,128]{4,3,2,1,0:T(8,128)}) %all-gather.3.cloned.1.call-update) | async-done | bytes 2097168 | tf_op jit(solution)/shard_map/all_gather | solution.py:14
  81.7 3.2 rev.7
  84.9 3.6 while.28
  88.6 2.2 fusion.35
  90.9 5.9 %fusion.18 = bf16[2,256,16,64]{1,3,2,0:T(8,128)(2,1)S(1)} fusion(f32[2,256,16,64]{1,3,2,0:T(8,128)S(1)} %fusion.35, bf16[2,256,16,64]{1,3,2,0:T(8,128)(2,1)S(1)} %copy-done.4, f32[2,256,256]{2,1,0:T(8,128)S(1)} %copy-done.14, f32[2,16,256]{2,1,0:T(8,128)S(1)} %copy_bitcast_fusion, pred[256,256]{1,0:T(8,128)(4,1)S(1)} %copy-done.16, ...), kind=kOutput, calls=%fused_computation.28 | convolution fusion | flops 1620574208 | bytes 4849664 | tf_op jit(solution)/shard_map/vmap(hst,shp->thp)/dot_general | solution.py:59
  99.1 28.9 %all-gather.5.cloned.1.call-done = f32[4,1,16,64,128]{4,3,2,1,0:T(8,128)} async-done(((f32[1,1,16,64,128]{4,3,2,1,0:T(8,128)}), f32[4,1,16,64,128]{4,3,2,1,0:T(8,128)}) %all-gather.5.cloned.1.call-update) | async-done | bytes 2097168 | tf_op jit(solution)/shard_map/all_gather | solution.py:14
  128.0 3.6 while.29
  131.6 2.2 fusion.31
  133.8 6.9 %fusion.17 = bf16[2,256,16,64]{1,3,2,0:T(8,128)(2,1)S(1)} fusion(f32[2,256,16,64]{1,3,2,0:T(8,128)S(1)} %fusion.31, bf16[2,256,16,64]{1,3,2,0:T(8,128)(2,1)S(1)} %copy-done.7, f32[2,256,256]{2,1,0:T(8,128)S(1)} %copy-done.15, f32[2,16,256]{2,1,0:T(8,128)S(1)} %copy_bitcast_fusion, pred[256,256]{1,0:T(8,128)(4,1)S(1)} %copy-done.17, ...), kind=kOutput, calls=%fused_computation.26 | convolution fusion | flops 1620574208 | bytes 4849664 | tf_op jit(solution)/shard_map/vmap(hts,shp->thp)/dot_general | solution.py:57
  145.0 4.1 pad_maximum_fusion
  149.4 4.6 multiply_reduce_fusion
  154.1 2.2 fusion.30
  156.3 2.2 fusion.29
  159.6 2.6 fusion.76
  162.2 2.4 convolution_add_fusion
  164.7 127.8 %reduce-scatter.9.cloned.1.call-done = f32[256,2048]{0,1:T(8,128)} async-done(((f32[1024,2048]{0,1:T(8,128)}), f32[256,2048]{0,1:T(8,128)}) %reduce-scatter.9.cloned.1.call-update) | async-done | bytes 2097168 | tf_op jit(solution)/shard_map/reduce_scatter | solution.py:147
  292.5 2.9 copy.82
  295.8 3.5 fusion.37
  299.4 5.6 %reduce-scatter.7.cloned.1.call-done = f32[512,512]{1,0:T(8,128)} async-done(((f32[512,1024]{1,0:T(8,128)}), f32[512,512]{1,0:T(8,128)}) %reduce-scatter.7.cloned.1.call-update) | async-done | bytes 1048592 | tf_op jit(solution)/shard_map/reduce_scatter | solution.py:174
  305.0 3.8 scatter_custom_fusion
  308.8 35.7 %reduce-scatter.13.cloned.1.call-done = f32[64,2048]{1,0:T(8,128)} async-done(((f32[256,2048]{1,0:T(8,128)}), f32[64,2048]{1,0:T(8,128)}) %reduce-scatter.13.cloned.1.call-update) | async-done | bytes 524304
  346.3 135.6 %reduce-scatter.11.cloned.1.call-done = f32[32,256]{1,0:T(8,128)} async-done(((f32[1024,256]{1,0:T(8,128)}), f32[32,256]{1,0:T(8,128)}) %reduce-scatter.11.cloned.1.call-update) | async-done | bytes 32784 | tf_op jit(solution)/shard_map/reduce_scatter | solution.py:167
  (101 shorter events, 27.8 us)
Async XLA Ops:
  7.2 25.8 %copy-start = (bf16[1024,1024]{1,0:T(8,128)(2,1)S(1)}, bf16[1024,1024]{1,0:T(8,128)(2,1)}, u32[]{:S(2)}) copy-start(bf16[1024,1024]{1,0:T(8,128)(2,1)} %param.17) | copy-start | bytes 6291460
  7.2 74.6 %all-gather.3.cloned.1.call-start = ((), (), s32[]{:S(2)}) async-start(), calls=%async_computation.4 | async-start | bytes 2621440 | tf_op jit(solution)/shard_map/all_gather | solution.py:14
  15.5 2.0 copy-start.1
  29.3 3.7 copy-start.2
  32.9 95.0 %all-gather.5.cloned.1.call-start = ((), (), s32[]{:S(2)}) async-start(), calls=%async_computation.5 | async-start | bytes 2621440 | tf_op jit(solution)/shard_map/all_gather | solution.py:14
  42.1 2.3 copy-start.6
  44.5 248.0 %reduce-scatter.9.cloned.1.call-start = ((), (), s32[]{:S(2)}) async-start(), calls=%async_computation.7 | async-start | bytes 10485760 | tf_op jit(solution)/shard_map/reduce_scatter | solution.py:147
  88.6 2.3 copy-start.4
  88.6 2.3 copy-start.14
  88.6 2.3 copy-start.16
  131.6 2.2 copy-start.7
  131.6 2.2 copy-start.15
  131.6 2.2 copy-start.17
  140.8 1.3 copy-start.11
  142.1 1.4 copy-start.3
  142.1 1.5 copy-start.12
  149.1 155.8 %reduce-scatter.7.cloned.1.call-start = ((), (), s32[]{:S(2)}) async-start(), calls=%async_computation.6 | async-start | bytes 3145728 | tf_op jit(solution)/shard_map/reduce_scatter | solution.py:174
  149.4 4.6 copy-start.8
  149.4 4.6 copy-start.9
  154.1 2.3 copy-start.5
  154.1 2.3 copy-start.10
  159.6 2.6 copy-start.13
  164.7 179.8 %reduce-scatter.13.cloned.1.call-start = ((), (), s32[]{:S(2)}) async-start(), calls=%async_computation.9 | async-start | bytes 2621440
  295.4 3.9 copy-start.18
  295.4 186.5 %reduce-scatter.11.cloned.1.call-start = ((), (), s32[]{:S(2)}) async-start(), calls=%async_computation.8 | async-start | bytes 1081344 | tf_op jit(solution)/shard_map/reduce_scatter | solution.py:167
Sparse Core Ops, SparseCore 0:
  33.1 48.6 all-gather.2
  83.3 44.6 all-gather.4
  149.2 143.2 reduce-scatter.8
  294.6 10.3 reduce-scatter.6
  308.0 36.3 reduce-scatter.12
  347.1 134.7 reduce-scatter.10
where the time goes:
time: 490 us; the launch traced here: 489 us
  waiting for transfers between devices  356 us (73%)
  matrix products  50.4 us (10%)
  local copies, waits for them, and re-layouts  33.7 us (7%)
  other arithmetic  20 us (4%)
  between operations  14.7 us (3%)
  blocking collectives  12.8 us (3%)
    reduce_scatter x1, waiting for transfers between devices, per_device(): lax.psum_scatter(bc_term, ('order', 'heads', 'seq'), scatter_dimension=0,...  136 us
    reduce_scatter x1, waiting for transfers between devices, per_device(): lax.psum_scatter(jnp.concatenate([lax.dot_general(flat_in, grad_x, contra...  128 us
    all_gather x2, waiting for transfers between devices, carried_in(): pieces = jax.tree.map(lambda part: lax.all_gather(part, axis), value)  51.5 us
    unnamed x7, waiting for transfers between devices  35.8 us
    all_gather x1, blocking collectives, carried_in(): pieces = jax.tree.map(lambda part: lax.all_gather(part, axis), value)  12.8 us
  transfers between devices with their start and end apart: 6, of which 6 were waited for; matrix products, arithmetic and copies ran while one was open for 12% of the time, Pallas kernels for 0%

commit v1 on v0

v1 whole, which is shorter than its diff:
```python
import functools

import jax
import jax.numpy as jnp
from jax import lax
from jax.experimental import pallas as pl
from jax.experimental.pallas import tpu as pltpu
from jax.sharding import PartitionSpec as P

CHUNK = 128
GROUPS = 4
LIMIT = 48 * 1024 * 1024
f32 = jnp.float32
bf16 = jnp.bfloat16


def dot(a, b, ca=1, cb=0):
    return lax.dot_general(a, b, (((ca,), (cb,)), ((), ())), preferred_element_type=f32)


def log2(n):
    bits = n.bit_length() - 1
    assert 1 << bits == n
    return bits


def place(index, order):
    out = 0
    for rank, bit in enumerate(order):
        out = out + (((index >> bit) & 1) << (len(order) - 1 - rank))
    return out


def block_at(position, order):
    out = 0
    for rank, bit in enumerate(order):
        out |= ((position >> (len(order) - 1 - rank)) & 1) << bit
    return out


def spread(values, first, heads, size):
    total = values.shape[1]
    row = lax.broadcasted_iota(jnp.int32, (total, heads * size), 0)
    col = lax.broadcasted_iota(jnp.int32, (total, heads * size), 1)
    low = (row - first) * size
    pick = jnp.where((col >= low) & (col < low + size), 1.0, 0.0).astype(bf16)
    high = values.astype(bf16)
    rest = values - high.astype(f32)
    middle = rest.astype(bf16)
    last = (rest - middle.astype(f32)).astype(bf16)
    return dot(high, pick) + dot(middle, pick) + dot(last, pick)


def triangle(upper):
    row = lax.broadcasted_iota(jnp.int32, (CHUNK, CHUNK), 0)
    col = lax.broadcasted_iota(jnp.int32, (CHUNK, CHUNK), 1)
    return row <= col if upper else row >= col


def one_hot_rows(offsets, rows):
    node = lax.broadcasted_iota(jnp.int32, (rows, offsets.shape[1]), 0)
    return jnp.where(node == offsets, 1.0, 0.0).astype(bf16)


def order_kernel(x_order, y_order, ids, off, tokens, cot, decays, w_state,
                 ordered, ordered_grad, ordered_t, grad_t, sc, sb, cum):
    me, base = ids[0], ids[1]
    rows, width = tokens.shape
    blocks = 1 << len(x_order)
    size = width // blocks
    hot = one_hot_rows(off[...] - base, rows)
    half = width // 2
    for source, plain, turned, order in ((tokens, ordered, ordered_t, x_order), (cot, ordered_grad, grad_t, y_order)):
        plain[...] = dot(hot, source[...], 0, 0).astype(bf16)
        for part in range(2):
            value = dot(source[:, part * half:(part + 1) * half], hot, 0, 0).astype(bf16)
            for block in range(blocks // 2):
                where = place((block + part * (blocks // 2)) ^ me, order)
                turned[pl.ds(pl.multiple_of(where * size, size), size), :] = value[block * size:(block + 1) * size]
    bc = dot(ordered[...], w_state[...]).astype(bf16)
    state = bc.shape[1] // 2
    lower = triangle(False)
    upper = triangle(True)
    ones = jnp.where(lower, 1.0, 0.0)
    rates = jnp.log(decays[...])
    for k in range(rows // CHUNK):
        span = slice(k * CHUNK, (k + 1) * CHUNK)
        b, c = bc[span, :state], bc[span, state:]
        sc[span, :CHUNK] = jnp.where(lower, dot(c, b, 1, 1), 0.0).astype(bf16)
        sc[span, CHUNK:] = c
        sb[span, :CHUNK] = jnp.where(upper, dot(b, c, 1, 1), 0.0).astype(bf16)
        sb[span, CHUNK:] = b
        cum[span, :] = jnp.dot(ones, rates[span], precision=lax.Precision.HIGHEST, preferred_element_type=f32)


def chunk_rows(cum_x, k):
    part = cum_x[k * CHUNK:(k + 1) * CHUNK]
    return part, part[CHUNK // 2 - 1:CHUNK // 2], part[CHUNK - 1:CHUNK]


def states_kernel(first, heads, size, ordered, ordered_grad, w_inner, w_out, sc, sb, cum,
                  xs, ys, fwd, bwd, total):
    cum_x = spread(cum[...], first, heads, size)
    x = dot(ordered[...], w_inner[...]).astype(bf16).astype(f32)
    dy = dot(ordered_grad[...], w_out[...]).astype(bf16).astype(f32)
    count = cum_x.shape[0] // CHUNK
    forward, back, decay = [], [], []
    for k in range(count):
        span = slice(k * CHUNK, (k + 1) * CHUNK)
        part, mid, last = chunk_rows(cum_x, k)
        x_s = (x[span] * jnp.exp(mid - part)).astype(bf16)
        y_s = (dy[span] * jnp.exp(part - mid)).astype(bf16)
        xs[span, :] = x_s
        ys[span, :] = y_s
        forward.append(jnp.exp(last - mid) * dot(sb[span, CHUNK:], x_s, 0, 0))
        back.append(jnp.exp(mid) * dot(sc[span, CHUNK:], y_s, 0, 0))
        decay.append(jnp.exp(last))
    run, run_back, factor = forward[0], back[-1], decay[0]
    for k in range(1, count):
        run = decay[k] * run + forward[k]
        factor = factor * decay[k]
        run_back = decay[count - 1 - k] * run_back + back[count - 1 - k]
    fwd[...] = run
    bwd[...] = run_back
    total[...] = factor


def outputs_kernel(first, heads, size, xs, ys, sc, sb, cum, fwd_in, bwd_in, ordered_t, grad_t,
                   keep_in, send_in, keep_out, send_out, grad_x, grad_bc, y_all):
    cum_x = spread(cum[...], first, heads, size)
    count = cum_x.shape[0] // CHUNK
    lower = triangle(False)
    upper = triangle(True)
    starts, afters = [fwd_in[...]], [bwd_in[...]]
    for k in range(count - 1):
        span = slice(k * CHUNK, (k + 1) * CHUNK)
        _, mid, last = chunk_rows(cum_x, k)
        starts.append(jnp.exp(last) * starts[-1] + jnp.exp(last - mid) * dot(sb[span, CHUNK:], xs[span, :], 0, 0))
    for k in range(count - 1, 0, -1):
        span = slice(k * CHUNK, (k + 1) * CHUNK)
        _, mid, last = chunk_rows(cum_x, k)
        afters.insert(0, jnp.exp(last) * afters[0] + jnp.exp(mid) * dot(sc[span, CHUNK:], ys[span, :], 0, 0))
    for k in range(count):
        span = slice(k * CHUNK, (k + 1) * CHUNK)
        part, mid, last = chunk_rows(cum_x, k)
        x_s, y_s = xs[span, :], ys[span, :]
        x_rows = jnp.concatenate([x_s, (starts[k] * jnp.exp(mid)).astype(bf16)], axis=0)
        y_rows = jnp.concatenate([y_s, (afters[k] * jnp.exp(last - mid)).astype(bf16)], axis=0)
        y_all[span, :] = (jnp.exp(part - mid) * dot(sc[span, :], x_rows)).astype(bf16)
        grad_x[span, :] = (jnp.exp(mid - part) * dot(sb[span, :], y_rows)).astype(bf16)
        by_y = dot(y_s, x_rows, 1, 1)
        by_x = dot(x_s, y_rows, 1, 1)
        pairs = jnp.where(lower, by_y[:, :CHUNK], 0.0).astype(bf16)
        turned = jnp.where(upper, by_x[:, :CHUNK], 0.0).astype(bf16)
        state = by_x.shape[1] - CHUNK
        grad_bc[span, :state] = dot(turned, sc[span, CHUNK:]) + by_x[:, CHUNK:]
        grad_bc[span, state:] = dot(pairs, sb[span, CHUNK:]) + by_y[:, CHUNK:]
    half = ordered_t.shape[0] // 2
    send_in[...] = dot(ordered_t[half:, :], grad_x[...])
    send_out[...] = dot(grad_t[half:, :], y_all[...])
    keep_in[...] = dot(ordered_t[:half, :], grad_x[...])
    keep_out[...] = dot(grad_t[:half, :], y_all[...])


def back_kernel(groups, x_order, s_order, ids, *refs):
    grads, sums = refs[:groups], refs[groups:2 * groups]
    w_inner, w_state, ordered_t, keep, send, state_keep, state_send, table = refs[2 * groups:]
    me, side, me_state = ids[0], ids[2], ids[3]
    grad_bc = sums[0][...]
    for part in sums[1:]:
        grad_bc = grad_bc + part[...]
    grad_bc = grad_bc.astype(bf16)
    half = w_inner.shape[0] // 2
    for out, which in ((send, 1 - side), (keep, side)):
        rows = pl.ds(pl.multiple_of(which * half, half), half)
        value = dot(grad_bc, w_state[rows, :], 1, 1)
        start = 0
        for part in grads:
            cols = part.shape[1]
            value = value + dot(part[...], w_inner[rows, start:start + cols], 1, 1)
            start += cols
        out[...] = value
    blocks = 1 << len(x_order)
    size = ordered_t.shape[0] // blocks
    fine = ordered_t.shape[0] >> len(s_order)
    step = ordered_t.shape[0] // 4
    for quarter in range(4):
        value = dot(ordered_t[quarter * step:(quarter + 1) * step, :], grad_bc)
        for piece in range(step // fine):
            row = quarter * step + piece * fine
            block = block_at(row // size, x_order) ^ me
            index = block * (size // fine) + (row % size) // fine
            where = place(index ^ me_state, s_order)
            table[pl.ds(pl.multiple_of(where * fine, fine), fine), :] = value[piece * fine:(piece + 1) * fine]
    middle = ordered_t.shape[0] // 2
    state_keep[...] = table[:middle, :]
    state_send[...] = table[middle:, :]


def place_kernel(ids, off, keep, came, out):
    hot = one_hot_rows(off[...] - ids[1], out.shape[0])
    out[...] = dot(hot, (keep[...] + came[...]).astype(bf16)).astype(bf16)


def flips(axis, bit):
    return [(i, i ^ (1 << bit)) for i in range(lax.axis_size(axis))]


def halving(keep, send, hops):
    parts = [keep]
    for rank, (axis, bit) in enumerate(hops):
        parts.append(lax.ppermute(send, axis, flips(axis, bit)))
        rows = send.shape[0]
        if rank + 1 < len(hops):
            rows //= 2
            send = sum(part[rows:2 * rows] for part in parts[1:]) + parts[0][rows:2 * rows]
            parts = [part[:rows] for part in parts]
    out = parts[0]
    for part in parts[1:]:
        out = out + part
    return out


def carries(forward, back, total):
    count, mine = lax.axis_size("order"), lax.axis_index("order")
    run, run_back = jnp.zeros_like(forward), jnp.zeros_like(back)
    for k in range(1, count):
        up, down = total * run + forward, total * run_back + back
        if count % 2 == 0:
            message = jnp.where(mine == k - 1, up, down)
            came = came_back = lax.ppermute(message, "order", [(k - 1, k), (count - k, count - k - 1)])
        else:
            came = lax.ppermute(up, "order", [(k - 1, k)])
            came_back = lax.ppermute(down, "order", [(count - k, count - k - 1)])
        run = jnp.where(mine == k, came, run)
        run_back = jnp.where(mine == count - k - 1, came_back, run_back)
    return run, run_back


def whole(array):
    return pl.BlockSpec(array.shape, lambda *_: (0,) * len(array.shape))


def call(kernel, outs, args, name, scratch=(), specs=None, flops=0):
    specs = specs or {}
    in_specs = []
    for i, arg in enumerate(args):
        if i in specs:
            in_specs.append(specs[i])
        elif arg.dtype == jnp.int32 and arg.ndim == 1:
            in_specs.append(pl.BlockSpec(memory_space=pltpu.SMEM))
        else:
            in_specs.append(whole(arg))
    moved = sum(a.size * a.dtype.itemsize for a in list(args) + list(outs))
    return pl.pallas_call(
        kernel,
        out_shape=tuple(outs),
        grid=(1,),
        in_specs=in_specs,
        out_specs=tuple(whole(o) for o in outs),
        scratch_shapes=list(scratch),
        compiler_params=pltpu.CompilerParams(vmem_limit_bytes=LIMIT),
        cost_estimate=pl.CostEstimate(flops=int(flops), bytes_accessed=int(moved), transcendentals=0),
        name=name,
    )(*args)


def per_device(tokens, cotangent, node_order, decays, w_inner, w_state, w_out):
    assert tokens.shape[0] == 1
    tokens, cotangent, decays = tokens[0], cotangent[0], decays[0]
    rows, width = tokens.shape
    heads = decays.shape[1]
    inner = w_inner.shape[1]
    size = inner // heads
    state = w_state.shape[1] // 2
    cols = inner // GROUPS
    group_heads = heads // GROUPS
    n_order, n_heads, n_seq = (lax.axis_size(a) for a in ("order", "heads", "seq"))
    o, h, s = (lax.axis_index(a) for a in ("order", "heads", "seq"))
    seq_bits, head_bits, order_bits = log2(n_seq), log2(n_heads), log2(n_order)
    seq_hops = [("seq", b) for b in range(seq_bits)]
    order_hops = [("order", b) for b in range(order_bits)]
    x_hops = seq_hops + order_hops
    y_hops = seq_hops[::-1] + order_hops
    s_hops = [("heads", b) for b in range(head_bits)] + order_hops + seq_hops
    shift = {"seq": 0, "order": seq_bits}
    shift_state = {"seq": 0, "heads": seq_bits, "order": seq_bits + head_bits}
    x_order = [shift[a] + b for a, b in x_hops]
    y_order = [shift[a] + b for a, b in y_hops]
    s_order = [shift_state[a] + b for a, b in s_hops]
    ids = jnp.stack([o * n_seq + s, o * rows, h, (o * n_heads + h) * n_seq + s]).astype(jnp.int32)
    S = jax.ShapeDtypeStruct
    full = S((rows, width), bf16)
    turned = S((width, rows), bf16)
    wide = S((rows, CHUNK + state), bf16)
    ordered, ordered_grad, ordered_t, grad_t, sc, sb, cum = call(
        functools.partial(order_kernel, x_order, y_order),
        [full, full, turned, turned, wide, wide, S((rows, heads), f32)],
        [ids, node_order, tokens, cotangent, decays, w_state], "order",
        flops=10 * rows * rows * width)
    states = []
    for g in range(GROUPS):
        column = pl.BlockSpec((width, cols), functools.partial(lambda g, _: (0, g), g))
        states.append(call(
            functools.partial(states_kernel, g * group_heads, group_heads, size),
            [S((rows, cols), bf16)] * 2 + [S((state, cols), f32)] * 2 + [S((1, cols), f32)],
            [ordered, ordered_grad, w_inner, w_out, sc, sb, cum], f"states_{g}", specs={2: column, 3: column},
            flops=4 * rows * width * cols))
    in_parts, out_parts, grads, sums = [], [], [], []
    for g in range(GROUPS):
        xs, ys, fwd, bwd, total = states[g]
        run, run_back = carries(fwd, bwd, total)
        half = S((width // 2, cols), f32)
        keep_in, send_in, keep_out, send_out, grad_x, grad_bc = call(
            functools.partial(outputs_kernel, g * group_heads, group_heads, size),
            [half] * 4 + [S((rows, cols), bf16), S((rows, 2 * state), f32)],
            [xs, ys, sc, sb, cum, run, run_back, ordered_t, grad_t], f"outputs_{g}",
            scratch=[pltpu.VMEM((rows, cols), bf16)],
            flops=4 * rows * width * cols)
        in_parts.append(halving(keep_in, send_in, x_hops))
        out_parts.append(halving(keep_out, send_out, y_hops))
        grads.append(grad_x)
        sums.append(grad_bc)
    piece = S((rows, width // 2), f32)
    half_state = S((width // 2, 2 * state), f32)
    keep, send, state_keep, state_send = call(
        functools.partial(back_kernel, GROUPS, x_order, s_order),
        [piece, piece, half_state, half_state],
        [ids] + grads + sums + [w_inner, w_state, ordered_t], "back",
        scratch=[pltpu.VMEM((width, 2 * state), f32)],
        flops=2 * rows * width * inner)
    came = lax.ppermute(send, "heads", flips("heads", 0))
    d_tokens = call(place_kernel, [S((rows, width // 2), bf16)], [ids, node_order, keep, came], "place",
                    flops=rows * rows * width)[0]
    d_w_state = halving(state_keep, state_send, s_hops)
    d_w_inner = jnp.concatenate(in_parts, axis=1)
    d_w_out = jnp.concatenate(out_parts, axis=1)
    return d_tokens[None], d_w_inner, d_w_state, d_w_out


def solution(mesh):
    in_specs = (
        P("seq", "order", None),
        P("seq", "order", None),
        P("seq", "order"),
        P("seq", "order", "heads"),
        P(None, "heads"),
        P(),
        P(None, "heads"),
    )
    out_specs = (
        P("seq", "order", "heads"),
        P(("order", "seq"), "heads"),
        P(("order", "heads", "seq"), None),
        P(("order", "seq"), "heads"),
    )
    return jax.shard_map(
        per_device, mesh=mesh, in_specs=in_specs, out_specs=out_specs, check_vma=False
    )
```

time: 490 us -> 185 us (0.38)
  waiting for transfers between devices: 356 us -> 53.1 us
  starting transfers between devices: 0.73 us -> 56.6 us
  matrix products: 50.4 us -> 0 us
  Pallas kernels: 0 us -> 36.1 us
  local copies, waits for them, and re-layouts: 33.7 us -> 4.8 us
  between operations: 14.7 us -> 1.37 us
  blocking collectives: 12.8 us -> 0 us
  other arithmetic: 20 us -> 31.3 us
    reduce_scatter x3 -> x0, waiting for transfers between devices: 269 us -> none  [the longest x1 136 us: per_device(): lax.psum_scatter(bc_term, ('order', 'heads', 'seq'), scatter_dimension=0,...]
    ppermute x0 -> x50, starting transfers between devices: none -> 56.6 us  [the longest x37 36.9 us: halving(): parts.append(lax.ppermute(send, axis, flips(axis, bit)))]
    ppermute x0 -> x50, waiting for transfers between devices: none -> 53.1 us  [the longest x37 44.5 us: halving(): parts.append(lax.ppermute(send, axis, flips(axis, bit)))]
    all_gather x2 -> x0, waiting for transfers between devices: 51.5 us -> none  [carried_in(): pieces = jax.tree.map(lambda part: lax.all_gather(part, axis), value)]
    dot_general x20 -> x0, matrix products: 50.4 us -> none  [the longest x1 6.93 us: block_outputs(): out_y = jnp.einsum('hts,shp->thp', weights, inner_x, precision=highest)]
    pallas_call x0 -> x11, Pallas kernels: none -> 36.1 us  [call(): pl.pallas_call(kernel, out_shape=tuple(outs), grid=(1,), in_specs=in_spec...]
    unnamed x7 -> x0, waiting for transfers between devices: 35.8 us -> none
    add x2 -> x37, other arithmetic: 2.24 us -> 15.7 us  [the longest x28 11.5 us: halving(): sum((part[rows:2 * rows] for part in parts[1:])) + parts[0][rows:2 * rows]]
  transfers between devices with their start and end apart: 6 -> 50, of which waited for: 6 -> 20; matrix products, arithmetic and copies ran while one was open for 12% -> 17% of each run, Pallas kernels for 0% -> 14%
where the time goes in v1:
time: 185 us; the launch traced here: 183 us
  starting transfers between devices  56.6 us (31%)
  waiting for transfers between devices  53.1 us (29%)
  Pallas kernels  36.1 us (20%)
  other arithmetic  31.3 us (17%)
  local copies, waits for them, and re-layouts  4.8 us (3%)
    ppermute x37, waiting for transfers between devices, halving(): parts.append(lax.ppermute(send, axis, flips(axis, bit)))  44.5 us
    ppermute x37, starting transfers between devices, halving(): parts.append(lax.ppermute(send, axis, flips(axis, bit)))  36.9 us
    pallas_call x11, Pallas kernels, call(): pl.pallas_call(kernel, out_shape=tuple(outs), grid=(1,), in_specs=in_spec...  36.1 us
    ppermute x12, starting transfers between devices, carries(): lax.ppermute(message, 'order', [(k - 1, k), (count - k, count - k - 1)])  19.5 us
    add x28, other arithmetic, halving(): sum((part[rows:2 * rows] for part in parts[1:])) + parts[0][rows:2 * rows]  11.5 us
    select_n x12, other arithmetic, carries(): message = jnp.where(mine == k - 1, up, down)  10.3 us
    ppermute x12, waiting for transfers between devices, carries(): lax.ppermute(message, 'order', [(k - 1, k), (count - k, count - k - 1)])  8.55 us
    unnamed x41, local copies, waits for them, and re-layouts  4.8 us
  transfers between devices with their start and end apart: 50, of which 20 were waited for; matrix products, arithmetic and copies ran while one was open for 17% of the time, Pallas kernels for 14%

profile of v1, /device:TPU:0, one launch (start us, length us, event | category | flops | bytes accessed | tf_op | source)
XLA Modules:
  0.0 183.1 jit_solution(18407844364540862491)
XLA Ops:
  3.3 5.3 %order.1 = (bf16[512,1024]{1,0:T(8,128)(2,1)S(1)}, bf16[512,1024]{1,0:T(8,128)(2,1)S(1)}, bf16[1024,512]{1,0:T(8,128)(2,1)S(1)}, bf16[1024,512]{1,0:T(8,128)(2,1...) custom-call(s32[4]{0:T(128)S(1)} %pad_add_fusion.ids, ...), custom_call_target="tpu_custom_call" | custom-call | flops 2684354560 | bytes 7407632 | tf_op jit(solution)/shard_map/order/pallas_call | solution.py:255
  8.7 2.8 %states_3.1 = (bf16[512,256]{1,0:T(8,128)(2,1)S(1)}, bf16[512,256]{1,0:T(8,128)(2,1)S(1)}, f32[128,256]{1,0:T(8,128)S(1)}, f32[128,256]{1,0:T(8,128)S(1)}, f32[1,256]{1,0:T(1,128)S(1)}) custom-call(bf16[512,1024]{1,0:T(8,128)(2,1)S(1)} %get-tuple-element.59.ordered, bf16[512,1024]{1,0:T(8,128)(2,1)S(1)} %get-tuple-element.60.ordered_grad, ...), custom_call_target="tpu_custom_call" | custom-call | flops 536870912 | bytes 7635968 | tf_op jit(solution)/shard_map/states_3/pallas_call | solution.py:255
  12.3 5.6 %collective-permute-start.9 = (f32[128,256]{1,0:T(8,128)}, f32[128,256]{1,0:T(8,128)}, u32[]{:S(2)}, u32[]{:S(2)}) collective-permute-start(f32[128,256]{1,0:T(8,128)} %add_select_fusion.2), channel_id=1, source_target_pairs={{0,8},{24,16},{1,9},{25,17},{2,10},{26,18},{3,11},{27,19},{4,12},{... | collective-permute-start | bytes 393224 | tf_op jit(solution)/shard_map/ppermute | solution.py:231
  17.8 2.4 %states_2.1 = (bf16[512,256]{1,0:T(8,128)(2,1)S(1)}, bf16[512,256]{1,0:T(8,128)(2,1)S(1)}, f32[128,256]{1,0:T(8,128)S(1)}, f32[128,256]{1,0:T(8,128)S(1)}, f32[1,256]{1,0:T(1,128)S(1)}) custom-call(bf16[512,1024]{1,0:T(8,128)(2,1)S(1)} %get-tuple-element.59.ordered, bf16[512,1024]{1,0:T(8,128)(2,1)S(1)} %get-tuple-element.60.ordered_grad, ...), custom_call_target="tpu_custom_call" | custom-call | flops 536870912 | bytes 7635968 | tf_op jit(solution)/shard_map/states_2/pallas_call | solution.py:255
  20.9 1.9 %collective-permute-start.6 = (f32[128,256]{1,0:T(8,128)}, f32[128,256]{1,0:T(8,128)}, u32[]{:S(2)}, u32[]{:S(2)}) collective-permute-start(f32[128,256]{1,0:T(8,128)} %add_select_fusion.5), channel_id=1, source_target_pairs={{0,8},{24,16},{1,9},{25,17},{2,10},{26,18},{3,11},{27,19},{4,12},{... | collective-permute-start | bytes 393224 | tf_op jit(solution)/shard_map/ppermute | solution.py:231
  22.8 2.4 %states_1.1 = (bf16[512,256]{1,0:T(8,128)(2,1)S(1)}, bf16[512,256]{1,0:T(8,128)(2,1)S(1)}, f32[128,256]{1,0:T(8,128)S(1)}, f32[128,256]{1,0:T(8,128)S(1)}, f32[1,256]{1,0:T(1,128)S(1)}) custom-call(bf16[512,1024]{1,0:T(8,128)(2,1)S(1)} %get-tuple-element.59.ordered, bf16[512,1024]{1,0:T(8,128)(2,1)S(1)} %get-tuple-element.60.ordered_grad, ...), custom_call_target="tpu_custom_call" | custom-call | flops 536870912 | bytes 7635968 | tf_op jit(solution)/shard_map/states_1/pallas_call | solution.py:255
  26.7 1.9 %collective-permute-start.3 = (f32[128,256]{1,0:T(8,128)}, f32[128,256]{1,0:T(8,128)}, u32[]{:S(2)}, u32[]{:S(2)}) collective-permute-start(f32[128,256]{1,0:T(8,128)} %add_select_fusion.8), channel_id=1, source_target_pairs={{0,8},{24,16},{1,9},{25,17},{2,10},{26,18},{3,11},{27,19},{4,12},{... | collective-permute-start | bytes 393224 | tf_op jit(solution)/shard_map/ppermute | solution.py:231
  28.7 2.4 %states_0.1 = (bf16[512,256]{1,0:T(8,128)(2,1)S(1)}, bf16[512,256]{1,0:T(8,128)(2,1)S(1)}, f32[128,256]{1,0:T(8,128)S(1)}, f32[128,256]{1,0:T(8,128)S(1)}, f32[1,256]{1,0:T(1,128)S(1)}) custom-call(bf16[512,1024]{1,0:T(8,128)(2,1)S(1)} %get-tuple-element.59.ordered, bf16[512,1024]{1,0:T(8,128)(2,1)S(1)} %get-tuple-element.60.ordered_grad, ...), custom_call_target="tpu_custom_call" | custom-call | flops 536870912 | bytes 7635968 | tf_op jit(solution)/shard_map/states_0/pallas_call | solution.py:255
  33.2 1.9 %collective-permute-start = (f32[128,256]{1,0:T(8,128)}, f32[128,256]{1,0:T(8,128)}, u32[]{:S(2)}, u32[]{:S(2)}) collective-permute-start(f32[128,256]{1,0:T(8,128)} %add_select_fusion.11), channel_id=1, source_target_pairs={{0,8},{24,16},{1,9},{25,17},{2,10},{26,18},{3,11},{27,19},{4,12},{... | collective-permute-start | bytes 393224 | tf_op jit(solution)/shard_map/ppermute | solution.py:231
  51.0 8.5 %collective-permute-done.2 = f32[128,256]{1,0:T(8,128)S(1)} collective-permute-done((f32[128,256]{1,0:T(8,128)S(1)}, f32[128,256]{1,0:T(8,128)S(1)}, u32[]{:S(2)}, u32[]{:S(2)}) %collective-permute-start.2) | collective-permute-done | bytes 131104 | tf_op jit(solution)/shard_map/ppermute | solution.py:231
  60.5 3.6 %outputs_0.1 = (f32[512,256]{1,0:T(8,128)S(1)}, f32[512,256]{1,0:T(8,128)S(1)}, f32[512,256]{1,0:T(8,128)S(1)}, f32[512,256]{1,0:T(8,128)S(1)}, bf16[512,256]{1,0:T(8,128)(2,1)S(1)}, /*index=5*/f32[512,256]{1,0:T(8,128)S(1)}) custom-call(bf16[512,256]{1,0:T(8,128)(2,1)S(1)} %copy-done.14, bf16[512,256]{1,0:T(8,128)(2,1)S(1)} %copy-done.16, ...), custom_call_target="tpu_custom_call" | custom-call | flops 536870912 | bytes 6324224 | tf_op jit(solution)/shard_map/outputs_0/pallas_call | solution.py:255
  68.2 3.5 %outputs_1.1 = (f32[512,256]{1,0:T(8,128)S(1)}, f32[512,256]{1,0:T(8,128)S(1)}, f32[512,256]{1,0:T(8,128)S(1)}, f32[512,256]{1,0:T(8,128)S(1)}, bf16[512,256]{1,0:T(8,128)(2,1)S(1)}, /*index=5*/f32[512,256]{1,0:T(8,128)S(1)}) custom-call(bf16[512,256]{1,0:T(8,128)(2,1)S(1)} %copy-done.10, bf16[512,256]{1,0:T(8,128)(2,1)S(1)} %copy-done.12, ...), custom_call_target="tpu_custom_call" | custom-call | flops 536870912 | bytes 6324224 | tf_op jit(solution)/shard_map/outputs_1/pallas_call | solution.py:255
  74.7 3.5 %outputs_2.1 = (f32[512,256]{1,0:T(8,128)S(1)}, f32[512,256]{1,0:T(8,128)S(1)}, f32[512,256]{1,0:T(8,128)S(1)}, f32[512,256]{1,0:T(8,128)S(1)}, bf16[512,256]{1,0:T(8,128)(2,1)S(1)}, /*index=5*/f32[512,256]{1,0:T(8,128)S(1)}) custom-call(bf16[512,256]{1,0:T(8,128)(2,1)S(1)} %get-tuple-element.78.xs, bf16[512,256]{1,0:T(8,128)(2,1)S(1)} %get-tuple-element.79.ys, ...), custom_call_target="tpu_custom_call" | custom-call | flops 536870912 | bytes 6324224 | tf_op jit(solution)/shard_map/outputs_2/pallas_call | solution.py:255
  78.2 3.6 %outputs_3.1 = (f32[512,256]{1,0:T(8,128)S(1)}, f32[512,256]{1,0:T(8,128)S(1)}, f32[512,256]{1,0:T(8,128)S(1)}, f32[512,256]{1,0:T(8,128)S(1)}, bf16[512,256]{1,0:T(8,128)(2,1)S(1)}, /*index=5*/f32[512,256]{1,0:T(8,128)S(1)}) custom-call(bf16[512,256]{1,0:T(8,128)(2,1)S(1)} %get-tuple-element.84.xs, bf16[512,256]{1,0:T(8,128)(2,1)S(1)} %get-tuple-element.85.ys, ...), custom_call_target="tpu_custom_call" | custom-call | flops 536870912 | bytes 6324224 | tf_op jit(solution)/shard_map/outputs_3/pallas_call | solution.py:255
  81.8 4.7 %back.1 = (f32[512,512]{1,0:T(8,128)S(1)}, f32[512,512]{1,0:T(8,128)}, f32[512,256]{1,0:T(8,128)S(1)}, f32[512,256]{1,0:T(8,128)S(1)}) custom-call(s32[4]{0:T(128)S(1)} %pad_add_fusion.ids, bf16[512,256]{1,0:T(8,128)(2,1)S(1)} %get-tuple-element.71.refs_0_, bf16[512,256]{1,0:T(8,128)(2,1)S(1)} %get-tuple-element.77.refs_1_, ...), custom_call_target="tpu_custom_call" | custom-call | flops 1073741824 | bytes 9961488 | tf_op jit(solution)/shard_map/back/pallas_call | solution.py:255
  89.1 1.6 collective-permute-start.46
  95.0 6.4 %collective-permute-done.25 = f32[512,256]{1,0:T(8,128)S(1)} collective-permute-done((f32[512,256]{1,0:T(8,128)S(1)}, f32[512,256]{1,0:T(8,128)S(1)}, u32[]{:S(2)}, u32[]{:S(2)}) %collective-permute-start.25) | collective-permute-done | bytes 524320 | tf_op jit(solution)/shard_map/ppermute | solution.py:212
  104.5 8.1 %collective-permute-done.21 = f32[512,256]{1,0:T(8,128)S(1)} collective-permute-done((f32[512,256]{1,0:T(8,128)S(1)}, f32[512,256]{1,0:T(8,128)S(1)}, u32[]{:S(2)}, u32[]{:S(2)}) %collective-permute-start.21) | collective-permute-done | bytes 524320 | tf_op jit(solution)/shard_map/ppermute | solution.py:212
  115.8 5.0 %collective-permute-done.14 = f32[256,256]{1,0:T(8,128)S(1)} collective-permute-done((f32[256,256]{1,0:T(8,128)S(1)}, f32[256,256]{1,0:T(8,128)S(1)}, u32[]{:S(2)}, u32[]{:S(2)}) %collective-permute-start.14) | collective-permute-done | bytes 262176 | tf_op jit(solution)/shard_map/ppermute | solution.py:212
  121.8 1.6 collective-permute-start.26
  124.3 2.1 %collective-permute-done.18 = f32[256,256]{1,0:T(8,128)S(1)} collective-permute-done((f32[256,256]{1,0:T(8,128)S(1)}, f32[256,256]{1,0:T(8,128)S(1)}, u32[]{:S(2)}, u32[]{:S(2)}) %collective-permute-start.18) | collective-permute-done | bytes 262176 | tf_op jit(solution)/shard_map/ppermute | solution.py:212
  133.1 2.2 %collective-permute-done.47 = f32[256,256]{1,0:T(8,128)S(1)} collective-permute-done((f32[256,256]{1,0:T(8,128)S(1)}, f32[256,256]{1,0:T(8,128)S(1)}, u32[]{:S(2)}, u32[]{:S(2)}) %collective-permute-start.47) | collective-permute-done | bytes 262176 | tf_op jit(solution)/shard_map/ppermute | solution.py:212
  139.1 2.9 %collective-permute-start.31 = (f32[128,256]{1,0:T(8,128)S(1)}, f32[128,256]{1,0:T(8,128)S(1)}, u32[]{:S(2)}, u32[]{:S(2)}) collective-permute-start(f32[128,256]{1,0:T(8,128)S(1)} %fusion.4), channel_id=1, source_target_pairs={{0,16},{8,24},{16,0},{24,8},{1,17},{9,25},{17,1},{25,9},{2,18},{10... | collective-permute-start | bytes 393224 | tf_op jit(solution)/shard_map/ppermute | solution.py:212
  144.0 3.3 %collective-permute-done.19 = f32[128,256]{1,0:T(8,128)S(1)} collective-permute-done((f32[128,256]{1,0:T(8,128)S(1)}, f32[128,256]{1,0:T(8,128)S(1)}, u32[]{:S(2)}, u32[]{:S(2)}) %collective-permute-start.19) | collective-permute-done | bytes 131104 | tf_op jit(solution)/shard_map/ppermute | solution.py:212
  148.1 1.9 %collective-permute-done.40 = f32[128,256]{1,0:T(8,128)S(1)} collective-permute-done((f32[128,256]{1,0:T(8,128)S(1)}, f32[128,256]{1,0:T(8,128)S(1)}, u32[]{:S(2)}, u32[]{:S(2)}) %collective-permute-start.40) | collective-permute-done | bytes 131104 | tf_op jit(solution)/shard_map/ppermute | solution.py:212
  151.1 1.9 %collective-permute-start.44 = (f32[128,256]{1,0:T(8,128)S(1)}, f32[128,256]{1,0:T(8,128)S(1)}, u32[]{:S(2)}, u32[]{:S(2)}) collective-permute-start(f32[128,256]{1,0:T(8,128)S(1)} %fusion.1), channel_id=1, source_target_pairs={{0,8},{8,0},{16,24},{24,16},{1,9},{9,1},{17,25},{25,17},{2,10},{10... | collective-permute-start | bytes 393224 | tf_op jit(solution)/shard_map/ppermute | solution.py:212
  154.3 2.1 %collective-permute-done.48 = f32[128,256]{1,0:T(8,128)S(1)} collective-permute-done((f32[128,256]{1,0:T(8,128)S(1)}, f32[128,256]{1,0:T(8,128)S(1)}, u32[]{:S(2)}, u32[]{:S(2)}) %collective-permute-start.48) | collective-permute-done | bytes 131104 | tf_op jit(solution)/shard_map/ppermute | solution.py:212
  157.0 4.2 %collective-permute-done.23 = f32[128,256]{1,0:T(8,128)S(1)} collective-permute-done((f32[128,256]{1,0:T(8,128)S(1)}, f32[128,256]{1,0:T(8,128)S(1)}, u32[]{:S(2)}, u32[]{:S(2)}) %collective-permute-start.23) | collective-permute-done | bytes 131104 | tf_op jit(solution)/shard_map/ppermute | solution.py:212
  167.7 2.1 %collective-permute-start.49 = (f32[64,256]{1,0:T(8,128)S(1)}, f32[64,256]{1,0:T(8,128)S(1)}, u32[]{:S(2)}, u32[]{:S(2)}) collective-permute-start(f32[64,256]{1,0:T(8,128)S(1)} %fusion.9), channel_id=1, source_target_pairs={{0,16},{8,24},{16,0},{24,8},{1,17},{9,25},{17,1},{25,9},{2,18},{10... | collective-permute-start | bytes 196616 | tf_op jit(solution)/shard_map/ppermute | solution.py:212
  172.6 2.9 %collective-permute-start.45 = (f32[64,256]{1,0:T(8,128)S(1)}, f32[64,256]{1,0:T(8,128)S(1)}, u32[]{:S(2)}, u32[]{:S(2)}) collective-permute-start(f32[64,256]{1,0:T(8,128)S(1)} %fusion.11), channel_id=1, source_target_pairs={{0,16},{8,24},{16,0},{24,8},{1,17},{9,25},{17,1},{25,9},{2,18},{10... | collective-permute-start | bytes 196616 | tf_op jit(solution)/shard_map/ppermute | solution.py:212
  175.5 2.8 %collective-permute-start.33 = (f32[32,256]{1,0:T(8,128)S(1)}, f32[32,256]{1,0:T(8,128)S(1)}, u32[]{:S(2)}, u32[]{:S(2)}) collective-permute-start(f32[32,256]{1,0:T(8,128)S(1)} %fusion.26), channel_id=1, source_target_pairs={{0,2},{1,3},{2,0},{3,1},{4,6},{5,7},{6,4},{7,5},{8,10},{9,11},{10,... | collective-permute-start | bytes 98312 | tf_op jit(solution)/shard_map/ppermute | solution.py:212
  181.3 1.8 place.1
  (180 shorter events, 74.6 us)
Async XLA Ops:
  12.3 22.8 %collective-permute-start.9 = (f32[128,256]{1,0:T(8,128)}, f32[128,256]{1,0:T(8,128)}, u32[]{:S(2)}, u32[]{:S(2)}) collective-permute-start(f32[128,256]{1,0:T(8,128)} %add_select_fusion.2), channel_id=1, source_target_pairs={{0,8},{24,16},{1,9},{25,17},{2,10},{26,18},{3,11},{27,19},{4,12},{... | collective-permute-start | bytes 393224 | tf_op jit(solution)/shard_map/ppermute | solution.py:231
  20.9 15.8 %collective-permute-start.6 = (f32[128,256]{1,0:T(8,128)}, f32[128,256]{1,0:T(8,128)}, u32[]{:S(2)}, u32[]{:S(2)}) collective-permute-start(f32[128,256]{1,0:T(8,128)} %add_select_fusion.5), channel_id=1, source_target_pairs={{0,8},{24,16},{1,9},{25,17},{2,10},{26,18},{3,11},{27,19},{4,12},{... | collective-permute-start | bytes 393224 | tf_op jit(solution)/shard_map/ppermute | solution.py:231
  26.7 11.8 %collective-permute-start.3 = (f32[128,256]{1,0:T(8,128)}, f32[128,256]{1,0:T(8,128)}, u32[]{:S(2)}, u32[]{:S(2)}) collective-permute-start(f32[128,256]{1,0:T(8,128)} %add_select_fusion.8), channel_id=1, source_target_pairs={{0,8},{24,16},{1,9},{25,17},{2,10},{26,18},{3,11},{27,19},{4,12},{... | collective-permute-start | bytes 393224 | tf_op jit(solution)/shard_map/ppermute | solution.py:231
  42.8 29.5 %collective-permute-start.11 = (f32[128,256]{1,0:T(8,128)S(1)}, f32[128,256]{1,0:T(8,128)S(1)}, u32[]{:S(2)}, u32[]{:S(2)}) collective-permute-start(f32[128,256]{1,0:T(8,128)S(1)} %add_select_fusion), channel_id=1, source_target_pairs={{16,24},{8,0},{17,25},{9,1},{18,26},{10,2},{19,27},{11,3},{20,28},... | collective-permute-start | bytes 393224 | tf_op jit(solution)/shard_map/ppermute | solution.py:231
  45.0 28.7 %collective-permute-start.8 = (f32[128,256]{1,0:T(8,128)S(1)}, f32[128,256]{1,0:T(8,128)S(1)}, u32[]{:S(2)}, u32[]{:S(2)}) collective-permute-start(f32[128,256]{1,0:T(8,128)S(1)} %add_select_fusion.3), channel_id=1, source_target_pairs={{16,24},{8,0},{17,25},{9,1},{18,26},{10,2},{19,27},{11,3},{20,28},... | collective-permute-start | bytes 393224 | tf_op jit(solution)/shard_map/ppermute | solution.py:231
  47.3 12.3 %collective-permute-start.2 = (f32[128,256]{1,0:T(8,128)S(1)}, f32[128,256]{1,0:T(8,128)S(1)}, u32[]{:S(2)}, u32[]{:S(2)}) collective-permute-start(f32[128,256]{1,0:T(8,128)S(1)} %add_select_fusion.9), channel_id=1, source_target_pairs={{16,24},{8,0},{17,25},{9,1},{18,26},{10,2},{19,27},{11,3},{20,28},... | collective-permute-start | bytes 393224 | tf_op jit(solution)/shard_map/ppermute | solution.py:231
  49.5 17.7 %collective-permute-start.5 = (f32[128,256]{1,0:T(8,128)S(1)}, f32[128,256]{1,0:T(8,128)S(1)}, u32[]{:S(2)}, u32[]{:S(2)}) collective-permute-start(f32[128,256]{1,0:T(8,128)S(1)} %add_select_fusion.6), channel_id=1, source_target_pairs={{16,24},{8,0},{17,25},{9,1},{18,26},{10,2},{19,27},{11,3},{20,28},... | collective-permute-start | bytes 393224 | tf_op jit(solution)/shard_map/ppermute | solution.py:231
  64.1 22.4 %collective-permute-start.13 = (f32[512,256]{1,0:T(8,128)S(1)}, f32[512,256]{1,0:T(8,128)}, u32[]{:S(2)}, u32[]{:S(2)}) collective-permute-start(f32[512,256]{1,0:T(8,128)S(1)} %get-tuple-element.97), channel_id=1, source_target_pairs={{0,1},{1,0},{2,3},{3,2},{4,5},{5,4},{6,7},{7,6},{8,9},{9,8},{10,11... | collective-permute-start | bytes 1572872 | tf_op jit(solution)/shard_map/ppermute | solution.py:212
  65.7 23.4 %collective-permute-start.34 = (f32[512,256]{1,0:T(8,128)S(1)}, f32[512,256]{1,0:T(8,128)}, u32[]{:S(2)}, u32[]{:S(2)}) collective-permute-start(f32[512,256]{1,0:T(8,128)S(1)} %get-tuple-element.107), channel_id=1, source_target_pairs={{0,2},{1,3},{2,0},{3,1},{4,6},{5,7},{6,4},{7,5},{8,10},{9,11},{10,... | collective-permute-start | bytes 1572872 | tf_op jit(solution)/shard_map/ppermute | solution.py:212
  71.7 20.0 %collective-permute-start.17 = (f32[512,256]{1,0:T(8,128)S(1)}, f32[512,256]{1,0:T(8,128)}, u32[]{:S(2)}, u32[]{:S(2)}) collective-permute-start(f32[512,256]{1,0:T(8,128)S(1)} %get-tuple-element.99), channel_id=1, source_target_pairs={{0,1},{1,0},{2,3},{3,2},{4,5},{5,4},{6,7},{7,6},{8,9},{9,8},{10,11... | collective-permute-start | bytes 1572872 | tf_op jit(solution)/shard_map/ppermute | solution.py:212
  72.3 21.0 %collective-permute-start.38 = (f32[512,256]{1,0:T(8,128)S(1)}, f32[512,256]{1,0:T(8,128)}, u32[]{:S(2)}, u32[]{:S(2)}) collective-permute-start(f32[512,256]{1,0:T(8,128)S(1)} %get-tuple-element.109), channel_id=1, source_target_pairs={{0,2},{1,3},{2,0},{3,1},{4,6},{5,7},{6,4},{7,5},{8,10},{9,11},{10,... | collective-permute-start | bytes 1572872 | tf_op jit(solution)/shard_map/ppermute | solution.py:212
  86.6 14.8 %collective-permute-start.25 = (f32[512,256]{1,0:T(8,128)S(1)}, f32[512,256]{1,0:T(8,128)S(1)}, u32[]{:S(2)}, u32[]{:S(2)}) collective-permute-start(f32[512,256]{1,0:T(8,128)S(1)} %get-tuple-element.103), channel_id=1, source_target_pairs={{0,1},{1,0},{2,3},{3,2},{4,5},{5,4},{6,7},{7,6},{8,9},{9,8},{10,11... | collective-permute-start | bytes 1572872 | tf_op jit(solution)/shard_map/ppermute | solution.py:212
  89.1 14.8 %collective-permute-start.46 = (f32[512,256]{1,0:T(8,128)S(1)}, f32[512,256]{1,0:T(8,128)S(1)}, u32[]{:S(2)}, u32[]{:S(2)}) collective-permute-start(f32[512,256]{1,0:T(8,128)S(1)} %get-tuple-element.113), channel_id=1, source_target_pairs={{0,2},{1,3},{2,0},{3,1},{4,6},{5,7},{6,4},{7,5},{8,10},{9,11},{10,... | collective-permute-start | bytes 1572872 | tf_op jit(solution)/shard_map/ppermute | solution.py:212
  91.7 20.9 %collective-permute-start.21 = (f32[512,256]{1,0:T(8,128)S(1)}, f32[512,256]{1,0:T(8,128)S(1)}, u32[]{:S(2)}, u32[]{:S(2)}) collective-permute-start(f32[512,256]{1,0:T(8,128)S(1)} %get-tuple-element.101), channel_id=1, source_target_pairs={{0,1},{1,0},{2,3},{3,2},{4,5},{5,4},{6,7},{7,6},{8,9},{9,8},{10,11... | collective-permute-start | bytes 1572872 | tf_op jit(solution)/shard_map/ppermute | solution.py:212
  93.3 21.9 %collective-permute-start.42 = (f32[512,256]{1,0:T(8,128)S(1)}, f32[512,256]{1,0:T(8,128)S(1)}, u32[]{:S(2)}, u32[]{:S(2)}) collective-permute-start(f32[512,256]{1,0:T(8,128)S(1)} %get-tuple-element.111), channel_id=1, source_target_pairs={{0,2},{1,3},{2,0},{3,1},{4,6},{5,7},{6,4},{7,5},{8,10},{9,11},{10,... | collective-permute-start | bytes 1572872 | tf_op jit(solution)/shard_map/ppermute | solution.py:212
  94.9 86.4 %collective-permute-start.12 = (f32[512,512]{1,0:T(8,128)S(1)}, f32[512,512]{1,0:T(8,128)S(1)}, u32[]{:S(2)}, u32[]{:S(2)}) collective-permute-start(f32[512,512]{1,0:T(8,128)S(1)} %copy-done.19), channel_id=1, source_target_pairs={{0,4},{4,0},{1,5},{5,1},{2,6},{6,2},{3,7},{7,3},{8,12},{12,8},{9,1... | collective-permute-start | bytes 3145736 | tf_op jit(solution)/shard_map/ppermute | solution.py:332
  101.4 19.4 %collective-permute-start.14 = (f32[256,256]{1,0:T(8,128)S(1)}, f32[256,256]{1,0:T(8,128)S(1)}, u32[]{:S(2)}, u32[]{:S(2)}) collective-permute-start(f32[256,256]{1,0:T(8,128)S(1)} %slice_add_fusion.8), channel_id=1, source_target_pairs={{0,2},{1,3},{2,0},{3,1},{4,6},{5,7},{6,4},{7,5},{8,10},{9,11},{10,... | collective-permute-start | bytes 786440 | tf_op jit(solution)/shard_map/ppermute | solution.py:212
  104.0 17.8 %collective-permute-start.35 = (f32[256,256]{1,0:T(8,128)S(1)}, f32[256,256]{1,0:T(8,128)S(1)}, u32[]{:S(2)}, u32[]{:S(2)}) collective-permute-start(f32[256,256]{1,0:T(8,128)S(1)} %slice_add_fusion.3), channel_id=1, source_target_pairs={{0,1},{1,0},{2,3},{3,2},{4,5},{5,4},{6,7},{7,6},{8,9},{9,8},{10,11... | collective-permute-start | bytes 786440 | tf_op jit(solution)/shard_map/ppermute | solution.py:212
  112.6 13.8 %collective-permute-start.18 = (f32[256,256]{1,0:T(8,128)S(1)}, f32[256,256]{1,0:T(8,128)S(1)}, u32[]{:S(2)}, u32[]{:S(2)}) collective-permute-start(f32[256,256]{1,0:T(8,128)S(1)} %slice_add_fusion.7), channel_id=1, source_target_pairs={{0,2},{1,3},{2,0},{3,1},{4,6},{5,7},{6,4},{7,5},{8,10},{9,11},{10,... | collective-permute-start | bytes 786440 | tf_op jit(solution)/shard_map/ppermute | solution.py:212
  115.2 12.7 %collective-permute-start.39 = (f32[256,256]{1,0:T(8,128)S(1)}, f32[256,256]{1,0:T(8,128)S(1)}, u32[]{:S(2)}, u32[]{:S(2)}) collective-permute-start(f32[256,256]{1,0:T(8,128)S(1)} %slice_add_fusion.2), channel_id=1, source_target_pairs={{0,1},{1,0},{2,3},{3,2},{4,5},{5,4},{6,7},{7,6},{8,9},{9,8},{10,11... | collective-permute-start | bytes 786440 | tf_op jit(solution)/shard_map/ppermute | solution.py:212
  120.8 9.6 %collective-permute-start.30 = (f32[256,256]{1,0:T(8,128)S(1)}, f32[256,256]{1,0:T(8,128)S(1)}, u32[]{:S(2)}, u32[]{:S(2)}) collective-permute-start(f32[256,256]{1,0:T(8,128)S(1)} %slice_add_fusion.4), channel_id=1, source_target_pairs={{0,8},{8,0},{16,24},{24,16},{1,9},{9,1},{17,25},{25,17},{2,10},{10... | collective-permute-start | bytes 786440 | tf_op jit(solution)/shard_map/ppermute | solution.py:212
  121.8 10.3 %collective-permute-start.26 = (f32[256,256]{1,0:T(8,128)S(1)}, f32[256,256]{1,0:T(8,128)S(1)}, u32[]{:S(2)}, u32[]{:S(2)}) collective-permute-start(f32[256,256]{1,0:T(8,128)S(1)} %slice_add_fusion.5), channel_id=1, source_target_pairs={{0,2},{1,3},{2,0},{3,1},{4,6},{5,7},{6,4},{7,5},{8,10},{9,11},{10,... | collective-permute-start | bytes 786440 | tf_op jit(solution)/shard_map/ppermute | solution.py:212
  136.9 10.4 %collective-permute-start.19 = (f32[128,256]{1,0:T(8,128)S(1)}, f32[128,256]{1,0:T(8,128)S(1)}, u32[]{:S(2)}, u32[]{:S(2)}) collective-permute-start(f32[128,256]{1,0:T(8,128)S(1)} %fusion.7), channel_id=1, source_target_pairs={{0,8},{8,0},{16,24},{24,16},{1,9},{9,1},{17,25},{25,17},{2,10},{10... | collective-permute-start | bytes 393224 | tf_op jit(solution)/shard_map/ppermute | solution.py:212
  138.8 11.3 %collective-permute-start.40 = (f32[128,256]{1,0:T(8,128)S(1)}, f32[128,256]{1,0:T(8,128)S(1)}, u32[]{:S(2)}, u32[]{:S(2)}) collective-permute-start(f32[128,256]{1,0:T(8,128)S(1)} %fusion.2), channel_id=1, source_target_pairs={{0,8},{8,0},{16,24},{24,16},{1,9},{9,1},{17,25},{25,17},{2,10},{10... | collective-permute-start | bytes 393224 | tf_op jit(solution)/shard_map/ppermute | solution.py:212
  139.1 12.0 %collective-permute-start.31 = (f32[128,256]{1,0:T(8,128)S(1)}, f32[128,256]{1,0:T(8,128)S(1)}, u32[]{:S(2)}, u32[]{:S(2)}) collective-permute-start(f32[128,256]{1,0:T(8,128)S(1)} %fusion.4), channel_id=1, source_target_pairs={{0,16},{8,24},{16,0},{24,8},{1,17},{9,25},{17,1},{25,9},{2,18},{10... | collective-permute-start | bytes 393224 | tf_op jit(solution)/shard_map/ppermute | solution.py:212
  143.1 10.0 %collective-permute-start.27 = (f32[128,256]{1,0:T(8,128)S(1)}, f32[128,256]{1,0:T(8,128)S(1)}, u32[]{:S(2)}, u32[]{:S(2)}) collective-permute-start(f32[128,256]{1,0:T(8,128)S(1)} %fusion.5), channel_id=1, source_target_pairs={{0,8},{8,0},{16,24},{24,16},{1,9},{9,1},{17,25},{25,17},{2,10},{10... | collective-permute-start | bytes 393224 | tf_op jit(solution)/shard_map/ppermute | solution.py:212
  150.1 11.1 %collective-permute-start.23 = (f32[128,256]{1,0:T(8,128)S(1)}, f32[128,256]{1,0:T(8,128)S(1)}, u32[]{:S(2)}, u32[]{:S(2)}) collective-permute-start(f32[128,256]{1,0:T(8,128)S(1)} %fusion.6), channel_id=1, source_target_pairs={{0,8},{8,0},{16,24},{24,16},{1,9},{9,1},{17,25},{25,17},{2,10},{10... | collective-permute-start | bytes 393224 | tf_op jit(solution)/shard_map/ppermute | solution.py:212
  151.1 11.8 %collective-permute-start.44 = (f32[128,256]{1,0:T(8,128)S(1)}, f32[128,256]{1,0:T(8,128)S(1)}, u32[]{:S(2)}, u32[]{:S(2)}) collective-permute-start(f32[128,256]{1,0:T(8,128)S(1)} %fusion.1), channel_id=1, source_target_pairs={{0,8},{8,0},{16,24},{24,16},{1,9},{9,1},{17,25},{25,17},{2,10},{10... | collective-permute-start | bytes 393224 | tf_op jit(solution)/shard_map/ppermute | solution.py:212
  153.1 11.2 %collective-permute-start.16 = (f32[64,256]{1,0:T(8,128)S(1)}, f32[64,256]{1,0:T(8,128)S(1)}, u32[]{:S(2)}, u32[]{:S(2)}) collective-permute-start(f32[64,256]{1,0:T(8,128)S(1)} %fusion.24), channel_id=1, source_target_pairs={{0,16},{8,24},{16,0},{24,8},{1,17},{9,25},{17,1},{25,9},{2,18},{10... | collective-permute-start | bytes 196616 | tf_op jit(solution)/shard_map/ppermute | solution.py:212
  156.4 9.6 %collective-permute-start.37 = (f32[64,256]{1,0:T(8,128)S(1)}, f32[64,256]{1,0:T(8,128)S(1)}, u32[]{:S(2)}, u32[]{:S(2)}) collective-permute-start(f32[64,256]{1,0:T(8,128)S(1)} %fusion.15), channel_id=1, source_target_pairs={{0,16},{8,24},{16,0},{24,8},{1,17},{9,25},{17,1},{25,9},{2,18},{10... | collective-permute-start | bytes 196616 | tf_op jit(solution)/shard_map/ppermute | solution.py:212
  166.0 9.5 %collective-permute-start.28 = (f32[64,256]{1,0:T(8,128)S(1)}, f32[64,256]{1,0:T(8,128)S(1)}, u32[]{:S(2)}, u32[]{:S(2)}) collective-permute-start(f32[64,256]{1,0:T(8,128)S(1)} %fusion.18), channel_id=1, source_target_pairs={{0,16},{8,24},{16,0},{24,8},{1,17},{9,25},{17,1},{25,9},{2,18},{10... | collective-permute-start | bytes 196616 | tf_op jit(solution)/shard_map/ppermute | solution.py:212
  167.7 10.6 %collective-permute-start.49 = (f32[64,256]{1,0:T(8,128)S(1)}, f32[64,256]{1,0:T(8,128)S(1)}, u32[]{:S(2)}, u32[]{:S(2)}) collective-permute-start(f32[64,256]{1,0:T(8,128)S(1)} %fusion.9), channel_id=1, source_target_pairs={{0,16},{8,24},{16,0},{24,8},{1,17},{9,25},{17,1},{25,9},{2,18},{10... | collective-permute-start | bytes 196616 | tf_op jit(solution)/shard_map/ppermute | solution.py:212
  (38 other events, 391.6 us)

commit v2 on v1

v2 whole, which is shorter than its diff:
```python
import functools

import jax
import jax.numpy as jnp
from jax import lax
from jax.experimental import pallas as pl
from jax.experimental.pallas import tpu as pltpu
from jax.sharding import PartitionSpec as P

CHUNK = 128
ROUNDS = 2
LIMIT = 48 * 1024 * 1024
f32 = jnp.float32
bf16 = jnp.bfloat16


def dot(a, b, ca=1, cb=0):
    return lax.dot_general(a, b, (((ca,), (cb,)), ((), ())), preferred_element_type=f32)


def log2(n):
    bits = n.bit_length() - 1
    assert 1 << bits == n
    return bits


def place(index, order):
    out = 0
    for rank, bit in enumerate(order):
        out = out + (((index >> bit) & 1) << (len(order) - 1 - rank))
    return out


def spread(values, first, heads, size):
    total = values.shape[1]
    row = lax.broadcasted_iota(jnp.int32, (total, heads * size), 0)
    col = lax.broadcasted_iota(jnp.int32, (total, heads * size), 1)
    low = (row - first) * size
    pick = jnp.where((col >= low) & (col < low + size), 1.0, 0.0).astype(bf16)
    high = values.astype(bf16)
    rest = values - high.astype(f32)
    middle = rest.astype(bf16)
    last = (rest - middle.astype(f32)).astype(bf16)
    return dot(high, pick) + dot(middle, pick) + dot(last, pick)


def triangle(upper):
    row = lax.broadcasted_iota(jnp.int32, (CHUNK, CHUNK), 0)
    col = lax.broadcasted_iota(jnp.int32, (CHUNK, CHUNK), 1)
    return row <= col if upper else row >= col


def one_hot_rows(offsets, rows):
    node = lax.broadcasted_iota(jnp.int32, (rows, offsets.shape[1]), 0)
    return jnp.where(node == offsets, 1.0, 0.0).astype(bf16)


def chunk_rows(cum_x, k):
    part = cum_x[k * CHUNK:(k + 1) * CHUNK]
    return part, part[CHUNK // 2 - 1:CHUNK // 2], part[CHUNK - 1:CHUNK]


def end_states(cum_x, x, dy, sc, sb, xs, ys, fwd, bwd, total):
    count = cum_x.shape[0] // CHUNK
    forward, back, decay = [], [], []
    for k in range(count):
        span = slice(k * CHUNK, (k + 1) * CHUNK)
        part, mid, last = chunk_rows(cum_x, k)
        x_s = (x[span] * jnp.exp(mid - part)).astype(bf16)
        y_s = (dy[span] * jnp.exp(part - mid)).astype(bf16)
        xs[span, :] = x_s
        ys[span, :] = y_s
        forward.append(jnp.exp(last - mid) * dot(sb[span, CHUNK:], x_s, 0, 0))
        back.append(jnp.exp(mid) * dot(sc[span, CHUNK:], y_s, 0, 0))
        decay.append(jnp.exp(last))
    run, run_back, factor = forward[0], back[-1], decay[0]
    for k in range(1, count):
        run = decay[k] * run + forward[k]
        factor = factor * decay[k]
        run_back = decay[count - 1 - k] * run_back + back[count - 1 - k]
    fwd[...] = run
    bwd[...] = run_back
    total[...] = factor


def order_kernel(heads, size, ids, off, tokens, cot, decays, w_state, w_inner, w_out,
                 ordered, ordered_grad, early_a, early_b, sc, sb, cum, xs, ys, fwd, bwd, total):
    base, side = ids[1], ids[2]
    rows, width = tokens.shape
    half = width // 2
    hot = one_hot_rows(off[...] - base, rows)
    ordered[...] = dot(hot, tokens[...], 0, 0).astype(bf16)
    ordered_grad[...] = dot(hot, cot[...], 0, 0).astype(bf16)
    first = jnp.where(side == 0, ordered[:, :half].astype(f32), ordered[:, half:].astype(f32))
    second = jnp.where(side == 0, ordered_grad[:, :half].astype(f32), ordered_grad[:, half:].astype(f32))
    early_a[...] = jnp.where(ids[4] == 0, second, first)
    early_b[...] = jnp.where(ids[5] == 0, second, first)
    bc = dot(ordered[...], w_state[...]).astype(bf16)
    state = bc.shape[1] // 2
    lower = triangle(False)
    upper = triangle(True)
    ones = jnp.where(lower, 1.0, 0.0)
    rates = jnp.log(decays[...])
    for k in range(rows // CHUNK):
        span = slice(k * CHUNK, (k + 1) * CHUNK)
        b, c = bc[span, :state], bc[span, state:]
        sc[span, :CHUNK] = jnp.where(lower, dot(c, b, 1, 1), 0.0).astype(bf16)
        sc[span, CHUNK:] = c
        sb[span, :CHUNK] = jnp.where(upper, dot(b, c, 1, 1), 0.0).astype(bf16)
        sb[span, CHUNK:] = b
        cum[span, :] = jnp.dot(ones, rates[span], precision=lax.Precision.HIGHEST, preferred_element_type=f32)
    cum_x = spread(cum[...], 0, heads, size)
    x = dot(ordered[...], w_inner[...]).astype(bf16).astype(f32)
    dy = dot(ordered_grad[...], w_out[...]).astype(bf16).astype(f32)
    end_states(cum_x, x, dy, sc, sb, xs, ys, fwd, bwd, total)


def states_kernel(first, heads, size, ordered, ordered_grad, w_inner, w_out, sc, sb, cum,
                  xs, ys, fwd, bwd, total):
    cum_x = spread(cum[...], first, heads, size)
    x = dot(ordered[...], w_inner[...]).astype(bf16).astype(f32)
    dy = dot(ordered_grad[...], w_out[...]).astype(bf16).astype(f32)
    end_states(cum_x, x, dy, sc, sb, xs, ys, fwd, bwd, total)


def turn_kernel(a_order, b_order, ids, ordered, ordered_grad, near_a, far_a, near_b, far_b, left_a, left_b):
    me, side = ids[0], ids[2]
    rows, width = ordered.shape
    half = width // 2
    blocks = 1 << len(a_order)
    size = width // blocks
    for left, order, role, near, far in ((left_a, a_order, ids[4], near_a, far_a), (left_b, b_order, ids[5], near_b, far_b)):
        for part in range(2):
            span = slice(part * half, (part + 1) * half)
            own = jnp.where(role == 0, ordered[:, span].astype(f32), ordered_grad[:, span].astype(f32)).astype(bf16)
            other = jnp.where(side == part, near[...], far[...]).astype(bf16)
            value = jnp.concatenate([own.T, other.T], axis=1)
            for block in range(blocks // 2):
                where = place((block + part * (blocks // 2)) ^ me, order)
                left[pl.ds(pl.multiple_of(where * size, size), size), :] = value[block * size:(block + 1) * size]


def outputs_kernel(first, heads, size, ids, xs, ys, sc, sb, cum, fwd_in, bwd_in,
                   own_a, send_a, own_b, send_b, grad_x, grad_bc):
    cum_x = spread(cum[...], first, heads, size)
    count = cum_x.shape[0] // CHUNK
    lower = triangle(False)
    upper = triangle(True)
    starts, afters = [fwd_in[...]], [bwd_in[...]]
    for k in range(count - 1):
        span = slice(k * CHUNK, (k + 1) * CHUNK)
        _, mid, last = chunk_rows(cum_x, k)
        starts.append(jnp.exp(last) * starts[-1] + jnp.exp(last - mid) * dot(sb[span, CHUNK:], xs[span, :], 0, 0))
    for k in range(count - 1, 0, -1):
        span = slice(k * CHUNK, (k + 1) * CHUNK)
        _, mid, last = chunk_rows(cum_x, k)
        afters.insert(0, jnp.exp(last) * afters[0] + jnp.exp(mid) * dot(sc[span, CHUNK:], ys[span, :], 0, 0))
    cols = xs.shape[1] // 2
    for k in range(count):
        span = slice(k * CHUNK, (k + 1) * CHUNK)
        part, mid, last = chunk_rows(cum_x, k)
        x_s, y_s = xs[span, :], ys[span, :]
        x_rows = jnp.concatenate([x_s, (starts[k] * jnp.exp(mid)).astype(bf16)], axis=0)
        y_rows = jnp.concatenate([y_s, (afters[k] * jnp.exp(last - mid)).astype(bf16)], axis=0)
        y = (jnp.exp(part - mid) * dot(sc[span, :], x_rows)).astype(bf16)
        dx = (jnp.exp(mid - part) * dot(sb[span, :], y_rows)).astype(bf16)
        grad_x[span, :] = dx
        y, dx = y.astype(f32), dx.astype(f32)
        for own, send, role, cut in ((own_a, send_a, ids[4], slice(0, cols)), (own_b, send_b, ids[5], slice(cols, 2 * cols))):
            own[span, :] = jnp.where(role == 0, dx[:, cut], y[:, cut]).astype(bf16)
            send[span, :] = jnp.where(role == 0, y[:, cut], dx[:, cut])
        by_y = dot(y_s, x_rows, 1, 1)
        by_x = dot(x_s, y_rows, 1, 1)
        pairs = jnp.where(lower, by_y[:, :CHUNK], 0.0).astype(bf16)
        turned = jnp.where(upper, by_x[:, :CHUNK], 0.0).astype(bf16)
        state = by_x.shape[1] - CHUNK
        grad_bc[span, :state] = dot(turned, sc[span, CHUNK:]) + by_x[:, CHUNK:]
        grad_bc[span, state:] = dot(pairs, sb[span, CHUNK:]) + by_y[:, CHUNK:]


def grads_kernel(left_a, left_b, own_a, came_a, own_b, came_b, keep_a, send_a, keep_b, send_b):
    half = left_a.shape[0] // 2
    for left, own, came, keep, send in ((left_a, own_a, came_a, keep_a, send_a), (left_b, own_b, came_b, keep_b, send_b)):
        right = jnp.concatenate([own[...], came[...].astype(bf16)], axis=0)
        send[...] = dot(left[half:, :], right)
        keep[...] = dot(left[:half, :], right)


def back_kernel(rounds, s_order, ids, *refs):
    grads, sums = refs[:rounds], refs[rounds:2 * rounds]
    w_inner, w_state, ordered, keep, send, state_keep, state_send, table = refs[2 * rounds:]
    side, me_state = ids[2], ids[3]
    grad_bc = sums[0][...]
    for part in sums[1:]:
        grad_bc = grad_bc + part[...]
    grad_bc = grad_bc.astype(bf16)
    width = ordered.shape[1]
    half = width // 2
    for out, which in ((send, 1 - side), (keep, side)):
        rows = pl.ds(pl.multiple_of(which * half, half), half)
        value = dot(grad_bc, w_state[rows, :], 1, 1)
        start = 0
        for part in grads:
            cols = part.shape[1]
            value = value + dot(part[...], w_inner[rows, start:start + cols], 1, 1)
            start += cols
        out[...] = value
    fine = width >> len(s_order)
    step = width // 4
    for quarter in range(4):
        value = dot(ordered[:, quarter * step:(quarter + 1) * step], grad_bc, 0, 0)
        for piece in range(step // fine):
            index = (quarter * step) // fine + piece
            where = place(index ^ me_state, s_order)
            table[pl.ds(pl.multiple_of(where * fine, fine), fine), :] = value[piece * fine:(piece + 1) * fine]
    state_keep[...] = table[:half, :]
    state_send[...] = table[half:, :]


def place_kernel(ids, off, keep, came, out):
    hot = one_hot_rows(off[...] - ids[1], out.shape[0])
    out[...] = dot(hot, (keep[...] + came[...]).astype(bf16)).astype(bf16)


def flips(axis, bit):
    return [(i, i ^ (1 << bit)) for i in range(lax.axis_size(axis))]


def total_of(parts, start, stop):
    out = parts[0][..., start:stop, :]
    for part in parts[1:]:
        out = out + part[..., start:stop, :]
    return out


def halving(parts, hops):
    rows = parts[0].shape[-2]
    for axis, bit in hops:
        rows //= 2
        parts = [p[..., :2 * rows, :] for p in parts]
        came = lax.ppermute(total_of(parts, rows, 2 * rows), axis, flips(axis, bit))
        parts = [p[..., :rows, :] for p in parts] + [came]
    return total_of(parts, 0, rows)


def carries(forward, back, total):
    count, mine = lax.axis_size("order"), lax.axis_index("order")
    run, run_back = jnp.zeros_like(forward), jnp.zeros_like(back)
    first = None
    for k in range(1, count):
        up, down = total * run + forward, total * run_back + back
        if count % 2 == 0:
            message = jnp.where(mine == k - 1, up, down)
            came = came_back = lax.ppermute(message, "order", [(k - 1, k), (count - k, count - k - 1)])
        else:
            message = up
            came = lax.ppermute(up, "order", [(k - 1, k)])
            came_back = lax.ppermute(down, "order", [(count - k, count - k - 1)])
        first = message if first is None else first
        run = jnp.where(mine == k, came, run)
        run_back = jnp.where(mine == count - k - 1, came_back, run_back)
    return run, run_back, first


def whole(array):
    return pl.BlockSpec(array.shape, lambda *_: (0,) * len(array.shape))


def call(kernel, outs, args, name, scratch=(), specs=None, flops=0):
    specs = specs or {}
    in_specs = []
    for i, arg in enumerate(args):
        if i in specs:
            in_specs.append(specs[i])
        elif arg.dtype == jnp.int32 and arg.ndim == 1:
            in_specs.append(pl.BlockSpec(memory_space=pltpu.SMEM))
        else:
            in_specs.append(whole(arg))
    moved = sum(a.size * a.dtype.itemsize for a in list(args) + list(outs))
    return pl.pallas_call(
        kernel,
        out_shape=tuple(outs),
        grid=(1,),
        in_specs=in_specs,
        out_specs=tuple(whole(o) for o in outs),
        scratch_shapes=list(scratch),
        compiler_params=pltpu.CompilerParams(vmem_limit_bytes=LIMIT),
        cost_estimate=pl.CostEstimate(flops=int(flops), bytes_accessed=int(moved), transcendentals=0),
        name=name,
    )(*args)


def per_device(tokens, cotangent, node_order, decays, w_inner, w_state, w_out):
    assert tokens.shape[0] == 1
    tokens, cotangent, decays = tokens[0], cotangent[0], decays[0]
    rows, width = tokens.shape
    heads = decays.shape[1]
    inner = w_inner.shape[1]
    size = inner // heads
    state = w_state.shape[1] // 2
    cols = inner // ROUNDS
    round_heads = heads // ROUNDS
    n_order, n_heads, n_seq = (lax.axis_size(a) for a in ("order", "heads", "seq"))
    o, h, s = (lax.axis_index(a) for a in ("order", "heads", "seq"))
    seq_bits, head_bits, order_bits = log2(n_seq), log2(n_heads), log2(n_order)
    assert seq_bits == 2 and head_bits == 1
    order_hops = [("order", b) for b in range(order_bits)]
    a_hops = [("seq", 1)] + order_hops + [("seq", 0)]
    b_hops = [("seq", 0)] + order_hops + [("seq", 1)]
    s_hops = [("heads", 0)] + order_hops + [("seq", 0), ("seq", 1)]
    shift = {"seq": 0, "order": seq_bits}
    shift_state = {"seq": 0, "heads": seq_bits, "order": seq_bits + head_bits}
    a_order = [shift[a] + b for a, b in a_hops]
    b_order = [shift[a] + b for a, b in b_hops]
    s_order = [shift_state[a] + b for a, b in s_hops]
    role_a, role_b = s & 1, (s >> 1) & 1
    ids = jnp.stack([o * n_seq + s, o * rows, h, (o * n_heads + h) * n_seq + s, role_a, role_b]).astype(jnp.int32)
    S = jax.ShapeDtypeStruct
    full = S((rows, width), bf16)
    half_wide = S((rows, width // 2), f32)
    wide = S((rows, CHUNK + state), bf16)
    ends = [S((rows, cols), bf16)] * 2 + [S((state, cols), f32)] * 2 + [S((1, cols), f32)]

    def column(r):
        return pl.BlockSpec((width, cols), lambda _: (0, r))

    ordered, ordered_grad, early_a, early_b, sc, sb, cum, *first = call(
        functools.partial(order_kernel, round_heads, size),
        [full, full, half_wide, half_wide, wide, wide, S((rows, heads), f32)] + ends,
        [ids, node_order, tokens, cotangent, decays, w_state, w_inner, w_out], "order",
        specs={6: column(0), 7: column(0)}, flops=10 * rows * rows * width)
    rounds = [first]
    run, run_back, message = carries(*first[2:])
    incoming = [(run, run_back)]
    for r in range(1, ROUNDS):
        cum_r, _ = lax.optimization_barrier((cum, message))
        rounds.append(call(
            functools.partial(states_kernel, r * round_heads, round_heads, size), ends,
            [ordered, ordered_grad, w_inner, w_out, sc, sb, cum_r], f"states_{r}",
            specs={2: column(r), 3: column(r)}, flops=4 * rows * width * cols))
        run, run_back, message = carries(*rounds[r][2:])
        incoming.append((run, run_back))
    near_a = lax.ppermute(early_a, "seq", flips("seq", 0))
    near_b = lax.ppermute(early_b, "seq", flips("seq", 1))
    far_a = lax.ppermute(near_a, "heads", flips("heads", 0))
    far_b = lax.ppermute(near_b, "heads", flips("heads", 0))
    pair = S((width, 2 * rows), bf16)
    left_a, left_b = call(
        functools.partial(turn_kernel, a_order, b_order), [pair, pair],
        [ids, ordered, ordered_grad, near_a, far_a, near_b, far_b], "turn", flops=rows * width)
    part = cols // 2
    halves, grads, sums = [], [], []
    for r in range(ROUNDS):
        xs, ys = rounds[r][:2]
        own_a, send_a, own_b, send_b, grad_x, grad_bc = call(
            functools.partial(outputs_kernel, r * round_heads, round_heads, size),
            [S((rows, part), bf16), S((rows, part), f32)] * 2 + [S((rows, cols), bf16), S((rows, 2 * state), f32)],
            [ids, xs, ys, sc, sb, cum, *incoming[r]], f"outputs_{r}",
            flops=8 * rows * 256 * cols)
        grads.append(grad_x)
        sums.append(grad_bc)
        came_a = lax.ppermute(send_a, "seq", flips("seq", 0))
        came_b = lax.ppermute(send_b, "seq", flips("seq", 1))
        half = S((width // 2, part), f32)
        keep_a, send_a, keep_b, send_b = call(
            grads_kernel, [half] * 4, [left_a, left_b, own_a, came_a, own_b, came_b], f"grads_{r}",
            flops=8 * rows * width * part)
        next_a = lax.ppermute(send_a, "seq", flips("seq", 1))
        next_b = lax.ppermute(send_b, "seq", flips("seq", 0))
        halves.append(halving([jnp.stack([keep_a, keep_b]), jnp.stack([next_a, next_b])], order_hops))
    piece = S((rows, width // 2), f32)
    half_state = S((width // 2, 2 * state), f32)
    keep, send, state_keep, state_send = call(
        functools.partial(back_kernel, ROUNDS, s_order),
        [piece, piece, half_state, half_state],
        [ids] + grads + sums + [w_inner, w_state, ordered], "back",
        scratch=[pltpu.VMEM((width, 2 * state), f32)],
        flops=2 * rows * width * inner)
    came = lax.ppermute(send, "heads", flips("heads", 0))
    d_tokens = call(place_kernel, [S((rows, width // 2), bf16)], [ids, node_order, keep, came], "place",
                    flops=rows * rows * width)[0]
    came_state = lax.ppermute(state_send, "heads", flips("heads", 0))
    d_w_state = halving([state_keep, came_state], s_hops[1:])
    block = width // (n_order * n_seq)
    both = jnp.stack(halves)
    swap_a = lax.ppermute(both[:, 0, block:], "seq", flips("seq", 0))
    swap_b = lax.ppermute(both[:, 1, block:], "seq", flips("seq", 1))
    own = both[:, :, :block]
    swapped = jnp.stack([swap_a, swap_b], axis=1)
    flag = jnp.stack([role_a, role_b])[None, :, None, None] == 0
    inner_blocks = jnp.where(flag, own, swapped)
    out_blocks = jnp.where(flag, swapped, own)
    d_w_inner = inner_blocks.transpose(2, 0, 1, 3).reshape(block, inner)
    d_w_out = out_blocks.transpose(2, 0, 1, 3).reshape(block, inner)
    return d_tokens[None], d_w_inner, d_w_state, d_w_out


def solution(mesh):
    in_specs = (
        P("seq", "order", None),
        P("seq", "order", None),
        P("seq", "order"),
        P("seq", "order", "heads"),
        P(None, "heads"),
        P(),
        P(None, "heads"),
    )
    out_specs = (
        P("seq", "order", "heads"),
        P(("order", "seq"), "heads"),
        P(("order", "heads", "seq"), None),
        P(("order", "seq"), "heads"),
    )
    return jax.shard_map(
        per_device, mesh=mesh, in_specs=in_specs, out_specs=out_specs, check_vma=False
    )
```

time: 185 us -> 157 us (0.85)
  starting transfers between devices: 56.6 us -> 34 us
  other arithmetic: 31.3 us -> 10.2 us
  waiting for transfers between devices: 53.1 us -> 63 us
  local copies, waits for them, and re-layouts: 4.8 us -> 12.5 us
    add x37 -> x9, other arithmetic: 15.7 us -> 0.95 us  [total_of(): out = out + part[..., start:stop, :]]
    ppermute x37 -> x23, starting transfers between devices: 36.9 us -> 23.2 us  [the longest x8 8.67 us: halving(): came = lax.ppermute(total_of(parts, rows, 2 * rows), axis, flips(axis, bit))]
    ppermute x12 -> x6, starting transfers between devices: 19.5 us -> 10.7 us  [carries(): lax.ppermute(message, 'order', [(k - 1, k), (count - k, count - k - 1)])]
    ppermute x12 -> x6, waiting for transfers between devices: 8.55 us -> 16.1 us  [carries(): lax.ppermute(message, 'order', [(k - 1, k), (count - k, count - k - 1)])]
    unnamed x41 -> x45, local copies, waits for them, and re-layouts: 4.8 us -> 10.1 us
    select_n x12 -> x6, other arithmetic: 10.3 us -> 6.73 us  [carries(): message = jnp.where(mine == k - 1, up, down)]
    ppermute x37 -> x23, waiting for transfers between devices: 44.5 us -> 46.9 us  [the longest x8 29.7 us: halving(): came = lax.ppermute(total_of(parts, rows, 2 * rows), axis, flips(axis, bit))]
    select_n x4 -> x2, other arithmetic: 3.73 us -> 2.21 us  [carries(): run_back = jnp.where(mine == count - k - 1, came_back, run_back)]
  transfers between devices with their start and end apart: 50 -> 30, of which waited for: 20 -> 15; matrix products, arithmetic and copies ran while one was open for 17% -> 6% of each run, Pallas kernels for 14% -> 18%
where the time goes in v2:
time: 157 us; the launch traced here: 156 us
  waiting for transfers between devices  63 us (40%)
  Pallas kernels  35.2 us (22%)
  starting transfers between devices  34 us (22%)
  local copies, waits for them, and re-layouts  12.5 us (8%)
  other arithmetic  10.2 us (6%)
    pallas_call x9, Pallas kernels, call(): pl.pallas_call(kernel, out_shape=tuple(outs), grid=(1,), in_specs=in_spec...  35.2 us
    ppermute x8, waiting for transfers between devices, halving(): came = lax.ppermute(total_of(parts, rows, 2 * rows), axis, flips(axis, bit))  29.7 us
    ppermute x6, waiting for transfers between devices, carries(): lax.ppermute(message, 'order', [(k - 1, k), (count - k, count - k - 1)])  16.1 us
    ppermute x2, waiting for transfers between devices, per_device(): next_a = lax.ppermute(send_a, 'seq', flips('seq', 1))  14.6 us
    ppermute x6, starting transfers between devices, carries(): lax.ppermute(message, 'order', [(k - 1, k), (count - k, count - k - 1)])  10.7 us
    unnamed x45, local copies, waits for them, and re-layouts  10.1 us
    ppermute x8, starting transfers between devices, halving(): came = lax.ppermute(total_of(parts, rows, 2 * rows), axis, flips(axis, bit))  8.67 us
    select_n x6, other arithmetic, carries(): message = jnp.where(mine == k - 1, up, down)  6.73 us
  transfers between devices with their start and end apart: 30, of which 15 were waited for; matrix products, arithmetic and copies ran while one was open for 6% of the time, Pallas kernels for 18%

profile of v2, /device:TPU:0, one launch (start us, length us, event | category | flops | bytes accessed | tf_op | source)
XLA Modules:
  0.0 155.9 jit_solution(14606585915893579269)
XLA Ops:
  0.6 1.6 %copy.14 = f32[1,512,16]{2,1,0:T(8,128)} copy(f32[1,512,16]{1,2,0:T(8,128)} %param.10) | data formatting | bytes 65536 | tf_op args[3]
  5.0 7.5 %order.1 = (bf16[512,1024]{1,0:T(8,128)(2,1)S(1)}, bf16[512,1024]{1,0:T(8,128)(2,1)S(1)}, f32[512,512]{1,0:T(8,128)}, f32[512,512]{1,0:T(8,128)}, bf16[512,256]{...) custom-call(s32[6]{0:T(128)S(1)} %stack.86.ids, ...), custom_call_target="tpu_custom_call" | custom-call | flops 2684354560 | bytes 13176856 | tf_op jit(solution)/shard_map/order/pallas_call | solution.py:280
  14.1 2.9 %collective-permute-start.7 = (f32[512,512]{1,0:T(8,128)}, f32[512,512]{1,0:T(8,128)}, u32[]{:S(2)}, u32[]{:S(2)}) collective-permute-start(f32[512,512]{1,0:T(8,128)} %get-tuple-element.70), channel_id=1, source_target_pairs={{0,1},{1,0},{2,3},{3,2},{4,5},{5,4},{6,7},{7,6},{8,9},{9,8},{10,11... | collective-permute-start | bytes 3145736 | tf_op jit(solution)/shard_map/ppermute | solution.py:343
  17.1 1.5 collective-permute-start.9
  19.3 3.7 %states_1.1 = (bf16[512,512]{1,0:T(8,128)(2,1)S(1)}, bf16[512,512]{1,0:T(8,128)(2,1)S(1)}, f32[128,512]{1,0:T(8,128)S(1)}, f32[128,512]{1,0:T(8,128)S(1)}, f32[1,512]{1,0:T(1,128)S(1)}) custom-call(bf16[512,1024]{1,0:T(8,128)(2,1)S(1)} %get-tuple-element.57.ordered.refs_6_, bf16[512,1024]{1,0:T(8,128)(2,1)S(1)} %get-tuple-element.58.ordered_grad, ...), custom_call_target="tpu_custom_call" | custom-call | flops 1073741824 | bytes 8423424 | tf_op jit(solution)/shard_map/states_1/pallas_call | solution.py:280
  24.6 3.6 %collective-permute-start.3 = (f32[128,512]{1,0:T(8,128)S(1)}, f32[128,512]{1,0:T(8,128)S(1)}, u32[]{:S(2)}, u32[]{:S(2)}) collective-permute-start(f32[128,512]{1,0:T(8,128)S(1)} %add_select_fusion.2), channel_id=1, source_target_pairs={{0,8},{24,16},{1,9},{25,17},{2,10},{26,18},{3,11},{27,19},{4,12},{... | collective-permute-start | bytes 786440 | tf_op jit(solution)/shard_map/ppermute | solution.py:254
  28.3 2.1 %collective-permute-start = (f32[128,512]{1,0:T(8,128)}, f32[128,512]{1,0:T(8,128)}, u32[]{:S(2)}, u32[]{:S(2)}) collective-permute-start(f32[128,512]{1,0:T(8,128)} %add_select_fusion.5), channel_id=1, source_target_pairs={{0,8},{24,16},{1,9},{25,17},{2,10},{26,18},{3,11},{27,19},{4,12},{... | collective-permute-start | bytes 786440 | tf_op jit(solution)/shard_map/ppermute | solution.py:254
  30.4 4.6 %collective-permute-done.3 = f32[128,512]{1,0:T(8,128)S(1)} collective-permute-done((f32[128,512]{1,0:T(8,128)S(1)}, f32[128,512]{1,0:T(8,128)S(1)}, u32[]{:S(2)}, u32[]{:S(2)}) %collective-permute-start.3) | collective-permute-done | bytes 262176 | tf_op jit(solution)/shard_map/ppermute | solution.py:254
  36.9 2.1 %collective-permute-done = f32[128,512]{1,0:T(8,128)} collective-permute-done((f32[128,512]{1,0:T(8,128)}, f32[128,512]{1,0:T(8,128)}, u32[]{:S(2)}, u32[]{:S(2)}) %collective-permute-start) | collective-permute-done | bytes 262176 | tf_op jit(solution)/shard_map/ppermute | solution.py:254
  38.9 1.7 %add_select_fusion.4 = f32[128,512]{1,0:T(8,128)} fusion(f32[128,512]{1,0:T(8,128)S(1)} %get-tuple-element.55, f32[128,512]{1,0:T(8,128)S(1)} %get-tuple-element.54, f32[128,512]{1,0:T(8,128)} %collective-permute-done, f32[512]{0:T(512)S(1)} %bitcast.50, pred[]{:T(512)S(6)} %eq.17, pred[]{:T(512)S(6)} %eq.16), kind=kLoop, calls=%fused_computation.43 | loop fusion | flops 458752 | bytes 1050626 | tf_op jit(solution)/shard_map/jit(_where)/select_n | solution.py:253
  40.7 1.5 collective-permute-start.1
  42.7 1.9 %add_select_fusion = f32[128,512]{1,0:T(8,128)} fusion(f32[128,512]{1,0:T(8,128)S(1)} %copy-done.6, f32[128,512]{1,0:T(8,128)S(1)} %copy-done.4, f32[512]{0:T(512)S(1)} %bitcast.54, pred[]{:T(512)S(6)} %eq.16, f32[128,512]{1,0:T(8,128)S(1)} %collective-permute-done.4, f32[128,512]{1,0:T(8,128)} %copy-done.20, pred[]{:T(512)S(6)} %eq.17), kind=kLoop, calls=%fused_computation.39 | loop fusion | flops 589824 | bytes 1312770 | tf_op jit(solution)/shard_map/jit(_where)/select_n | solution.py:253
  47.0 1.5 collective-permute-start.2
  48.5 9.4 %collective-permute-done.5 = f32[128,512]{1,0:T(8,128)S(1)} collective-permute-done((f32[128,512]{1,0:T(8,128)}, f32[128,512]{1,0:T(8,128)S(1)}, u32[]{:S(2)}, u32[]{:S(2)}) %collective-permute-start.5) | collective-permute-done | bytes 262176 | tf_op jit(solution)/shard_map/ppermute | solution.py:254
  60.2 3.8 %outputs_1.1 = (bf16[512,256]{1,0:T(8,128)(2,1)S(1)}, f32[512,256]{1,0:T(8,128)}, bf16[512,256]{1,0:T(8,128)(2,1)S(1)}, f32[512,256]{1,0:T(8,128)}, bf16[512,512...) custom-call(s32[6]{0:T(128)S(1)} %stack.86.ids, bf16[512,512]{1,0:T(8,128)(2,1)S(1)} %copy-done.14, ...), custom_call_target="tpu_custom_call" | custom-call | flops 536870912 | bytes 4751384 | tf_op jit(solution)/shard_map/outputs_1/pallas_call | solution.py:280
  66.1 3.7 %outputs_0.1 = (bf16[512,256]{1,0:T(8,128)(2,1)S(1)}, f32[512,256]{1,0:T(8,128)}, bf16[512,256]{1,0:T(8,128)(2,1)S(1)}, f32[512,256]{1,0:T(8,128)S(1)}, bf16[512...) custom-call(s32[6]{0:T(128)S(1)} %stack.86.ids, bf16[512,512]{1,0:T(8,128)(2,1)S(1)} %copy-done.10, ...), custom_call_target="tpu_custom_call" | custom-call | flops 536870912 | bytes 4751384 | tf_op jit(solution)/shard_map/outputs_0/pallas_call | solution.py:280
  71.3 1.5 collective-permute-start.12
  72.8 3.9 %back.1 = (f32[512,512]{1,0:T(8,128)S(1)}, f32[512,512]{1,0:T(8,128)S(1)}, f32[512,256]{1,0:T(8,128)S(1)}, f32[512,256]{1,0:T(8,128)S(1)}) custom-call(s32[6]{0:T(128)S(1)} %stack.86.ids, bf16[512,512]{1,0:T(8,128)(2,1)S(1)} %get-tuple-element.56.refs_0_, bf16[512,512]{1,0:T(8,128)(2,1)S(1)} %get-tuple-element.65.refs_1_, ...), custom_call_target="tpu_custom_call" | custom-call | flops 1073741824 | bytes 8912920 | tf_op jit(solution)/shard_map/back/pallas_call | solution.py:280
  76.8 5.3 %turn.1 = (bf16[1024,1024]{1,0:T(8,128)(2,1)}, bf16[1024,1024]{1,0:T(8,128)(2,1)}) custom-call(s32[6]{0:T(128)S(1)} %stack.86.ids, bf16[512,1024]{1,0:T(8,128)(2,1)S(1)} %copy-done.1, bf16[512,1024]{1,0:T(8,128)(2,1)S(1)} %get-tuple-element.58.ordered_grad, f32[512,512]{1,0:T(8,128)} %collective-permute-done.7.near_a, ...), custom_call_target="tpu_custom_call" | custom-call | flops 524288 | bytes 10485784 | tf_op jit(solution)/shard_map/turn/pallas_call | solution.py:280
  82.1 1.6 %copy-done.2 = bf16[1024,1024]{1,0:T(8,128)(2,1)S(1)} copy-done((bf16[1024,1024]{1,0:T(8,128)(2,1)S(1)}, bf16[1024,1024]{1,0:T(8,128)(2,1)}, u32[]{:S(2)}) %copy-start.2) | copy-done | bytes 2097176
  83.7 2.8 %grads_1.1 = (f32[512,256]{1,0:T(8,128)S(1)}, f32[512,256]{1,0:T(8,128)S(1)}, f32[512,256]{1,0:T(8,128)S(1)}, f32[512,256]{1,0:T(8,128)S(1)}) custom-call(bf16[1024,1024]{1,0:T(8,128)(2,1)S(1)} %copy-done.2, bf16[1024,1024]{1,0:T(8,128)(2,1)} %get-tuple-element.73.left_b, bf16[512,256]{1,0:T(8,128)(2,1)S(1)} %get-tuple-element.82.own_a, ...), custom_call_target="tpu_custom_call" | custom-call | flops 1073741824 | bytes 7864320 | tf_op jit(solution)/shard_map/grads_1/pallas_call | solution.py:280
  88.3 2.8 %grads_0.1 = (f32[512,256]{1,0:T(8,128)S(1)}, f32[512,256]{1,0:T(8,128)S(1)}, f32[512,256]{1,0:T(8,128)S(1)}, f32[512,256]{1,0:T(8,128)S(1)}) custom-call(bf16[1024,1024]{1,0:T(8,128)(2,1)S(1)} %copy-done.2, bf16[1024,1024]{1,0:T(8,128)(2,1)} %get-tuple-element.73.left_b, bf16[512,256]{1,0:T(8,128)(2,1)S(1)} %get-tuple-element.74.own_a, ...), custom_call_target="tpu_custom_call" | custom-call | flops 1073741824 | bytes 7864320 | tf_op jit(solution)/shard_map/grads_0/pallas_call | solution.py:280
  92.0 1.5 collective-permute-start.14
  93.7 7.6 %collective-permute-done.19 = f32[512,256]{1,0:T(8,128)S(1)} collective-permute-done((f32[512,256]{1,0:T(8,128)S(1)}, f32[512,256]{1,0:T(8,128)S(1)}, u32[]{:S(2)}, u32[]{:S(2)}) %collective-permute-start.19) | collective-permute-done | bytes 524320 | tf_op jit(solution)/shard_map/ppermute | solution.py:368
  102.0 3.1 %collective-permute-start.27 = (f32[128,256]{1,0:T(8,128)S(1)}, f32[128,256]{1,0:T(8,128)S(1)}, u32[]{:S(2)}, u32[]{:S(2)}) collective-permute-start(f32[128,256]{1,0:T(8,128)S(1)} %slice_add_fusion.5), channel_id=1, source_target_pairs={{0,16},{8,24},{16,0},{24,8},{1,17},{9,25},{17,1},{25,9},{2,18},{10... | collective-permute-start | bytes 393224 | tf_op jit(solution)/shard_map/ppermute | solution.py:241
  105.1 7.0 %collective-permute-done.13 = f32[512,256]{1,0:T(8,128)S(1)} collective-permute-done((f32[512,256]{1,0:T(8,128)S(1)}, f32[512,256]{1,0:T(8,128)S(1)}, u32[]{:S(2)}, u32[]{:S(2)}) %collective-permute-start.13) | collective-permute-done | bytes 524320 | tf_op jit(solution)/shard_map/ppermute | solution.py:368
  112.6 4.6 %collective-permute-done.27 = f32[128,256]{1,0:T(8,128)S(1)} collective-permute-done((f32[128,256]{1,0:T(8,128)S(1)}, f32[128,256]{1,0:T(8,128)S(1)}, u32[]{:S(2)}, u32[]{:S(2)}) %collective-permute-start.27) | collective-permute-done | bytes 131104 | tf_op jit(solution)/shard_map/ppermute | solution.py:241
  118.7 2.6 %collective-permute-start.22 = (f32[2,128,256]{2,1,0:T(8,128)S(1)}, f32[2,128,256]{2,1,0:T(8,128)S(1)}, u32[]{:S(2)}, u32[]{:S(2)}) collective-permute-start(f32[2,128,256]{2,1,0:T(8,128)S(1)} %slice_add_fusion.1), channel_id=1, source_target_pairs={{0,16},{8,24},{16,0},{24,8},{1,17},{9,25},{17,1},{25,9},{2,18},{10... | collective-permute-start | bytes 786440 | tf_op jit(solution)/shard_map/ppermute | solution.py:241
  121.3 12.9 %collective-permute-done.15 = f32[2,256,256]{2,1,0:T(8,128)S(1)} collective-permute-done((f32[2,256,256]{2,1,0:T(8,128)S(1)}, f32[2,256,256]{2,1,0:T(8,128)S(1)}, u32[]{:S(2)}, u32[]{:S(2)}) %collective-permute-start.15) | collective-permute-done | bytes 524320 | tf_op jit(solution)/shard_map/ppermute | solution.py:241
  134.9 1.5 collective-permute-start.29
  136.5 11.3 %collective-permute-done.16 = f32[2,128,256]{2,1,0:T(8,128)S(1)} collective-permute-done((f32[2,128,256]{2,1,0:T(8,128)S(1)}, f32[2,128,256]{2,1,0:T(8,128)S(1)}, u32[]{:S(2)}, u32[]{:S(2)}) %collective-permute-start.16) | collective-permute-done | bytes 262176 | tf_op jit(solution)/shard_map/ppermute | solution.py:241
  150.6 1.8 %place.1 = bf16[512,512]{1,0:T(8,128)(2,1)} custom-call(s32[6]{0:T(128)S(1)} %stack.86.ids, s32[1,512]{1,0:T(1,128)S(1)} %copy-done.19, f32[512,512]{1,0:T(8,128)S(1)} %get-tuple-element.68.keep, f32[512,512]{1,0:T(8,128)S(1)} %collective-permute-done.6.came), custom_call_target="tpu_custom_call" | custom-call | flops 268435456 | bytes 2623512 | tf_op jit(solution)/shard_map/place/pallas_call | solution.py:280
  (111 shorter events, 30.0 us)
Async XLA Ops:
  14.1 28.1 %collective-permute-start.7 = (f32[512,512]{1,0:T(8,128)}, f32[512,512]{1,0:T(8,128)}, u32[]{:S(2)}, u32[]{:S(2)}) collective-permute-start(f32[512,512]{1,0:T(8,128)} %get-tuple-element.70), channel_id=1, source_target_pairs={{0,1},{1,0},{2,3},{3,2},{4,5},{5,4},{6,7},{7,6},{8,9},{9,8},{10,11... | collective-permute-start | bytes 3145736 | tf_op jit(solution)/shard_map/ppermute | solution.py:343
  17.1 25.1 %collective-permute-start.9 = (f32[512,512]{1,0:T(8,128)}, f32[512,512]{1,0:T(8,128)}, u32[]{:S(2)}, u32[]{:S(2)}) collective-permute-start(f32[512,512]{1,0:T(8,128)} %get-tuple-element.71), channel_id=1, source_target_pairs={{0,2},{1,3},{2,0},{3,1},{4,6},{5,7},{6,4},{7,5},{8,10},{9,11},{10,... | collective-permute-start | bytes 3145736 | tf_op jit(solution)/shard_map/ppermute | solution.py:344
  24.6 18.1 %copy-start.4 = (f32[128,512]{1,0:T(8,128)S(1)}, f32[128,512]{1,0:T(8,128)}, u32[]{:S(2)}) copy-start(f32[128,512]{1,0:T(8,128)} %copy-done.3) | copy-start | bytes 786436
  24.6 10.4 %collective-permute-start.3 = (f32[128,512]{1,0:T(8,128)S(1)}, f32[128,512]{1,0:T(8,128)S(1)}, u32[]{:S(2)}, u32[]{:S(2)}) collective-permute-start(f32[128,512]{1,0:T(8,128)S(1)} %add_select_fusion.2), channel_id=1, source_target_pairs={{0,8},{24,16},{1,9},{25,17},{2,10},{26,18},{3,11},{27,19},{4,12},{... | collective-permute-start | bytes 786440 | tf_op jit(solution)/shard_map/ppermute | solution.py:254
  28.3 10.7 %collective-permute-start = (f32[128,512]{1,0:T(8,128)}, f32[128,512]{1,0:T(8,128)}, u32[]{:S(2)}, u32[]{:S(2)}) collective-permute-start(f32[128,512]{1,0:T(8,128)} %add_select_fusion.5), channel_id=1, source_target_pairs={{0,8},{24,16},{1,9},{25,17},{2,10},{26,18},{3,11},{27,19},{4,12},{... | collective-permute-start | bytes 786440 | tf_op jit(solution)/shard_map/ppermute | solution.py:254
  36.2 6.5 %collective-permute-start.4 = (f32[128,512]{1,0:T(8,128)S(1)}, f32[128,512]{1,0:T(8,128)S(1)}, u32[]{:S(2)}, u32[]{:S(2)}) collective-permute-start(f32[128,512]{1,0:T(8,128)S(1)} %add_select_fusion.1), channel_id=1, source_target_pairs={{8,16},{16,8},{9,17},{17,9},{10,18},{18,10},{11,19},{19,11},{12,20... | collective-permute-start | bytes 786440 | tf_op jit(solution)/shard_map/ppermute | solution.py:254
  40.7 18.4 %copy-start.14 = (bf16[512,512]{1,0:T(8,128)(2,1)S(1)}, bf16[512,512]{1,0:T(8,128)(2,1)}, u32[]{:S(2)}) copy-start(bf16[512,512]{1,0:T(8,128)(2,1)} %copy-done.13) | copy-start | bytes 1572868
  40.7 5.2 %collective-permute-start.1 = (f32[128,512]{1,0:T(8,128)}, f32[128,512]{1,0:T(8,128)}, u32[]{:S(2)}, u32[]{:S(2)}) collective-permute-start(f32[128,512]{1,0:T(8,128)} %add_select_fusion.4), channel_id=1, source_target_pairs={{8,16},{16,8},{9,17},{17,9},{10,18},{18,10},{11,19},{19,11},{12,20... | collective-permute-start | bytes 786440 | tf_op jit(solution)/shard_map/ppermute | solution.py:254
  42.2 29.1 %collective-permute-start.8 = (f32[512,512]{1,0:T(8,128)}, f32[512,512]{1,0:T(8,128)}, u32[]{:S(2)}, u32[]{:S(2)}) collective-permute-start(f32[512,512]{1,0:T(8,128)} %collective-permute-done.7.near_a), channel_id=1, source_target_pairs={{0,4},{4,0},{1,5},{5,1},{2,6},{6,2},{3,7},{7,3},{8,12},{12,8},{9,1... | collective-permute-start | bytes 3145736 | tf_op jit(solution)/shard_map/ppermute | solution.py:345
  42.2 34.5 %collective-permute-start.10 = (f32[512,512]{1,0:T(8,128)}, f32[512,512]{1,0:T(8,128)}, u32[]{:S(2)}, u32[]{:S(2)}) collective-permute-start(f32[512,512]{1,0:T(8,128)} %collective-permute-done.9.near_b), channel_id=1, source_target_pairs={{0,4},{4,0},{1,5},{5,1},{2,6},{6,2},{3,7},{7,3},{8,12},{12,8},{9,1... | collective-permute-start | bytes 3145736 | tf_op jit(solution)/shard_map/ppermute | solution.py:346
  44.6 13.4 %collective-permute-start.5 = (f32[128,512]{1,0:T(8,128)}, f32[128,512]{1,0:T(8,128)S(1)}, u32[]{:S(2)}, u32[]{:S(2)}) collective-permute-start(f32[128,512]{1,0:T(8,128)} %add_select_fusion), channel_id=1, source_target_pairs={{16,24},{8,0},{17,25},{9,1},{18,26},{10,2},{19,27},{11,3},{20,28},... | collective-permute-start | bytes 786440 | tf_op jit(solution)/shard_map/ppermute | solution.py:254
  47.0 18.0 %collective-permute-start.2 = (f32[128,512]{1,0:T(8,128)S(1)}, f32[128,512]{1,0:T(8,128)S(1)}, u32[]{:S(2)}, u32[]{:S(2)}) collective-permute-start(f32[128,512]{1,0:T(8,128)S(1)} %add_select_fusion.3), channel_id=1, source_target_pairs={{16,24},{8,0},{17,25},{9,1},{18,26},{10,2},{19,27},{11,3},{20,28},... | collective-permute-start | bytes 786440 | tf_op jit(solution)/shard_map/ppermute | solution.py:254
  64.0 18.1 %collective-permute-start.17 = (f32[512,256]{1,0:T(8,128)}, f32[512,256]{1,0:T(8,128)S(1)}, u32[]{:S(2)}, u32[]{:S(2)}) collective-permute-start(f32[512,256]{1,0:T(8,128)} %get-tuple-element.83), channel_id=1, source_target_pairs={{0,1},{1,0},{2,3},{3,2},{4,5},{5,4},{6,7},{7,6},{8,9},{9,8},{10,11... | collective-permute-start | bytes 1572872 | tf_op jit(solution)/shard_map/ppermute | solution.py:362
  64.5 17.6 %collective-permute-start.18 = (f32[512,256]{1,0:T(8,128)}, f32[512,256]{1,0:T(8,128)S(1)}, u32[]{:S(2)}, u32[]{:S(2)}) collective-permute-start(f32[512,256]{1,0:T(8,128)} %get-tuple-element.85), channel_id=1, source_target_pairs={{0,2},{1,3},{2,0},{3,1},{4,6},{5,7},{6,4},{7,5},{8,10},{9,11},{10,... | collective-permute-start | bytes 1572872 | tf_op jit(solution)/shard_map/ppermute | solution.py:363
  69.8 18.2 %collective-permute-start.11 = (f32[512,256]{1,0:T(8,128)}, f32[512,256]{1,0:T(8,128)S(1)}, u32[]{:S(2)}, u32[]{:S(2)}) collective-permute-start(f32[512,256]{1,0:T(8,128)} %get-tuple-element.75), channel_id=1, source_target_pairs={{0,1},{1,0},{2,3},{3,2},{4,5},{5,4},{6,7},{7,6},{8,9},{9,8},{10,11... | collective-permute-start | bytes 1572872 | tf_op jit(solution)/shard_map/ppermute | solution.py:362
  71.3 17.0 %collective-permute-start.12 = (f32[512,256]{1,0:T(8,128)S(1)}, f32[512,256]{1,0:T(8,128)S(1)}, u32[]{:S(2)}, u32[]{:S(2)}) collective-permute-start(f32[512,256]{1,0:T(8,128)S(1)} %get-tuple-element.77), channel_id=1, source_target_pairs={{0,2},{1,3},{2,0},{3,1},{4,6},{5,7},{6,4},{7,5},{8,10},{9,11},{10,... | collective-permute-start | bytes 1572872 | tf_op jit(solution)/shard_map/ppermute | solution.py:363
  76.7 16.8 %collective-permute-start.25 = (f32[512,256]{1,0:T(8,128)S(1)}, f32[512,256]{1,0:T(8,128)S(1)}, u32[]{:S(2)}, u32[]{:S(2)}) collective-permute-start(f32[512,256]{1,0:T(8,128)S(1)} %get-tuple-element.91), channel_id=1, source_target_pairs={{0,4},{4,0},{1,5},{5,1},{2,6},{6,2},{3,7},{7,3},{8,12},{12,8},{9,1... | collective-permute-start | bytes 1572872 | tf_op jit(solution)/shard_map/ppermute | solution.py:382
  86.5 14.8 %collective-permute-start.19 = (f32[512,256]{1,0:T(8,128)S(1)}, f32[512,256]{1,0:T(8,128)S(1)}, u32[]{:S(2)}, u32[]{:S(2)}) collective-permute-start(f32[512,256]{1,0:T(8,128)S(1)} %get-tuple-element.88), channel_id=1, source_target_pairs={{0,2},{1,3},{2,0},{3,1},{4,6},{5,7},{6,4},{7,5},{8,10},{9,11},{10,... | collective-permute-start | bytes 1572872 | tf_op jit(solution)/shard_map/ppermute | solution.py:368
  87.1 14.8 %collective-permute-start.20 = (f32[512,256]{1,0:T(8,128)S(1)}, f32[512,256]{1,0:T(8,128)S(1)}, u32[]{:S(2)}, u32[]{:S(2)}) collective-permute-start(f32[512,256]{1,0:T(8,128)S(1)} %get-tuple-element.89), channel_id=1, source_target_pairs={{0,1},{1,0},{2,3},{3,2},{4,5},{5,4},{6,7},{7,6},{8,9},{9,8},{10,11... | collective-permute-start | bytes 1572872 | tf_op jit(solution)/shard_map/ppermute | solution.py:369
  91.1 21.0 %collective-permute-start.13 = (f32[512,256]{1,0:T(8,128)S(1)}, f32[512,256]{1,0:T(8,128)S(1)}, u32[]{:S(2)}, u32[]{:S(2)}) collective-permute-start(f32[512,256]{1,0:T(8,128)S(1)} %get-tuple-element.80), channel_id=1, source_target_pairs={{0,2},{1,3},{2,0},{3,1},{4,6},{5,7},{6,4},{7,5},{8,10},{9,11},{10,... | collective-permute-start | bytes 1572872 | tf_op jit(solution)/shard_map/ppermute | solution.py:368
  92.0 20.3 %collective-permute-start.14 = (f32[512,256]{1,0:T(8,128)S(1)}, f32[512,256]{1,0:T(8,128)S(1)}, u32[]{:S(2)}, u32[]{:S(2)}) collective-permute-start(f32[512,256]{1,0:T(8,128)S(1)} %get-tuple-element.81), channel_id=1, source_target_pairs={{0,1},{1,0},{2,3},{3,2},{4,5},{5,4},{6,7},{7,6},{8,9},{9,8},{10,11... | collective-permute-start | bytes 1572872 | tf_op jit(solution)/shard_map/ppermute | solution.py:369
  93.6 8.4 %collective-permute-start.26 = (f32[256,256]{1,0:T(8,128)S(1)}, f32[256,256]{1,0:T(8,128)S(1)}, u32[]{:S(2)}, u32[]{:S(2)}) collective-permute-start(f32[256,256]{1,0:T(8,128)S(1)} %slice_add_fusion), channel_id=1, source_target_pairs={{0,8},{8,0},{16,24},{24,16},{1,9},{9,1},{17,25},{25,17},{2,10},{10... | collective-permute-start | bytes 786440 | tf_op jit(solution)/shard_map/ppermute | solution.py:241
  101.9 16.8 %collective-permute-start.21 = (f32[2,256,256]{2,1,0:T(8,128)S(1)}, f32[2,256,256]{2,1,0:T(8,128)S(1)}, u32[]{:S(2)}, u32[]{:S(2)}) collective-permute-start(f32[2,256,256]{2,1,0:T(8,128)S(1)} %fusion.1), channel_id=1, source_target_pairs={{0,8},{8,0},{16,24},{24,16},{1,9},{9,1},{17,25},{25,17},{2,10},{10... | collective-permute-start | bytes 1572872 | tf_op jit(solution)/shard_map/ppermute | solution.py:241
  102.0 15.1 %collective-permute-start.27 = (f32[128,256]{1,0:T(8,128)S(1)}, f32[128,256]{1,0:T(8,128)S(1)}, u32[]{:S(2)}, u32[]{:S(2)}) collective-permute-start(f32[128,256]{1,0:T(8,128)S(1)} %slice_add_fusion.5), channel_id=1, source_target_pairs={{0,16},{8,24},{16,0},{24,8},{1,17},{9,25},{17,1},{25,9},{2,18},{10... | collective-permute-start | bytes 393224 | tf_op jit(solution)/shard_map/ppermute | solution.py:241
  112.4 21.8 %collective-permute-start.15 = (f32[2,256,256]{2,1,0:T(8,128)S(1)}, f32[2,256,256]{2,1,0:T(8,128)S(1)}, u32[]{:S(2)}, u32[]{:S(2)}) collective-permute-start(f32[2,256,256]{2,1,0:T(8,128)S(1)} %fusion.4), channel_id=1, source_target_pairs={{0,8},{8,0},{16,24},{24,16},{1,9},{9,1},{17,25},{25,17},{2,10},{10... | collective-permute-start | bytes 1572872 | tf_op jit(solution)/shard_map/ppermute | solution.py:241
  112.6 38.0 %collective-permute-start.6 = (f32[512,512]{1,0:T(8,128)S(1)}, f32[512,512]{1,0:T(8,128)S(1)}, u32[]{:S(2)}, u32[]{:S(2)}) collective-permute-start(f32[512,512]{1,0:T(8,128)S(1)} %get-tuple-element.69), channel_id=1, source_target_pairs={{0,4},{4,0},{1,5},{5,1},{2,6},{6,2},{3,7},{7,3},{8,12},{12,8},{9,1... | collective-permute-start | bytes 3145736 | tf_op jit(solution)/shard_map/ppermute | solution.py:379
  117.2 17.7 %collective-permute-start.28 = (f32[64,256]{1,0:T(8,128)S(1)}, f32[64,256]{1,0:T(8,128)S(1)}, u32[]{:S(2)}, u32[]{:S(2)}) collective-permute-start(f32[64,256]{1,0:T(8,128)S(1)} %slice_add_fusion.7), channel_id=1, source_target_pairs={{0,1},{1,0},{2,3},{3,2},{4,5},{5,4},{6,7},{7,6},{8,9},{9,8},{10,11... | collective-permute-start | bytes 196616 | tf_op jit(solution)/shard_map/ppermute | solution.py:241
  118.7 17.7 %collective-permute-start.22 = (f32[2,128,256]{2,1,0:T(8,128)S(1)}, f32[2,128,256]{2,1,0:T(8,128)S(1)}, u32[]{:S(2)}, u32[]{:S(2)}) collective-permute-start(f32[2,128,256]{2,1,0:T(8,128)S(1)} %slice_add_fusion.1), channel_id=1, source_target_pairs={{0,16},{8,24},{16,0},{24,8},{1,17},{9,25},{17,1},{25,9},{2,18},{10... | collective-permute-start | bytes 786440 | tf_op jit(solution)/shard_map/ppermute | solution.py:241
  134.3 13.6 %collective-permute-start.16 = (f32[2,128,256]{2,1,0:T(8,128)S(1)}, f32[2,128,256]{2,1,0:T(8,128)S(1)}, u32[]{:S(2)}, u32[]{:S(2)}) collective-permute-start(f32[2,128,256]{2,1,0:T(8,128)S(1)} %slice_add_fusion.3), channel_id=1, source_target_pairs={{0,16},{8,24},{16,0},{24,8},{1,17},{9,25},{17,1},{25,9},{2,18},{10... | collective-permute-start | bytes 786440 | tf_op jit(solution)/shard_map/ppermute | solution.py:241
  134.9 15.0 %collective-permute-start.29 = (f32[32,256]{1,0:T(8,128)S(1)}, f32[32,256]{1,0:T(8,128)S(1)}, u32[]{:S(2)}, u32[]{:S(2)}) collective-permute-start(f32[32,256]{1,0:T(8,128)S(1)} %slice_add_fusion.10), channel_id=1, source_target_pairs={{0,2},{1,3},{2,0},{3,1},{4,6},{5,7},{6,4},{7,5},{8,10},{9,11},{10,... | collective-permute-start | bytes 98312 | tf_op jit(solution)/shard_map/ppermute | solution.py:241
  147.9 5.5 %collective-permute-start.23 = (f32[2,64,256]{2,1,0:T(8,128)S(1)}, f32[2,64,256]{2,1,0:T(8,128)S(1)}, u32[]{:S(2)}, u32[]{:S(2)}) collective-permute-start(f32[2,64,256]{2,1,0:T(8,128)S(1)} %get-tuple-element.98), channel_id=1, source_target_pairs={{0,1},{1,0},{2,3},{3,2},{4,5},{5,4},{6,7},{7,6},{8,9},{9,8},{10,11... | collective-permute-start | bytes 393224 | tf_op jit(solution)/shard_map/ppermute | solution.py:386
  148.5 5.0 %collective-permute-start.24 = (f32[2,64,256]{2,1,0:T(8,128)S(1)}, f32[2,64,256]{2,1,0:T(8,128)S(1)}, u32[]{:S(2)}, u32[]{:S(2)}) collective-permute-start(f32[2,64,256]{2,1,0:T(8,128)S(1)} %get-tuple-element.99), channel_id=1, source_target_pairs={{0,2},{1,3},{2,0},{3,1},{4,6},{5,7},{6,4},{7,5},{8,10},{9,11},{10,... | collective-permute-start | bytes 393224 | tf_op jit(solution)/shard_map/ppermute | solution.py:387
  (20 other events, 83.9 us)

commit v3 on v2

v3 whole, which is shorter than its diff:
```python
import functools

import jax
import jax.numpy as jnp
from jax import lax
from jax.experimental import pallas as pl
from jax.experimental.pallas import tpu as pltpu
from jax.sharding import PartitionSpec as P

CHUNK = 128
SHARES = (1, 1, 1, 1)
LIMIT = 24 * 1024 * 1024
LARGE = 60 * 1024 * 1024
SMALL = 16 * 1024 * 1024
f32 = jnp.float32
bf16 = jnp.bfloat16


def dot(a, b, ca=1, cb=0):
    return lax.dot_general(a, b, (((ca,), (cb,)), ((), ())), preferred_element_type=f32)


def log2(n):
    bits = n.bit_length() - 1
    assert 1 << bits == n
    return bits


def place(index, order):
    out = 0
    for rank, bit in enumerate(order):
        out = out + (((index >> bit) & 1) << (len(order) - 1 - rank))
    return out


def spread(values, first, heads, size):
    total = values.shape[0]
    row = lax.broadcasted_iota(jnp.int32, (total, heads * size), 0)
    col = lax.broadcasted_iota(jnp.int32, (total, heads * size), 1)
    low = (row - first) * size
    pick = jnp.where((col >= low) & (col < low + size), 1.0, 0.0).astype(bf16)
    high = values.astype(bf16)
    rest = values - high.astype(f32)
    middle = rest.astype(bf16)
    last = (rest - middle.astype(f32)).astype(bf16)
    return dot(high, pick, 0, 0) + dot(middle, pick, 0, 0) + dot(last, pick, 0, 0)


def triangle(upper):
    row = lax.broadcasted_iota(jnp.int32, (CHUNK, CHUNK), 0)
    col = lax.broadcasted_iota(jnp.int32, (CHUNK, CHUNK), 1)
    return row <= col if upper else row >= col


def one_hot_rows(offsets, rows):
    node = lax.broadcasted_iota(jnp.int32, (rows, offsets.shape[1]), 0)
    return jnp.where(node == offsets, 1.0, 0.0).astype(bf16)


def chunk_rows(cum_x, k):
    part = cum_x[k * CHUNK:(k + 1) * CHUNK]
    return part, part[CHUNK // 2 - 1:CHUNK // 2], part[CHUNK - 1:CHUNK]


def end_states(cum_x, x, dy, sc, sb, xs, ys, near):
    count = cum_x.shape[0] // CHUNK
    forward, back, decay = [], [], []
    for k in range(count):
        span = slice(k * CHUNK, (k + 1) * CHUNK)
        part, mid, last = chunk_rows(cum_x, k)
        x_s = (x[span] * jnp.exp(mid - part)).astype(bf16)
        y_s = (dy[span] * jnp.exp(part - mid)).astype(bf16)
        xs[span, :] = x_s
        ys[span, :] = y_s
        forward.append(jnp.exp(last - mid) * dot(sb[span, CHUNK:], x_s, 0, 0))
        back.append(jnp.exp(mid) * dot(sc[span, CHUNK:], y_s, 0, 0))
        decay.append(jnp.exp(last))
    run, run_back, factor = forward[0], back[-1], decay[0]
    for k in range(1, count):
        run = decay[k] * run + forward[k]
        factor = factor * decay[k]
        run_back = decay[count - 1 - k] * run_back + back[count - 1 - k]
    state = run.shape[0]
    near[:state, :] = run
    near[state:2 * state, :] = run_back
    near[2 * state:, :] = jnp.broadcast_to(factor, (8, factor.shape[1]))


def order_kernel(firsts, counts, size, ids, off, decays, *refs):
    sources, refs = refs[:5], refs[5:]
    outs = len(refs) // 2 - 3
    targets, refs = refs[:outs], refs[outs:]
    (tokens_v, cot_v, state_v, inner_v, out_v), refs = refs[:5], refs[5:]
    held, sems = refs[:outs], refs[outs]
    ordered, ordered_grad, early, sc, sb, cum = held[:6]
    loads = [pltpu.make_async_copy(source, target, sems.at[i])
             for i, (source, target) in enumerate(zip(sources, (tokens_v, cot_v, state_v, inner_v, out_v)))]
    stores = [pltpu.make_async_copy(source, target, sems.at[5 + i]) for i, (source, target) in enumerate(zip(held, targets))]
    for load in loads:
        load.start()
    base, role = ids[1], ids[4]
    rows = tokens_v.shape[0]
    hot = one_hot_rows(off[...] - base, rows)
    lower = triangle(False)
    upper = triangle(True)
    ones = jnp.where(upper, 1.0, 0.0)
    rates = jnp.log(decays[...])
    for k in range(rows // CHUNK):
        span = slice(k * CHUNK, (k + 1) * CHUNK)
        cum[:, span] = jnp.dot(rates[:, span], ones, precision=lax.Precision.HIGHEST, preferred_element_type=f32)
    stores[5].start()
    loads[0].wait()
    ordered[...] = dot(hot, tokens_v[...], 0, 0).astype(bf16)
    stores[0].start()
    loads[1].wait()
    ordered_grad[...] = dot(hot, cot_v[...], 0, 0).astype(bf16)
    stores[1].start()
    early[...] = jnp.where(role == 0, ordered_grad[...].astype(f32), ordered[...].astype(f32))
    stores[2].start()
    loads[2].wait()
    bc = dot(ordered[...], state_v[...]).astype(bf16)
    state = bc.shape[1] // 2
    for k in range(rows // CHUNK):
        span = slice(k * CHUNK, (k + 1) * CHUNK)
        b, c = bc[span, :state], bc[span, state:]
        sc[span, :CHUNK] = jnp.where(lower, dot(c, b, 1, 1), 0.0).astype(bf16)
        sc[span, CHUNK:] = c
        sb[span, :CHUNK] = jnp.where(upper, dot(b, c, 1, 1), 0.0).astype(bf16)
        sb[span, CHUNK:] = b
    stores[3].start()
    stores[4].start()
    loads[3].wait()
    loads[4].wait()
    for r, (first, heads) in enumerate(zip(firsts, counts)):
        cut = slice(first * size, (first + heads) * size)
        cum_x = spread(cum[...], first, heads, size)
        x = dot(ordered[...], inner_v[:, cut]).astype(bf16).astype(f32)
        dy = dot(ordered_grad[...], out_v[:, cut]).astype(bf16).astype(f32)
        end_states(cum_x, x, dy, sc, sb, *held[6 + 3 * r:9 + 3 * r])
        for i in range(6 + 3 * r, 9 + 3 * r):
            stores[i].start()
    for store in stores:
        store.wait()


def join_kernel(ids, near, came, out):
    state = out.shape[0]
    lower, odd = ids[5] < 2, ids[5] & 1 == 1
    own = jnp.where(lower, near[:state, :], near[state:2 * state, :])
    other = jnp.where(lower, came[:state, :], came[state:2 * state, :])
    out[...] = jnp.where(odd == lower, own + near[2 * state:2 * state + 1, :] * other,
                         other + came[2 * state:2 * state + 1, :] * own)


def turn_kernel(orders, ids, ordered, ordered_grad, near, left):
    me, side, role = ids[0], ids[2], ids[4]
    rows, width = ordered.shape
    half = width // 2
    blocks = 1 << len(orders[0])
    size = width // blocks
    for part in range(2):
        span = slice(part * half, (part + 1) * half)
        own = jnp.where(role == 0, ordered[:, span].astype(f32), ordered_grad[:, span].astype(f32)).astype(bf16)
        value = jnp.concatenate([own.T, near[:, span].astype(bf16).T], axis=1)
        for block in range(blocks // 2):
            index = (block + part * (blocks // 2)) ^ me
            where = jnp.where(side == 0, place(index, orders[0]), place(index, orders[1]))
            left[pl.ds(pl.multiple_of(where * size, size), size), :] = value[block * size:(block + 1) * size]


def outputs_kernel(first, heads, size, pieces, ready, ids, xs, ys, sc, sb, cum, came, *refs):
    far = None if ready else refs[0]
    refs = refs if ready else refs[1:]
    owns, sends, (grad_x, grad_bc) = refs[:pieces], refs[pieces:2 * pieces], refs[2 * pieces:]
    cum_x = spread(cum[...], first, heads, size)
    count = cum_x.shape[0] // CHUNK
    lower = triangle(False)
    upper = triangle(True)
    role = ids[4]
    state = (came.shape[0] - 8) // 2
    before, after = came[:state, :], came[state:2 * state, :]
    if not ready:
        factor = came[2 * state:2 * state + 1, :]
        first_half, odd = ids[5] < 2, ids[5] & 1 == 1
        before, after = (
            jnp.where(odd, before + jnp.where(first_half, 0.0, factor * far[...]), jnp.where(first_half, 0.0, far[...])),
            jnp.where(odd, jnp.where(first_half, far[...], 0.0), after + jnp.where(first_half, factor * far[...], 0.0)))
    starts, afters = [before], [after]
    for k in range(count - 1):
        span = slice(k * CHUNK, (k + 1) * CHUNK)
        _, mid, last = chunk_rows(cum_x, k)
        starts.append(jnp.exp(last) * starts[-1] + jnp.exp(last - mid) * dot(sb[span, CHUNK:], xs[span, :], 0, 0))
    for k in range(count - 1, 0, -1):
        span = slice(k * CHUNK, (k + 1) * CHUNK)
        _, mid, last = chunk_rows(cum_x, k)
        afters.insert(0, jnp.exp(last) * afters[0] + jnp.exp(mid) * dot(sc[span, CHUNK:], ys[span, :], 0, 0))
    for k in range(count):
        span = slice(k * CHUNK, (k + 1) * CHUNK)
        part, mid, last = chunk_rows(cum_x, k)
        x_s, y_s = xs[span, :], ys[span, :]
        x_rows = jnp.concatenate([x_s, (starts[k] * jnp.exp(mid)).astype(bf16)], axis=0)
        y_rows = jnp.concatenate([y_s, (afters[k] * jnp.exp(last - mid)).astype(bf16)], axis=0)
        y = (jnp.exp(part - mid) * dot(sc[span, :], x_rows)).astype(bf16)
        dx = (jnp.exp(mid - part) * dot(sb[span, :], y_rows)).astype(bf16)
        grad_x[span, :] = dx
        y, dx = y.astype(f32), dx.astype(f32)
        for i, (own, send) in enumerate(zip(owns, sends)):
            cut = slice(i * own.shape[1], (i + 1) * own.shape[1])
            own[span, :] = jnp.where(role == 0, dx[:, cut], y[:, cut]).astype(bf16)
            send[span, :] = jnp.where(role == 0, y[:, cut], dx[:, cut])
        by_y = dot(y_s, x_rows, 1, 1)
        by_x = dot(x_s, y_rows, 1, 1)
        pairs = jnp.where(lower, by_y[:, :CHUNK], 0.0).astype(bf16)
        turned = jnp.where(upper, by_x[:, :CHUNK], 0.0).astype(bf16)
        grad_bc[span, :state] = dot(turned, sc[span, CHUNK:]) + by_x[:, CHUNK:]
        grad_bc[span, state:] = dot(pairs, sb[span, CHUNK:]) + by_y[:, CHUNK:]


def grads_kernel(left, own, came, keep, send):
    half = left.shape[0] // 2
    right = jnp.concatenate([own[...], came[...].astype(bf16)], axis=0)
    send[...] = dot(left[half:, :], right)
    keep[...] = dot(left[:half, :], right)


def back_kernel(rounds, s_order, ids, *refs):
    grads, sums = refs[:rounds], refs[rounds:2 * rounds]
    w_inner, w_state, ordered, keep, state_keep, send, table = refs[2 * rounds:]
    side, me_state = ids[2], ids[3]
    grad_bc = sums[0][...]
    for part in sums[1:]:
        grad_bc = grad_bc + part[...]
    grad_bc = grad_bc.astype(bf16)
    width = ordered.shape[1]
    half = width // 2
    for out, which in ((send, 1 - side), (keep, side)):
        rows = pl.ds(pl.multiple_of(which * half, half), half)
        value = dot(grad_bc, w_state[rows, :], 1, 1)
        start = 0
        for part in grads:
            cols = part.shape[1]
            value = value + dot(part[...], w_inner[rows, start:start + cols], 1, 1)
            start += cols
        out[:, :half] = value
    fine = width >> len(s_order)
    step = width // 4
    for quarter in range(4):
        value = dot(ordered[:, quarter * step:(quarter + 1) * step], grad_bc, 0, 0)
        for piece in range(step // fine):
            index = (quarter * step) // fine + piece
            where = place(index ^ me_state, s_order)
            table[pl.ds(pl.multiple_of(where * fine, fine), fine), :] = value[piece * fine:(piece + 1) * fine]
    state_keep[...] = table[:half, :]
    send[:, half:] = table[half:, :]


def place_kernel(ids, off, keep, came, out):
    hot = one_hot_rows(off[...] - ids[1], out.shape[0])
    out[...] = dot(hot, (keep[...] + came[:, :keep.shape[1]]).astype(bf16)).astype(bf16)


def finish_kernel(rounds, ids, *refs):
    halves, (swap, d_inner, d_out) = refs[:rounds], refs[rounds:]
    block = d_inner.shape[0]
    start = 0
    for half in halves:
        cut = slice(start, start + half.shape[1])
        own, other = half[:block, :], swap[:, cut]
        d_inner[:, cut] = jnp.where(ids[4] == 0, own, other)
        d_out[:, cut] = jnp.where(ids[4] == 0, other, own)
        start += half.shape[1]


def flips(axis, bit):
    return [(i, i ^ (1 << bit)) for i in range(lax.axis_size(axis))]


def cross(value, bits):
    count = lax.axis_size("seq")
    pairs = [(h * count + s, h * count + (s ^ (1 << bit))) for h, bit in enumerate(bits) for s in range(count)]
    return lax.ppermute(value, ("heads", "seq"), pairs)


def total_of(parts, start, stop):
    out = parts[0][start:stop]
    for part in parts[1:]:
        out = out + part[start:stop]
    return out


def chain(near):
    count, mine = lax.axis_size("order"), lax.axis_index("order")
    state = (near.shape[0] - 8) // 2
    forward, back, total = near[:state], near[state:2 * state], near[2 * state:2 * state + 1]
    run, run_back = jnp.zeros_like(forward), jnp.zeros_like(back)
    for k in range(1, count):
        up = lax.ppermute(total * run + forward, "order", [(k - 1, k)])
        down = lax.ppermute(total * run_back + back, "order", [(count - k, count - k - 1)])
        run = jnp.where(mine == k, up, run)
        run_back = jnp.where(mine == count - k - 1, down, run_back)
    return jnp.concatenate([run, run_back, jnp.zeros_like(near[2 * state:])], axis=0)


class Line:
    def __init__(self, value):
        self.last = value

    def tie(self, *values):
        out = lax.optimization_barrier((self.last,) + values)
        self.last = out[0]
        return out[1:] if len(values) > 1 else out[1]

    def did(self, value):
        self.last = value


class Sum:
    def __init__(self, line, parts, hops):
        self.line, self.parts, self.hops = line, parts, list(hops)

    def hop(self):
        axis, bit = self.hops.pop(0)
        rows = self.parts[0].shape[0] // 2
        tied = self.line.tie(*self.parts)
        message = total_of(tied, rows, 2 * rows)
        self.line.did(message)
        self.parts = [p[:rows] for p in tied] + [lax.ppermute(message, axis, flips(axis, bit))]

    def result(self):
        return total_of(self.parts, 0, self.parts[0].shape[0])


def whole(array):
    return pl.BlockSpec(array.shape, lambda *_: (0,) * len(array.shape))


def call(kernel, outs, args, name, scratch=(), specs=None, limit=LIMIT, out_specs=None):
    specs = specs or {}
    out_specs = out_specs or {}
    in_specs = []
    for i, arg in enumerate(args):
        if i in specs:
            in_specs.append(specs[i])
        elif arg.dtype == jnp.int32 and arg.ndim == 1:
            in_specs.append(pl.BlockSpec(memory_space=pltpu.SMEM))
        else:
            in_specs.append(whole(arg))
    return pl.pallas_call(
        kernel,
        out_shape=tuple(outs),
        grid=(1,),
        in_specs=in_specs,
        out_specs=tuple(out_specs.get(i, whole(o)) for i, o in enumerate(outs)),
        scratch_shapes=list(scratch),
        compiler_params=pltpu.CompilerParams(vmem_limit_bytes=limit),
        cost_estimate=pl.CostEstimate(flops=16_000_000_000, bytes_accessed=1000, transcendentals=0),
        name=name,
    )(*args)


def per_device(tokens, cotangent, node_order, decays, w_inner, w_state, w_out):
    assert tokens.shape[0] == 1
    tokens, cotangent, decays = tokens[0], cotangent[0], decays[0]
    rows, width = tokens.shape
    heads = decays.shape[1]
    inner = w_inner.shape[1]
    size = inner // heads
    state = w_state.shape[1] // 2
    unit = heads // sum(SHARES)
    firsts = [unit * sum(SHARES[:r]) for r in range(len(SHARES))]
    counts = [unit * share for share in SHARES]
    n_order, n_heads, n_seq = (lax.axis_size(a) for a in ("order", "heads", "seq"))
    o, h, s = (lax.axis_index(a) for a in ("order", "heads", "seq"))
    seq_bits, head_bits, order_bits = log2(n_seq), log2(n_heads), log2(n_order)
    assert seq_bits == 2 and head_bits == 1
    order_hops = [("order", b) for b in range(order_bits)]
    s_hops = [("heads", 0)] + order_hops + [("seq", 0), ("seq", 1)]
    shift_state = {"seq": 0, "heads": seq_bits, "order": seq_bits + head_bits}
    s_order = [shift_state[a] + b for a, b in s_hops]
    pair_bits, sum_bits = (0, 1), (1, 0)
    orders = [[sum_bits[c]] + [seq_bits + b for b in range(order_bits)] + [pair_bits[c]] for c in range(2)]
    role = jnp.where(h == 0, s & 1, (s >> 1) & 1)
    ids = jnp.stack([o * n_seq + s, o * rows, h, (o * n_heads + h) * n_seq + s, role, o]).astype(jnp.int32)
    S = jax.ShapeDtypeStruct
    full = S((rows, width), bf16)
    sent = S((rows, width), f32)
    wide = S((rows, CHUNK + state), bf16)
    far_space = pl.BlockSpec(memory_space=pltpu.HBM)

    outs = [full, full, sent, wide, wide, S((heads, rows), f32)]
    for count in counts:
        outs += [S((rows, count * size), bf16)] * 2 + [S((2 * state + 8, count * size), f32)]
    order_args = [ids, node_order, decays.T, tokens, cotangent, w_state, w_inner, w_out]
    made = call(
        functools.partial(order_kernel, firsts, counts, size), outs, order_args, "order",
        specs={i: far_space for i in range(3, 8)}, out_specs={i: far_space for i in range(len(outs))},
        scratch=[pltpu.VMEM(a.shape, a.dtype) for a in order_args[3:] + outs] + [pltpu.SemaphoreType.DMA((5 + len(outs),))],
        limit=LARGE)
    ordered, ordered_grad, early, sc, sb, cum = made[:6]
    count_rounds = len(SHARES)
    line = Line(ids)
    tree = n_order == 4
    nears = {0: lax.ppermute(made[8], "order", flips("order", 0)) if tree else chain(made[8])}
    near_tokens = cross(early, pair_bits)
    incoming, owns, swapped, grads, sums, halves = {}, {}, {}, {}, {}, {}
    held = {}

    def join(r):
        near = made[8 + 3 * r]
        if tree:
            came = nears[r]
            joined, = call(join_kernel, [S((state, near.shape[1]), f32)], [line.tie(ids), near, came], f"join_{r}")
            line.did(joined)
            incoming[r] = (came, lax.ppermute(joined, "order", flips("order", 1)))
            if r + 1 < count_rounds:
                following, _ = lax.optimization_barrier((made[11 + 3 * r], joined))
                nears[r + 1] = lax.ppermute(following, "order", flips("order", 0))
        else:
            incoming[r] = (nears[r],)
            if r + 1 < count_rounds:
                nears[r + 1] = chain(made[11 + 3 * r])

    def outputs(r):
        cols = counts[r] * size
        own, send, grads[r], sums[r] = call(
            functools.partial(outputs_kernel, firsts[r], counts[r], size, 1, not tree),
            [S((rows, cols), bf16), S((rows, cols), f32), S((rows, cols), bf16), S((rows, 2 * state), f32)],
            [line.tie(ids), *made[6 + 3 * r:8 + 3 * r], sc, sb, cum, *incoming[r]], f"outputs_{r}")
        line.did(send)
        owns[r], swapped[r] = own, cross(send, pair_bits)

    def turn():
        held["left"], = call(functools.partial(turn_kernel, orders), [S((width, 2 * rows), bf16)],
                             [line.tie(ids), ordered, ordered_grad, near_tokens], "turn")
        line.did(held["left"])

    def gradients(r):
        half = S((width // 2, counts[r] * size), f32)
        keep, send = call(grads_kernel, [half] * 2, [held["left"], line.tie(owns[r]), swapped[r]], f"grads_{r}")
        line.did(send)
        halves[r] = Sum(line, [keep, cross(send, sum_bits)], order_hops)

    def back():
        keep, state_keep, send = call(
            functools.partial(back_kernel, count_rounds, s_order),
            [S((rows, width // 2), f32), S((width // 2, 2 * state), f32), S((rows, width // 2 + 2 * state), f32)],
            [line.tie(ids)] + [grads[r] for r in range(count_rounds)] + [sums[r] for r in range(count_rounds)]
            + [w_inner, w_state, ordered], "back", scratch=[pltpu.VMEM((width, 2 * state), f32)])
        line.did(send)
        held["keep"], held["came"] = keep, lax.ppermute(send, "heads", flips("heads", 0))
        held["state"] = Sum(line, [state_keep, held["came"][:, width // 2:]], s_hops[1:])

    def place_rows():
        held["tokens"], = call(place_kernel, [S((rows, width // 2), bf16)],
                               [line.tie(ids), node_order, held["keep"], held["came"]], "place")
        line.did(held["tokens"])

    steps = [(8.0, turn), (8.5 * count_rounds - 8, back), (8.5 * count_rounds + 1, place_rows)]
    for r in range(count_rounds):
        start = 8.5 * r
        steps += [(start - 9.5, functools.partial(join, r)), (start, functools.partial(outputs, r)),
                  (start + 11, functools.partial(gradients, r))]
        steps += [(start + 23 + 8 * k, lambda r=r: halves[r].hop()) for k in range(order_bits)]
    steps += [(8.5 * count_rounds + 10 + 8 * k, lambda: held["state"].hop()) for k in range(order_bits)]
    for _, step in sorted(steps, key=lambda entry: entry[0]):
        step()
    halves = [halves[r].result() for r in range(count_rounds)]
    d_tokens = held["tokens"]
    while held["state"].hops:
        held["state"].hop()
    d_w_state = held["state"].result()
    block = width // (n_order * n_seq)
    swap = cross(jnp.concatenate([h[block:] for h in halves], axis=1), pair_bits)
    final = S((block, inner), f32)
    d_w_inner, d_w_out = call(functools.partial(finish_kernel, len(halves)), [final, final],
                              [ids] + halves + [swap], "finish", limit=SMALL)
    return d_tokens[None], d_w_inner, d_w_state, d_w_out


def solution(mesh):
    in_specs = (
        P("seq", "order", None),
        P("seq", "order", None),
        P("seq", "order"),
        P("seq", "order", "heads"),
        P(None, "heads"),
        P(),
        P(None, "heads"),
    )
    out_specs = (
        P("seq", "order", "heads"),
        P(("order", "seq"), "heads"),
        P(("order", "heads", "seq"), None),
        P(("order", "seq"), "heads"),
    )
    return jax.shard_map(
        per_device, mesh=mesh, in_specs=in_specs, out_specs=out_specs, check_vma=False
    )
```

time: 157 us -> 145 us (0.924)
  starting transfers between devices: 34 us -> 48.8 us
  local copies, waits for them, and re-layouts: 12.5 us -> 1.79 us
  other arithmetic: 10.2 us -> 1.36 us
  Pallas kernels: 35.2 us -> 31.9 us
  waiting for transfers between devices: 63 us -> 59.8 us
    ppermute x30 -> x31, starting transfers between devices: 34 us -> 48.8 us  [the longest x12 19.6 us: hop(): lax.ppermute(message, axis, flips(axis, bit))]
    unnamed x45 -> x48, local copies, waits for them, and re-layouts: 10.1 us -> 1.06 us
    select_n x8 -> x0, other arithmetic: 8.94 us -> none  [the longest x6 6.73 us: carries(): message = jnp.where(mine == k - 1, up, down)]
    pallas_call x9 -> x17, Pallas kernels: 35.2 us -> 31.9 us  [call(): pl.pallas_call(kernel, out_shape=tuple(outs), grid=(1,), in_specs=in_spec...]
    ppermute x30 -> x31, waiting for transfers between devices: 63 us -> 59.8 us  [the longest x12 23.8 us: hop(): lax.ppermute(message, axis, flips(axis, bit))]
    reshape x2 -> x0, local copies, waits for them, and re-layouts: 1.83 us -> none  [the longest x1 0.91 us: per_device(): d_w_out = out_blocks.transpose(2, 0, 1, 3).reshape(block, inner)]
  transfers between devices with their start and end apart: 30 -> 31, of which waited for: 15 -> 17; matrix products, arithmetic and copies ran while one was open for 6% -> 1% of each run, Pallas kernels for 18% -> 14%
where the time goes in v3:
time: 145 us
  waiting for transfers between devices  59.8 us (41%)
  starting transfers between devices  48.8 us (34%)
  Pallas kernels  31.9 us (22%)
  local copies, waits for them, and re-layouts  1.79 us (1%)
    pallas_call x17, Pallas kernels, call(): pl.pallas_call(kernel, out_shape=tuple(outs), grid=(1,), in_specs=in_spec...  31.9 us
    ppermute x12, waiting for transfers between devices, hop(): lax.ppermute(message, axis, flips(axis, bit))  23.8 us
    ppermute x10, waiting for transfers between devices, cross(): return lax.ppermute(value, ('heads', 'seq'), pairs)  23.6 us
    ppermute x12, starting transfers between devices, hop(): lax.ppermute(message, axis, flips(axis, bit))  19.6 us
    ppermute x10, starting transfers between devices, cross(): return lax.ppermute(value, ('heads', 'seq'), pairs)  12.2 us
    ppermute x4, starting transfers between devices, join(): incoming[r] = (came, lax.ppermute(joined, 'order', flips('order', 1)))  8.11 us
    ppermute x1, waiting for transfers between devices, per_device(): lax.ppermute(made[8], 'order', flips('order', 0))  6.67 us
    ppermute x3, starting transfers between devices, join(): nears[r + 1] = lax.ppermute(following, 'order', flips('order', 0))  5.77 us
  transfers between devices with their start and end apart: 31, of which 17 were waited for; matrix products, arithmetic and copies ran while one was open for 1% of the time, Pallas kernels for 14%

profile of v3, /device:TPU:0, one launch (start us, length us, event | category | flops | bytes accessed | tf_op | source)
XLA Modules:
  0.0 144.9 jit_solution(11898343861790870512)
XLA Ops:
  1.3 10.4 %order.1 = (bf16[512,1024]{1,0:T(8,128)(2,1)}, bf16[512,1024]{1,0:T(8,128)(2,1)}, f32[512,1024]{1,0:T(8,128)}, bf16[512,256]{1,0:T(8,128)(2,1)}, bf16[512,256]{1...) custom-call(s32[6]{0:T(128)} %stack.27.ids, ...), custom_call_target="tpu_custom_call" | custom-call | flops 16000000000 | bytes 1000 | tf_op jit(solution)/shard_map/order/pallas_call | solution.py:348
  11.7 3.1 %collective-permute-start = (f32[264,256]{1,0:T(8,128)}, f32[264,256]{1,0:T(8,128)S(1)}, u32[]{:S(2)}, u32[]{:S(2)}) collective-permute-start(f32[264,256]{1,0:T(8,128)} %get-tuple-element.104.near), channel_id=1, source_target_pairs={{0,8},{8,0},{16,24},{24,16},{1,9},{9,1},{17,25},{25,17},{2,10},{10... | collective-permute-start | bytes 811016 | tf_op jit(solution)/shard_map/ppermute | solution.py:403
  14.8 6.7 %collective-permute-done.came = f32[264,256]{1,0:T(8,128)S(1)} collective-permute-done((f32[264,256]{1,0:T(8,128)}, f32[264,256]{1,0:T(8,128)S(1)}, u32[]{:S(2)}, u32[]{:S(2)}) %collective-permute-start) | collective-permute-done | bytes 270368 | tf_op jit(solution)/shard_map/ppermute | solution.py:403
  23.0 1.8 %collective-permute-start.1 = (f32[264,256]{1,0:T(8,128)S(1)}, f32[264,256]{1,0:T(8,128)S(1)}, u32[]{:S(2)}, u32[]{:S(2)}) collective-permute-start(f32[264,256]{1,0:T(8,128)S(1)} %copy-done.7), channel_id=1, source_target_pairs={{0,8},{8,0},{16,24},{24,16},{1,9},{9,1},{17,25},{25,17},{2,10},{10... | collective-permute-start | bytes 811016 | tf_op jit(solution)/shard_map/ppermute | solution.py:417
  26.5 2.6 %collective-permute-start.2 = (f32[128,256]{1,0:T(8,128)S(1)}, f32[128,256]{1,0:T(8,128)S(1)}, u32[]{:S(2)}, u32[]{:S(2)}) collective-permute-start(f32[128,256]{1,0:T(8,128)S(1)} %join_0.1), channel_id=1, source_target_pairs={{0,16},{8,24},{16,0},{24,8},{1,17},{9,25},{17,1},{25,9},{2,18},{10... | collective-permute-start | bytes 393224 | tf_op jit(solution)/shard_map/ppermute | solution.py:414
  29.0 4.4 %collective-permute-done.1.came = f32[264,256]{1,0:T(8,128)S(1)} collective-permute-done((f32[264,256]{1,0:T(8,128)S(1)}, f32[264,256]{1,0:T(8,128)S(1)}, u32[]{:S(2)}, u32[]{:S(2)}) %collective-permute-start.1) | collective-permute-done | bytes 270368 | tf_op jit(solution)/shard_map/ppermute | solution.py:417
  35.6 2.5 %collective-permute-start.3 = (f32[264,256]{1,0:T(8,128)S(1)}, f32[264,256]{1,0:T(8,128)S(1)}, u32[]{:S(2)}, u32[]{:S(2)}) collective-permute-start(f32[264,256]{1,0:T(8,128)S(1)} %copy-done.6), channel_id=1, source_target_pairs={{0,8},{8,0},{16,24},{24,16},{1,9},{9,1},{17,25},{25,17},{2,10},{10... | collective-permute-start | bytes 811016 | tf_op jit(solution)/shard_map/ppermute | solution.py:417
  38.1 2.3 %outputs_0.1 = (bf16[512,256]{1,0:T(8,128)(2,1)S(1)}, f32[512,256]{1,0:T(8,128)S(1)}, bf16[512,256]{1,0:T(8,128)(2,1)S(1)}, f32[512,256]{1,0:T(8,128)S(1)}) custom-call(s32[6]{0:T(128)S(1)} %copy-done.2, bf16[512,256]{1,0:T(8,128)(2,1)S(1)} %copy-done.20, bf16[512,256]{1,0:T(8,128)(2,1)S(1)} %copy-done.21, bf16[512,256]{1,0:T(8,128)(2,1)S(1)} %copy-done.12, ...), custom_call_target="tpu_custom_call" | custom-call | flops 16000000000 | bytes 1000 | tf_op jit(solution)/shard_map/outputs_0/pallas_call | solution.py:348
  40.4 1.7 %collective-permute-start.6 = (f32[512,256]{1,0:T(8,128)S(1)}, f32[512,256]{1,0:T(8,128)S(1)}, u32[]{:S(2)}, u32[]{:S(2)}) collective-permute-start(f32[512,256]{1,0:T(8,128)S(1)} %get-tuple-element.114), channel_id=1, source_target_pairs={{0,1},{1,0},{2,3},{3,2},{4,6},{5,7},{6,4},{7,5},{8,9},{9,8},{10,11... | collective-permute-start | bytes 1572872 | tf_op jit(solution)/shard_map/ppermute | solution.py:281
  46.9 4.1 %collective-permute-done.4.near = f32[512,1024]{1,0:T(8,128)S(1)} collective-permute-done((f32[512,1024]{1,0:T(8,128)S(1)}, f32[512,1024]{1,0:T(8,128)S(1)}, u32[]{:S(2)}, u32[]{:S(2)}) %collective-permute-start.4) | collective-permute-done | bytes 2097184 | tf_op jit(solution)/shard_map/ppermute | solution.py:281
  52.3 2.3 %outputs_1.1 = (bf16[512,256]{1,0:T(8,128)(2,1)S(1)}, f32[512,256]{1,0:T(8,128)S(1)}, bf16[512,256]{1,0:T(8,128)(2,1)S(1)}, f32[512,256]{1,0:T(8,128)S(1)}) custom-call(s32[6]{0:T(128)S(1)} %copy-done.2, bf16[512,256]{1,0:T(8,128)(2,1)S(1)} %copy-done.18, bf16[512,256]{1,0:T(8,128)(2,1)S(1)} %copy-done.19, bf16[512,256]{1,0:T(8,128)(2,1)S(1)} %copy-done.12, ...), custom_call_target="tpu_custom_call" | custom-call | flops 16000000000 | bytes 1000 | tf_op jit(solution)/shard_map/outputs_1/pallas_call | solution.py:348
  54.6 2.0 %collective-permute-done.6.came = f32[512,256]{1,0:T(8,128)S(1)} collective-permute-done((f32[512,256]{1,0:T(8,128)S(1)}, f32[512,256]{1,0:T(8,128)S(1)}, u32[]{:S(2)}, u32[]{:S(2)}) %collective-permute-start.6) | collective-permute-done | bytes 524320 | tf_op jit(solution)/shard_map/ppermute | solution.py:281
  57.9 2.7 %collective-permute-start.11 = (f32[128,256]{1,0:T(8,128)S(1)}, f32[128,256]{1,0:T(8,128)S(1)}, u32[]{:S(2)}, u32[]{:S(2)}) collective-permute-start(f32[128,256]{1,0:T(8,128)S(1)} %join_3.1), channel_id=1, source_target_pairs={{0,16},{8,24},{16,0},{24,8},{1,17},{9,25},{17,1},{25,9},{2,18},{10... | collective-permute-start | bytes 393224 | tf_op jit(solution)/shard_map/ppermute | solution.py:414
  63.6 2.5 %outputs_2.1 = (bf16[512,256]{1,0:T(8,128)(2,1)S(1)}, f32[512,256]{1,0:T(8,128)S(1)}, bf16[512,256]{1,0:T(8,128)(2,1)S(1)}, f32[512,256]{1,0:T(8,128)S(1)}) custom-call(s32[6]{0:T(128)S(1)} %copy-done.2, bf16[512,256]{1,0:T(8,128)(2,1)S(1)} %copy-done.16, bf16[512,256]{1,0:T(8,128)(2,1)S(1)} %copy-done.17, bf16[512,256]{1,0:T(8,128)(2,1)S(1)} %copy-done.12, ...), custom_call_target="tpu_custom_call" | custom-call | flops 16000000000 | bytes 1000 | tf_op jit(solution)/shard_map/outputs_2/pallas_call | solution.py:348
  66.7 5.3 %collective-permute-done.9.came = f32[512,256]{1,0:T(8,128)S(1)} collective-permute-done((f32[512,256]{1,0:T(8,128)S(1)}, f32[512,256]{1,0:T(8,128)S(1)}, u32[]{:S(2)}, u32[]{:S(2)}) %collective-permute-start.9) | collective-permute-done | bytes 524320 | tf_op jit(solution)/shard_map/ppermute | solution.py:281
  72.7 2.8 %collective-permute-done.10 = f32[512,256]{1,0:T(8,128)S(1)} collective-permute-done((f32[512,256]{1,0:T(8,128)S(1)}, f32[512,256]{1,0:T(8,128)S(1)}, u32[]{:S(2)}, u32[]{:S(2)}) %collective-permute-start.10) | collective-permute-done | bytes 524320 | tf_op jit(solution)/shard_map/ppermute | solution.py:281
  76.6 2.3 %outputs_3.1 = (bf16[512,256]{1,0:T(8,128)(2,1)S(1)}, f32[512,256]{1,0:T(8,128)S(1)}, bf16[512,256]{1,0:T(8,128)(2,1)S(1)}, f32[512,256]{1,0:T(8,128)S(1)}) custom-call(s32[6]{0:T(128)S(1)} %copy-done.2, bf16[512,256]{1,0:T(8,128)(2,1)S(1)} %copy-done.14, bf16[512,256]{1,0:T(8,128)(2,1)S(1)} %copy-done.15, bf16[512,256]{1,0:T(8,128)(2,1)S(1)} %copy-done.12, ...), custom_call_target="tpu_custom_call" | custom-call | flops 16000000000 | bytes 1000 | tf_op jit(solution)/shard_map/outputs_3/pallas_call | solution.py:348
  82.0 2.5 %back.1 = (f32[512,512]{1,0:T(8,128)S(1)}, f32[512,256]{1,0:T(8,128)S(1)}, f32[512,768]{1,0:T(8,128)S(1)}) custom-call(s32[6]{0:T(128)S(1)} %copy-done.2, bf16[512,256]{1,0:T(8,128)(2,1)S(1)} %get-tuple-element.147.refs_0_, bf16[512,256]{1,0:T(8,128)(2,1)S(1)} %get-tuple-element.148.refs_1_, bf16[512,256]{1,0:T(8,128)(2,1)S(1)} %get-tuple-element.149.refs_2_, ...), custom_call_target="tpu_custom_call" | custom-call | flops 16000000000 | bytes 1000 | tf_op jit(solution)/shard_map/back/pallas_call | solution.py:348
  86.3 3.7 %collective-permute-done.14 = f32[512,256]{1,0:T(8,128)S(1)} collective-permute-done((f32[512,256]{1,0:T(8,128)S(1)}, f32[512,256]{1,0:T(8,128)S(1)}, u32[]{:S(2)}, u32[]{:S(2)}) %collective-permute-start.14) | collective-permute-done | bytes 524320 | tf_op jit(solution)/shard_map/ppermute | solution.py:281
  91.4 1.8 %place.1 = bf16[512,512]{1,0:T(8,128)(2,1)} custom-call(s32[6]{0:T(128)S(1)} %copy-done.2, s32[1,512]{1,0:T(1,128)S(1)} %copy-done.9, f32[512,512]{1,0:T(8,128)S(1)} %get-tuple-element.166.keep, f32[512,768]{1,0:T(8,128)S(1)} %collective-permute-done.15.came), custom_call_target="tpu_custom_call" | custom-call | flops 16000000000 | bytes 1000 | tf_op jit(solution)/shard_map/place/pallas_call | solution.py:348
  93.9 1.6 %collective-permute-start.23 = (f32[512,256]{1,0:T(8,128)S(1)}, f32[512,256]{1,0:T(8,128)S(1)}, u32[]{:S(2)}, u32[]{:S(2)}) collective-permute-start(f32[512,256]{1,0:T(8,128)S(1)} %get-tuple-element.169), channel_id=1, source_target_pairs={{0,2},{1,3},{2,0},{3,1},{4,5},{5,4},{6,7},{7,6},{8,10},{9,11},{10,... | collective-permute-start | bytes 1572872 | tf_op jit(solution)/shard_map/ppermute | solution.py:281
  95.5 2.6 %collective-permute-done.18 = f32[256,256]{1,0:T(8,128)S(1)} collective-permute-done((f32[256,256]{1,0:T(8,128)S(1)}, f32[256,256]{1,0:T(8,128)S(1)}, u32[]{:S(2)}, u32[]{:S(2)}) %collective-permute-start.18) | collective-permute-done | bytes 262176 | tf_op jit(solution)/shard_map/ppermute | solution.py:327
  98.4 2.6 %collective-permute-start.19 = (f32[128,256]{1,0:T(8,128)S(1)}, f32[128,256]{1,0:T(8,128)S(1)}, u32[]{:S(2)}, u32[]{:S(2)}) collective-permute-start(f32[128,256]{1,0:T(8,128)S(1)} %slice_add_fusion.8), channel_id=1, source_target_pairs={{0,16},{8,24},{16,0},{24,8},{1,17},{9,25},{17,1},{25,9},{2,18},{10... | collective-permute-start | bytes 393224 | tf_op jit(solution)/shard_map/ppermute | solution.py:327
  101.8 7.2 %collective-permute-done.21 = f32[256,256]{1,0:T(8,128)S(1)} collective-permute-done((f32[256,256]{1,0:T(8,128)S(1)}, f32[256,256]{1,0:T(8,128)S(1)}, u32[]{:S(2)}, u32[]{:S(2)}) %collective-permute-start.21) | collective-permute-done | bytes 262176 | tf_op jit(solution)/shard_map/ppermute | solution.py:327
  109.2 5.3 %collective-permute-start.22 = (f32[128,256]{1,0:T(8,128)S(1)}, f32[128,256]{1,0:T(8,128)S(1)}, u32[]{:S(2)}, u32[]{:S(2)}) collective-permute-start(f32[128,256]{1,0:T(8,128)S(1)} %slice_add_fusion.7), channel_id=1, source_target_pairs={{0,16},{8,24},{16,0},{24,8},{1,17},{9,25},{17,1},{25,9},{2,18},{10... | collective-permute-start | bytes 393224 | tf_op jit(solution)/shard_map/ppermute | solution.py:327
  116.0 3.4 %collective-permute-start.28 = (f32[128,256]{1,0:T(8,128)S(1)}, f32[128,256]{1,0:T(8,128)S(1)}, u32[]{:S(2)}, u32[]{:S(2)}) collective-permute-start(f32[128,256]{1,0:T(8,128)S(1)} %get-tuple-element.218), channel_id=1, source_target_pairs={{0,16},{8,24},{16,0},{24,8},{1,17},{9,25},{17,1},{25,9},{2,18},{10... | collective-permute-start | bytes 393224 | tf_op jit(solution)/shard_map/ppermute | solution.py:327
  119.5 4.1 %collective-permute-done.25 = f32[256,256]{1,0:T(8,128)S(1)} collective-permute-done((f32[256,256]{1,0:T(8,128)S(1)}, f32[256,256]{1,0:T(8,128)S(1)}, u32[]{:S(2)}, u32[]{:S(2)}) %collective-permute-start.25) | collective-permute-done | bytes 262176 | tf_op jit(solution)/shard_map/ppermute | solution.py:327
  123.6 4.0 %collective-permute-done.28 = f32[128,256]{1,0:T(8,128)S(1)} collective-permute-done((f32[128,256]{1,0:T(8,128)S(1)}, f32[128,256]{1,0:T(8,128)S(1)}, u32[]{:S(2)}, u32[]{:S(2)}) %collective-permute-start.28) | collective-permute-done | bytes 131104 | tf_op jit(solution)/shard_map/ppermute | solution.py:327
  127.7 3.2 %collective-permute-start.29 = (f32[64,256]{1,0:T(8,128)S(1)}, f32[64,256]{1,0:T(8,128)S(1)}, u32[]{:S(2)}, u32[]{:S(2)}) collective-permute-start(f32[64,256]{1,0:T(8,128)S(1)} %get-tuple-element.222), channel_id=1, source_target_pairs={{0,1},{1,0},{2,3},{3,2},{4,5},{5,4},{6,7},{7,6},{8,9},{9,8},{10,11... | collective-permute-start | bytes 196616 | tf_op jit(solution)/shard_map/ppermute | solution.py:327
  131.1 2.1 %collective-permute-done.29 = f32[64,256]{1,0:T(8,128)S(1)} collective-permute-done((f32[64,256]{1,0:T(8,128)S(1)}, f32[64,256]{1,0:T(8,128)S(1)}, u32[]{:S(2)}, u32[]{:S(2)}) %collective-permute-start.29) | collective-permute-done | bytes 65568 | tf_op jit(solution)/shard_map/ppermute | solution.py:327
  134.6 2.3 %collective-permute-done.26 = f32[128,256]{1,0:T(8,128)S(1)} collective-permute-done((f32[128,256]{1,0:T(8,128)S(1)}, f32[128,256]{1,0:T(8,128)S(1)}, u32[]{:S(2)}, u32[]{:S(2)}) %collective-permute-start.26) | collective-permute-done | bytes 131104 | tf_op jit(solution)/shard_map/ppermute | solution.py:327
  137.8 5.7 %collective-permute-done.27.refs_4_ = f32[64,1024]{1,0:T(8,128)S(1)} collective-permute-done((f32[64,1024]{1,0:T(8,128)S(1)}, f32[64,1024]{1,0:T(8,128)S(1)}, u32[]{:S(2)}, u32[]{:S(2)}) %collective-permute-start.27) | collective-permute-done | bytes 262176 | tf_op jit(solution)/shard_map/ppermute | solution.py:281
  (120 shorter events, 32.1 us)
Async XLA Ops:
  11.7 9.8 %collective-permute-start = (f32[264,256]{1,0:T(8,128)}, f32[264,256]{1,0:T(8,128)S(1)}, u32[]{:S(2)}, u32[]{:S(2)}) collective-permute-start(f32[264,256]{1,0:T(8,128)} %get-tuple-element.104.near), channel_id=1, source_target_pairs={{0,8},{8,0},{16,24},{24,16},{1,9},{9,1},{17,25},{25,17},{2,10},{10... | collective-permute-start | bytes 811016 | tf_op jit(solution)/shard_map/ppermute | solution.py:403
  23.0 10.4 %collective-permute-start.1 = (f32[264,256]{1,0:T(8,128)S(1)}, f32[264,256]{1,0:T(8,128)S(1)}, u32[]{:S(2)}, u32[]{:S(2)}) collective-permute-start(f32[264,256]{1,0:T(8,128)S(1)} %copy-done.7), channel_id=1, source_target_pairs={{0,8},{8,0},{16,24},{24,16},{1,9},{9,1},{17,25},{25,17},{2,10},{10... | collective-permute-start | bytes 811016 | tf_op jit(solution)/shard_map/ppermute | solution.py:417
  24.9 26.1 %collective-permute-start.4 = (f32[512,1024]{1,0:T(8,128)S(1)}, f32[512,1024]{1,0:T(8,128)S(1)}, u32[]{:S(2)}, u32[]{:S(2)}) collective-permute-start(f32[512,1024]{1,0:T(8,128)S(1)} %copy-done.23), channel_id=1, source_target_pairs={{0,1},{1,0},{2,3},{3,2},{4,6},{5,7},{6,4},{7,5},{8,9},{9,8},{10,11... | collective-permute-start | bytes 6291464 | tf_op jit(solution)/shard_map/ppermute | solution.py:281
  26.5 11.6 %collective-permute-start.2 = (f32[128,256]{1,0:T(8,128)S(1)}, f32[128,256]{1,0:T(8,128)S(1)}, u32[]{:S(2)}, u32[]{:S(2)}) collective-permute-start(f32[128,256]{1,0:T(8,128)S(1)} %join_0.1), channel_id=1, source_target_pairs={{0,16},{8,24},{16,0},{24,8},{1,17},{9,25},{17,1},{25,9},{2,18},{10... | collective-permute-start | bytes 393224 | tf_op jit(solution)/shard_map/ppermute | solution.py:414
  34.0 18.3 %collective-permute-start.5 = (f32[128,256]{1,0:T(8,128)S(1)}, f32[128,256]{1,0:T(8,128)S(1)}, u32[]{:S(2)}, u32[]{:S(2)}) collective-permute-start(f32[128,256]{1,0:T(8,128)S(1)} %join_1.1), channel_id=1, source_target_pairs={{0,16},{8,24},{16,0},{24,8},{1,17},{9,25},{17,1},{25,9},{2,18},{10... | collective-permute-start | bytes 393224 | tf_op jit(solution)/shard_map/ppermute | solution.py:414
  35.6 7.9 %collective-permute-start.3 = (f32[264,256]{1,0:T(8,128)S(1)}, f32[264,256]{1,0:T(8,128)S(1)}, u32[]{:S(2)}, u32[]{:S(2)}) collective-permute-start(f32[264,256]{1,0:T(8,128)S(1)} %copy-done.6), channel_id=1, source_target_pairs={{0,8},{8,0},{16,24},{24,16},{1,9},{9,1},{17,25},{25,17},{2,10},{10... | collective-permute-start | bytes 811016 | tf_op jit(solution)/shard_map/ppermute | solution.py:417
  40.4 16.2 %collective-permute-start.6 = (f32[512,256]{1,0:T(8,128)S(1)}, f32[512,256]{1,0:T(8,128)S(1)}, u32[]{:S(2)}, u32[]{:S(2)}) collective-permute-start(f32[512,256]{1,0:T(8,128)S(1)} %get-tuple-element.114), channel_id=1, source_target_pairs={{0,1},{1,0},{2,3},{3,2},{4,6},{5,7},{6,4},{7,5},{8,9},{9,8},{10,11... | collective-permute-start | bytes 1572872 | tf_op jit(solution)/shard_map/ppermute | solution.py:281
  44.1 19.5 %collective-permute-start.8 = (f32[128,256]{1,0:T(8,128)S(1)}, f32[128,256]{1,0:T(8,128)S(1)}, u32[]{:S(2)}, u32[]{:S(2)}) collective-permute-start(f32[128,256]{1,0:T(8,128)S(1)} %join_2.1), channel_id=1, source_target_pairs={{0,16},{8,24},{16,0},{24,8},{1,17},{9,25},{17,1},{25,9},{2,18},{10... | collective-permute-start | bytes 393224 | tf_op jit(solution)/shard_map/ppermute | solution.py:414
  45.4 12.0 %collective-permute-start.7 = (f32[264,256]{1,0:T(8,128)S(1)}, f32[264,256]{1,0:T(8,128)S(1)}, u32[]{:S(2)}, u32[]{:S(2)}) collective-permute-start(f32[264,256]{1,0:T(8,128)S(1)} %copy-done.5), channel_id=1, source_target_pairs={{0,8},{8,0},{16,24},{24,16},{1,9},{9,1},{17,25},{25,17},{2,10},{10... | collective-permute-start | bytes 811016 | tf_op jit(solution)/shard_map/ppermute | solution.py:417
  57.9 18.6 %collective-permute-start.11 = (f32[128,256]{1,0:T(8,128)S(1)}, f32[128,256]{1,0:T(8,128)S(1)}, u32[]{:S(2)}, u32[]{:S(2)}) collective-permute-start(f32[128,256]{1,0:T(8,128)S(1)} %join_3.1), channel_id=1, source_target_pairs={{0,16},{8,24},{16,0},{24,8},{1,17},{9,25},{17,1},{25,9},{2,18},{10... | collective-permute-start | bytes 393224 | tf_op jit(solution)/shard_map/ppermute | solution.py:414
  60.6 14.9 %collective-permute-start.10 = (f32[512,256]{1,0:T(8,128)S(1)}, f32[512,256]{1,0:T(8,128)S(1)}, u32[]{:S(2)}, u32[]{:S(2)}) collective-permute-start(f32[512,256]{1,0:T(8,128)S(1)} %get-tuple-element.128), channel_id=1, source_target_pairs={{0,2},{1,3},{2,0},{3,1},{4,5},{5,4},{6,7},{7,6},{8,10},{9,11},{10,... | collective-permute-start | bytes 1572872 | tf_op jit(solution)/shard_map/ppermute | solution.py:281
  62.1 9.9 %collective-permute-start.9 = (f32[512,256]{1,0:T(8,128)S(1)}, f32[512,256]{1,0:T(8,128)S(1)}, u32[]{:S(2)}, u32[]{:S(2)}) collective-permute-start(f32[512,256]{1,0:T(8,128)S(1)} %get-tuple-element.125), channel_id=1, source_target_pairs={{0,1},{1,0},{2,3},{3,2},{4,6},{5,7},{6,4},{7,5},{8,9},{9,8},{10,11... | collective-permute-start | bytes 1572872 | tf_op jit(solution)/shard_map/ppermute | solution.py:281
  66.1 18.4 %collective-permute-start.12 = (f32[512,256]{1,0:T(8,128)S(1)}, f32[512,256]{1,0:T(8,128)S(1)}, u32[]{:S(2)}, u32[]{:S(2)}) collective-permute-start(f32[512,256]{1,0:T(8,128)S(1)} %get-tuple-element.135), channel_id=1, source_target_pairs={{0,1},{1,0},{2,3},{3,2},{4,6},{5,7},{6,4},{7,5},{8,9},{9,8},{10,11... | collective-permute-start | bytes 1572872 | tf_op jit(solution)/shard_map/ppermute | solution.py:281
  75.6 10.3 %collective-permute-start.13 = (f32[256,256]{1,0:T(8,128)S(1)}, f32[256,256]{1,0:T(8,128)S(1)}, u32[]{:S(2)}, u32[]{:S(2)}) collective-permute-start(f32[256,256]{1,0:T(8,128)S(1)} %get-tuple-element.215), channel_id=1, source_target_pairs={{0,8},{8,0},{16,24},{24,16},{1,9},{9,1},{17,25},{25,17},{2,10},{10... | collective-permute-start | bytes 786440 | tf_op jit(solution)/shard_map/ppermute | solution.py:327
  78.9 14.3 %collective-permute-start.17 = (f32[512,256]{1,0:T(8,128)S(1)}, f32[512,256]{1,0:T(8,128)S(1)}, u32[]{:S(2)}, u32[]{:S(2)}) collective-permute-start(f32[512,256]{1,0:T(8,128)S(1)} %get-tuple-element.145), channel_id=1, source_target_pairs={{0,1},{1,0},{2,3},{3,2},{4,6},{5,7},{6,4},{7,5},{8,9},{9,8},{10,11... | collective-permute-start | bytes 1572872 | tf_op jit(solution)/shard_map/ppermute | solution.py:281
  80.4 9.6 %collective-permute-start.14 = (f32[512,256]{1,0:T(8,128)S(1)}, f32[512,256]{1,0:T(8,128)S(1)}, u32[]{:S(2)}, u32[]{:S(2)}) collective-permute-start(f32[512,256]{1,0:T(8,128)S(1)} %get-tuple-element.138), channel_id=1, source_target_pairs={{0,2},{1,3},{2,0},{3,1},{4,5},{5,4},{6,7},{7,6},{8,10},{9,11},{10,... | collective-permute-start | bytes 1572872 | tf_op jit(solution)/shard_map/ppermute | solution.py:281
  84.5 6.9 %collective-permute-start.15 = (f32[512,768]{1,0:T(8,128)S(1)}, f32[512,768]{1,0:T(8,128)S(1)}, u32[]{:S(2)}, u32[]{:S(2)}) collective-permute-start(f32[512,768]{1,0:T(8,128)S(1)} %get-tuple-element.155), channel_id=1, source_target_pairs={{0,4},{4,0},{1,5},{5,1},{2,6},{6,2},{3,7},{7,3},{8,12},{12,8},{9,1... | collective-permute-start | bytes 4718600 | tf_op jit(solution)/shard_map/ppermute | solution.py:450
  85.3 12.8 %collective-permute-start.20 = (f32[512,256]{1,0:T(8,128)S(1)}, f32[512,256]{1,0:T(8,128)S(1)}, u32[]{:S(2)}, u32[]{:S(2)}) collective-permute-start(f32[512,256]{1,0:T(8,128)S(1)} %get-tuple-element.158), channel_id=1, source_target_pairs={{0,2},{1,3},{2,0},{3,1},{4,5},{5,4},{6,7},{7,6},{8,10},{9,11},{10,... | collective-permute-start | bytes 1572872 | tf_op jit(solution)/shard_map/ppermute | solution.py:281
  85.9 12.4 %collective-permute-start.16 = (f32[128,256]{1,0:T(8,128)S(1)}, f32[128,256]{1,0:T(8,128)S(1)}, u32[]{:S(2)}, u32[]{:S(2)}) collective-permute-start(f32[128,256]{1,0:T(8,128)S(1)} %slice_add_fusion.9), channel_id=1, source_target_pairs={{0,16},{8,24},{16,0},{24,8},{1,17},{9,25},{17,1},{25,9},{2,18},{10... | collective-permute-start | bytes 393224 | tf_op jit(solution)/shard_map/ppermute | solution.py:327
  90.1 8.0 %collective-permute-start.18 = (f32[256,256]{1,0:T(8,128)S(1)}, f32[256,256]{1,0:T(8,128)S(1)}, u32[]{:S(2)}, u32[]{:S(2)}) collective-permute-start(f32[256,256]{1,0:T(8,128)S(1)} %get-tuple-element.212), channel_id=1, source_target_pairs={{0,8},{8,0},{16,24},{24,16},{1,9},{9,1},{17,25},{25,17},{2,10},{10... | collective-permute-start | bytes 786440 | tf_op jit(solution)/shard_map/ppermute | solution.py:327
  93.9 15.1 %collective-permute-start.23 = (f32[512,256]{1,0:T(8,128)S(1)}, f32[512,256]{1,0:T(8,128)S(1)}, u32[]{:S(2)}, u32[]{:S(2)}) collective-permute-start(f32[512,256]{1,0:T(8,128)S(1)} %get-tuple-element.169), channel_id=1, source_target_pairs={{0,2},{1,3},{2,0},{3,1},{4,5},{5,4},{6,7},{7,6},{8,10},{9,11},{10,... | collective-permute-start | bytes 1572872 | tf_op jit(solution)/shard_map/ppermute | solution.py:281
  98.2 10.7 %collective-permute-start.21 = (f32[256,256]{1,0:T(8,128)S(1)}, f32[256,256]{1,0:T(8,128)S(1)}, u32[]{:S(2)}, u32[]{:S(2)}) collective-permute-start(f32[256,256]{1,0:T(8,128)S(1)} %get-tuple-element.209), channel_id=1, source_target_pairs={{0,8},{8,0},{16,24},{24,16},{1,9},{9,1},{17,25},{25,17},{2,10},{10... | collective-permute-start | bytes 786440 | tf_op jit(solution)/shard_map/ppermute | solution.py:327
  98.4 10.8 %collective-permute-start.19 = (f32[128,256]{1,0:T(8,128)S(1)}, f32[128,256]{1,0:T(8,128)S(1)}, u32[]{:S(2)}, u32[]{:S(2)}) collective-permute-start(f32[128,256]{1,0:T(8,128)S(1)} %slice_add_fusion.8), channel_id=1, source_target_pairs={{0,16},{8,24},{16,0},{24,8},{1,17},{9,25},{17,1},{25,9},{2,18},{10... | collective-permute-start | bytes 393224 | tf_op jit(solution)/shard_map/ppermute | solution.py:327
  101.1 14.9 %collective-permute-start.24 = (f32[256,256]{1,0:T(8,128)S(1)}, f32[256,256]{1,0:T(8,128)S(1)}, u32[]{:S(2)}, u32[]{:S(2)}) collective-permute-start(f32[256,256]{1,0:T(8,128)S(1)} %get-tuple-element.206), channel_id=1, source_target_pairs={{0,8},{8,0},{16,24},{24,16},{1,9},{9,1},{17,25},{25,17},{2,10},{10... | collective-permute-start | bytes 786440 | tf_op jit(solution)/shard_map/ppermute | solution.py:327
  109.1 14.5 %collective-permute-start.25 = (f32[256,256]{1,0:T(8,128)S(1)}, f32[256,256]{1,0:T(8,128)S(1)}, u32[]{:S(2)}, u32[]{:S(2)}) collective-permute-start(f32[256,256]{1,0:T(8,128)S(1)} %get-tuple-element.203), channel_id=1, source_target_pairs={{0,8},{8,0},{16,24},{24,16},{1,9},{9,1},{17,25},{25,17},{2,10},{10... | collective-permute-start | bytes 786440 | tf_op jit(solution)/shard_map/ppermute | solution.py:327
  109.2 21.7 %collective-permute-start.22 = (f32[128,256]{1,0:T(8,128)S(1)}, f32[128,256]{1,0:T(8,128)S(1)}, u32[]{:S(2)}, u32[]{:S(2)}) collective-permute-start(f32[128,256]{1,0:T(8,128)S(1)} %slice_add_fusion.7), channel_id=1, source_target_pairs={{0,16},{8,24},{16,0},{24,8},{1,17},{9,25},{17,1},{25,9},{2,18},{10... | collective-permute-start | bytes 393224 | tf_op jit(solution)/shard_map/ppermute | solution.py:327
  116.0 27.5 %copy-start.1 = (f32[128,256]{1,0:T(8,128)S(1)}, f32[128,256]{1,0:T(8,128)}, u32[]{:S(2)}) copy-start(f32[128,256]{1,0:T(8,128)} %copy-done) | copy-start | bytes 393220
  116.0 11.6 %collective-permute-start.28 = (f32[128,256]{1,0:T(8,128)S(1)}, f32[128,256]{1,0:T(8,128)S(1)}, u32[]{:S(2)}, u32[]{:S(2)}) collective-permute-start(f32[128,256]{1,0:T(8,128)S(1)} %get-tuple-element.218), channel_id=1, source_target_pairs={{0,16},{8,24},{16,0},{24,8},{1,17},{9,25},{17,1},{25,9},{2,18},{10... | collective-permute-start | bytes 393224 | tf_op jit(solution)/shard_map/ppermute | solution.py:327
  127.7 5.5 %collective-permute-start.29 = (f32[64,256]{1,0:T(8,128)S(1)}, f32[64,256]{1,0:T(8,128)S(1)}, u32[]{:S(2)}, u32[]{:S(2)}) collective-permute-start(f32[64,256]{1,0:T(8,128)S(1)} %get-tuple-element.222), channel_id=1, source_target_pairs={{0,1},{1,0},{2,3},{3,2},{4,5},{5,4},{6,7},{7,6},{8,9},{9,8},{10,11... | collective-permute-start | bytes 196616 | tf_op jit(solution)/shard_map/ppermute | solution.py:327
  131.0 5.9 %collective-permute-start.26 = (f32[128,256]{1,0:T(8,128)S(1)}, f32[128,256]{1,0:T(8,128)S(1)}, u32[]{:S(2)}, u32[]{:S(2)}) collective-permute-start(f32[128,256]{1,0:T(8,128)S(1)} %slice_add_fusion.5), channel_id=1, source_target_pairs={{0,16},{8,24},{16,0},{24,8},{1,17},{9,25},{17,1},{25,9},{2,18},{10... | collective-permute-start | bytes 393224 | tf_op jit(solution)/shard_map/ppermute | solution.py:327
  133.2 4.0 %collective-permute-start.30 = (f32[32,256]{1,0:T(8,128)S(1)}, f32[32,256]{1,0:T(8,128)S(1)}, u32[]{:S(2)}, u32[]{:S(2)}) collective-permute-start(f32[32,256]{1,0:T(8,128)S(1)} %slice_add_fusion.11), channel_id=1, source_target_pairs={{0,2},{1,3},{2,0},{3,1},{4,6},{5,7},{6,4},{7,5},{8,10},{9,11},{10,... | collective-permute-start | bytes 98312 | tf_op jit(solution)/shard_map/ppermute | solution.py:327
  137.0 6.4 %collective-permute-start.27 = (f32[64,1024]{1,0:T(8,128)S(1)}, f32[64,1024]{1,0:T(8,128)S(1)}, u32[]{:S(2)}, u32[]{:S(2)}) collective-permute-start(f32[64,1024]{1,0:T(8,128)S(1)} %pad_maximum_fusion), channel_id=1, source_target_pairs={{0,1},{1,0},{2,3},{3,2},{4,6},{5,7},{6,4},{7,5},{8,9},{9,8},{10,11... | collective-permute-start | bytes 786440 | tf_op jit(solution)/shard_map/ppermute | solution.py:281
  (24 other events, 221.2 us)

commit v4 on v3

--- a/solution.py
+++ b/solution.py
@@ -11,6 +11,8 @@
 SHARES = (1, 1, 1, 1)
 LIMIT = 24 * 1024 * 1024
 LARGE = 60 * 1024 * 1024
+HEAVY = 16_000_000_000
+LIGHT = 16_000_000_000
 SMALL = 16 * 1024 * 1024
 f32 = jnp.float32
 bf16 = jnp.bfloat16
@@ -86,13 +88,15 @@
     near[2 * state:, :] = jnp.broadcast_to(factor, (8, factor.shape[1]))
 
 
-def order_kernel(firsts, counts, size, ids, off, decays, *refs):
+def order_kernel(heads, size, ids, off, decays, *refs):
     sources, refs = refs[:5], refs[5:]
     outs = len(refs) // 2 - 3
     targets, refs = refs[:outs], refs[outs:]
     (tokens_v, cot_v, state_v, inner_v, out_v), refs = refs[:5], refs[5:]
     held, sems = refs[:outs], refs[outs]
     ordered, ordered_grad, early, sc, sb, cum = held[:6]
+    cut = pl.ds(0, heads * size)
+    sources = [*sources[:3], sources[3].at[:, cut], sources[4].at[:, cut]]
     loads = [pltpu.make_async_copy(source, target, sems.at[i])
              for i, (source, target) in enumerate(zip(sources, (tokens_v, cot_v, state_v, inner_v, out_v)))]
     stores = [pltpu.make_async_copy(source, target, sems.at[5 + i]) for i, (source, target) in enumerate(zip(held, targets))]
@@ -130,15 +134,39 @@
     stores[3].start()
     stores[4].start()
     loads[3].wait()
+    x = dot(ordered[...], inner_v[...]).astype(bf16).astype(f32)
     loads[4].wait()
+    dy = dot(ordered_grad[...], out_v[...]).astype(bf16).astype(f32)
+    end_states(spread(cum[...], 0, heads, size), x, dy, sc, sb, *held[6:9])
+    for store in stores[6:]:
+        store.start()
+    for store in stores:
+        store.wait()
+
+
+def rest_kernel(firsts, counts, size, sc, sb, cum, *refs):
+    sources, refs = refs[:4], refs[4:]
+    outs = len(refs) // 2 - 2
+    targets, refs = refs[:outs], refs[outs:]
+    (ordered, ordered_grad, inner_v, out_v), refs = refs[:4], refs[4:]
+    held, sems = refs[:outs], refs[outs]
+    base = firsts[0] * size
+    cut = pl.ds(base, inner_v.shape[1])
+    sources = [sources[0], sources[1], sources[2].at[:, cut], sources[3].at[:, cut]]
+    loads = [pltpu.make_async_copy(source, target, sems.at[i])
+             for i, (source, target) in enumerate(zip(sources, (ordered, ordered_grad, inner_v, out_v)))]
+    stores = [pltpu.make_async_copy(source, target, sems.at[4 + i]) for i, (source, target) in enumerate(zip(held, targets))]
+    for load in loads:
+        load.start()
+    for load in loads:
+        load.wait()
     for r, (first, heads) in enumerate(zip(firsts, counts)):
-        cut = slice(first * size, (first + heads) * size)
-        cum_x = spread(cum[...], first, heads, size)
+        cut = slice(first * size - base, (first + heads) * size - base)
         x = dot(ordered[...], inner_v[:, cut]).astype(bf16).astype(f32)
         dy = dot(ordered_grad[...], out_v[:, cut]).astype(bf16).astype(f32)
-        end_states(cum_x, x, dy, sc, sb, *held[6 + 3 * r:9 + 3 * r])
-        for i in range(6 + 3 * r, 9 + 3 * r):
-            stores[i].start()
+        end_states(spread(cum[...], first, heads, size), x, dy, sc, sb, *held[3 * r:3 * r + 3])
+        for store in stores[3 * r:3 * r + 3]:
+            store.start()
     for store in stores:
         store.wait()
 
@@ -223,7 +251,7 @@
     keep[...] = dot(left[:half, :], right)
 
 
-def back_kernel(rounds, s_order, ids, *refs):
+def back_kernel(rounds, s_orders, ids, *refs):
     grads, sums = refs[:rounds], refs[rounds:2 * rounds]
     w_inner, w_state, ordered, keep, state_keep, send, table = refs[2 * rounds:]
     side, me_state = ids[2], ids[3]
@@ -242,13 +270,15 @@
             value = value + dot(part[...], w_inner[rows, start:start + cols], 1, 1)
             start += cols
         out[:, :half] = value
-    fine = width >> len(s_order)
+    fine = width >> len(s_orders[0])
     step = width // 4
     for quarter in range(4):
         value = dot(ordered[:, quarter * step:(quarter + 1) * step], grad_bc, 0, 0)
         for piece in range(step // fine):
             index = (quarter * step) // fine + piece
-            where = place(index ^ me_state, s_order)
+            index = index ^ me_state
+            owner = side ^ ((index >> s_orders[0][0]) & 1)
+            where = jnp.where(owner == 0, place(index, s_orders[0]), place(index, s_orders[1]))
             table[pl.ds(pl.multiple_of(where * fine, fine), fine), :] = value[piece * fine:(piece + 1) * fine]
     state_keep[...] = table[:half, :]
     send[:, half:] = table[half:, :]
@@ -260,15 +290,16 @@
 
 
 def finish_kernel(rounds, ids, *refs):
-    halves, (swap, d_inner, d_out) = refs[:rounds], refs[rounds:]
-    block = d_inner.shape[0]
+    halves, (state, most, last, d_inner, d_out, d_state) = refs[:rounds], refs[rounds:]
+    block, fine = d_inner.shape[0], d_state.shape[0]
     start = 0
-    for half in halves:
+    for r, half in enumerate(halves):
         cut = slice(start, start + half.shape[1])
-        own, other = half[:block, :], swap[:, cut]
+        own, other = half[:block, :], most[:, cut] if r + 1 < rounds else last[:block, :]
         d_inner[:, cut] = jnp.where(ids[4] == 0, own, other)
         d_out[:, cut] = jnp.where(ids[4] == 0, other, own)
         start += half.shape[1]
+    d_state[...] = state[:fine, :] + last[block:, :]
 
 
 def flips(axis, bit):
@@ -315,26 +346,39 @@
 
 
 class Sum:
-    def __init__(self, line, parts, hops):
-        self.line, self.parts, self.hops = line, parts, list(hops)
+    def __init__(self, line, segments, hops):
+        self.line, self.segments, self.hops = line, segments, list(hops)
 
     def hop(self):
         axis, bit = self.hops.pop(0)
-        rows = self.parts[0].shape[0] // 2
-        tied = self.line.tie(*self.parts)
-        message = total_of(tied, rows, 2 * rows)
+        halves = [parts[0].shape[0] // 2 for parts in self.segments]
+        flat = self.line.tie(*[part for parts in self.segments for part in parts])
+        tied, start = [], 0
+        for parts in self.segments:
+            tied.append(flat[start:start + len(parts)])
+            start += len(parts)
+        message = rows_of([total_of(parts, half, 2 * half) for parts, half in zip(tied, halves)])
         self.line.did(message)
-        self.parts = [p[:rows] for p in tied] + [lax.ppermute(message, axis, flips(axis, bit))]
+        came = lax.ppermute(message, axis, flips(axis, bit))
+        start = 0
+        self.segments = []
+        for parts, half in zip(tied, halves):
+            self.segments.append([p[:half] for p in parts] + [came[start:start + half]])
+            start += half
 
     def result(self):
-        return total_of(self.parts, 0, self.parts[0].shape[0])
+        return [total_of(parts, 0, parts[0].shape[0]) for parts in self.segments]
+
+
+def rows_of(arrays):
+    return arrays[0] if len(arrays) == 1 else jnp.concatenate(arrays, axis=0)
 
 
 def whole(array):
     return pl.BlockSpec(array.shape, lambda *_: (0,) * len(array.shape))
 
 
-def call(kernel, outs, args, name, scratch=(), specs=None, limit=LIMIT, out_specs=None):
+def call(kernel, outs, args, name, scratch=(), specs=None, limit=LIMIT, out_specs=None, cost=LIGHT):
     specs = specs or {}
     out_specs = out_specs or {}
     in_specs = []
@@ -353,7 +397,7 @@
         out_specs=tuple(out_specs.get(i, whole(o)) for i, o in enumerate(outs)),
         scratch_shapes=list(scratch),
         compiler_params=pltpu.CompilerParams(vmem_limit_bytes=limit),
-        cost_estimate=pl.CostEstimate(flops=16_000_000_000, bytes_accessed=1000, transcendentals=0),
+        cost_estimate=pl.CostEstimate(flops=cost, bytes_accessed=1000, transcendentals=0),
         name=name,
     )(*args)
 
@@ -374,11 +418,9 @@
     seq_bits, head_bits, order_bits = log2(n_seq), log2(n_heads), log2(n_order)
     assert seq_bits == 2 and head_bits == 1
     order_hops = [("order", b) for b in range(order_bits)]
-    s_hops = [("heads", 0)] + order_hops + [("seq", 0), ("seq", 1)]
-    shift_state = {"seq": 0, "heads": seq_bits, "order": seq_bits + head_bits}
-    s_order = [shift_state[a] + b for a, b in s_hops]
     pair_bits, sum_bits = (0, 1), (1, 0)
     orders = [[sum_bits[c]] + [seq_bits + b for b in range(order_bits)] + [pair_bits[c]] for c in range(2)]
+    s_orders = [[seq_bits, sum_bits[c]] + [seq_bits + 1 + b for b in range(order_bits)] + [pair_bits[c]] for c in range(2)]
     role = jnp.where(h == 0, s & 1, (s >> 1) & 1)
     ids = jnp.stack([o * n_seq + s, o * rows, h, (o * n_heads + h) * n_seq + s, role, o]).astype(jnp.int32)
     S = jax.ShapeDtypeStruct
@@ -387,21 +429,36 @@
     wide = S((rows, CHUNK + state), bf16)
     far_space = pl.BlockSpec(memory_space=pltpu.HBM)
 
-    outs = [full, full, sent, wide, wide, S((heads, rows), f32)]
-    for count in counts:
-        outs += [S((rows, count * size), bf16)] * 2 + [S((2 * state + 8, count * size), f32)]
+    def ends(count):
+        return [S((rows, count * size), bf16)] * 2 + [S((2 * state + 8, count * size), f32)]
+
+    outs = [full, full, sent, wide, wide, S((heads, rows), f32)] + ends(counts[0])
     order_args = [ids, node_order, decays.T, tokens, cotangent, w_state, w_inner, w_out]
+    cols = counts[0] * size
     made = call(
-        functools.partial(order_kernel, firsts, counts, size), outs, order_args, "order",
+        functools.partial(order_kernel, counts[0], size), outs, order_args, "order",
         specs={i: far_space for i in range(3, 8)}, out_specs={i: far_space for i in range(len(outs))},
-        scratch=[pltpu.VMEM(a.shape, a.dtype) for a in order_args[3:] + outs] + [pltpu.SemaphoreType.DMA((5 + len(outs),))],
-        limit=LARGE)
+        scratch=[pltpu.VMEM(a.shape, a.dtype) for a in order_args[3:6]] + [pltpu.VMEM((width, cols), bf16)] * 2
+        + [pltpu.VMEM(a.shape, a.dtype) for a in outs] + [pltpu.SemaphoreType.DMA((5 + len(outs),))],
+        limit=LARGE, cost=HEAVY)
     ordered, ordered_grad, early, sc, sb, cum = made[:6]
+    near_first = lax.ppermute(made[8], "order", flips("order", 0)) if n_order == 4 else chain(made[8])
+    near_tokens = cross(early, pair_bits)
+    outs = [out for count in counts[1:] for out in ends(count)]
+    made += call(
+        functools.partial(rest_kernel, firsts[1:], counts[1:], size), outs,
+        [sc, sb, cum, ordered, ordered_grad, w_inner, w_out], "rest",
+        specs={i: far_space for i in range(3, 7)}, out_specs={i: far_space for i in range(len(outs))},
+        scratch=[pltpu.VMEM((rows, width), bf16)] * 2 + [pltpu.VMEM((width, inner - cols), bf16)] * 2
+        + [pltpu.VMEM(a.shape, a.dtype) for a in outs] + [pltpu.SemaphoreType.DMA((4 + len(outs),))],
+        limit=LARGE, cost=HEAVY)
     count_rounds = len(SHARES)
+    block = width // (n_order * n_seq)
+    fine = block // n_heads
     line = Line(ids)
     tree = n_order == 4
-    nears = {0: lax.ppermute(made[8], "order", flips("order", 0)) if tree else chain(made[8])}
-    near_tokens = cross(early, pair_bits)
+    nears = {0: near_first}
+    line.did(made[11])
     incoming, owns, swapped, grads, sums, halves = {}, {}, {}, {}, {}, {}
     held = {}
 
@@ -425,7 +482,7 @@
         own, send, grads[r], sums[r] = call(
             functools.partial(outputs_kernel, firsts[r], counts[r], size, 1, not tree),
             [S((rows, cols), bf16), S((rows, cols), f32), S((rows, cols), bf16), S((rows, 2 * state), f32)],
-            [line.tie(ids), *made[6 + 3 * r:8 + 3 * r], sc, sb, cum, *incoming[r]], f"outputs_{r}")
+            [line.tie(ids), *made[6 + 3 * r:8 + 3 * r], sc, sb, cum, *incoming[r]], f"outputs_{r}", cost=HEAVY)
         line.did(send)
         owns[r], swapped[r] = own, cross(send, pair_bits)
 
@@ -438,22 +495,38 @@
         half = S((width // 2, counts[r] * size), f32)
         keep, send = call(grads_kernel, [half] * 2, [held["left"], line.tie(owns[r]), swapped[r]], f"grads_{r}")
         line.did(send)
-        halves[r] = Sum(line, [keep, cross(send, sum_bits)], order_hops)
+        segments = [[keep]]
+        if r == count_rounds - 1:
+            whole_state = held["state"]
+            middle = whole_state[0].shape[0] // 2
+            send = rows_of([send, total_of(whole_state, middle, 2 * middle)])
+            segments.append([part[:middle] for part in whole_state])
+        came, start = cross(send, sum_bits), 0
+        for parts in segments:
+            parts.append(came[start:start + parts[0].shape[0]])
+            start += parts[0].shape[0]
+        halves[r] = Sum(line, segments, order_hops)
 
     def back():
         keep, state_keep, send = call(
-            functools.partial(back_kernel, count_rounds, s_order),
+            functools.partial(back_kernel, count_rounds, s_orders),
             [S((rows, width // 2), f32), S((width // 2, 2 * state), f32), S((rows, width // 2 + 2 * state), f32)],
             [line.tie(ids)] + [grads[r] for r in range(count_rounds)] + [sums[r] for r in range(count_rounds)]
             + [w_inner, w_state, ordered], "back", scratch=[pltpu.VMEM((width, 2 * state), f32)])
         line.did(send)
         held["keep"], held["came"] = keep, lax.ppermute(send, "heads", flips("heads", 0))
-        held["state"] = Sum(line, [state_keep, held["came"][:, width // 2:]], s_hops[1:])
+        held["state"] = [state_keep, held["came"][:, width // 2:]]
 
     def place_rows():
         held["tokens"], = call(place_kernel, [S((rows, width // 2), bf16)],
                                [line.tie(ids), node_order, held["keep"], held["came"]], "place")
         line.did(held["tokens"])
+
+    def swap_most():
+        held["most"] = [halves[r].result()[0] for r in range(count_rounds - 1)]
+        message = jnp.concatenate([line.tie(h)[block:] for h in held["most"]], axis=1)
+        line.did(message)
+        held["swap"] = cross(message, pair_bits)
 
     steps = [(8.0, turn), (8.5 * count_rounds - 8, back), (8.5 * count_rounds + 1, place_rows)]
     for r in range(count_rounds):
@@ -461,19 +534,16 @@
         steps += [(start - 9.5, functools.partial(join, r)), (start, functools.partial(outputs, r)),
                   (start + 11, functools.partial(gradients, r))]
         steps += [(start + 23 + 8 * k, lambda r=r: halves[r].hop()) for k in range(order_bits)]
-    steps += [(8.5 * count_rounds + 10 + 8 * k, lambda: held["state"].hop()) for k in range(order_bits)]
+    steps.append((8.5 * count_rounds + 15 + 8 * order_bits - 7.5, swap_most))
     for _, step in sorted(steps, key=lambda entry: entry[0]):
         step()
-    halves = [halves[r].result() for r in range(count_rounds)]
+    last, state_sum = halves[count_rounds - 1].result()
+    swap = cross(rows_of([last[block:], state_sum[fine:]]), pair_bits)
+    final = S((block, inner), f32)
+    d_w_inner, d_w_out, d_w_state = call(
+        functools.partial(finish_kernel, count_rounds), [final, final, S((fine, 2 * state), f32)],
+        [ids] + held["most"] + [last, state_sum, held["swap"], swap], "finish", limit=SMALL)
     d_tokens = held["tokens"]
-    while held["state"].hops:
-        held["state"].hop()
-    d_w_state = held["state"].result()
-    block = width // (n_order * n_seq)
-    swap = cross(jnp.concatenate([h[block:] for h in halves], axis=1), pair_bits)
-    final = S((block, inner), f32)
-    d_w_inner, d_w_out = call(functools.partial(finish_kernel, len(halves)), [final, final],
-                              [ids] + halves + [swap], "finish", limit=SMALL)
     return d_tokens[None], d_w_inner, d_w_state, d_w_out
 
 

time: 145 us -> 136 us (0.938)
  starting transfers between devices: 48.8 us -> 38.3 us
  Pallas kernels: 31.9 us -> 37 us
  waiting for transfers between devices: 59.8 us -> 56.4 us
    ppermute x12 -> x8, starting transfers between devices: 19.6 us -> 9.56 us  [hop(): came = lax.ppermute(message, axis, flips(axis, bit))]
    ppermute x1, waiting for transfers between devices: 6.67 us -> 0.01 us  [per_device(): lax.ppermute(made[8], 'order', flips('order', 0))]
    pallas_call x17 -> x18, Pallas kernels: 31.9 us -> 37 us  [call(): pl.pallas_call(kernel, out_shape=tuple(outs), grid=(1,), in_specs=in_spec...]
    ppermute x3, waiting for transfers between devices: 5.75 us -> 9.46 us  [join(): nears[r + 1] = lax.ppermute(following, 'order', flips('order', 0))]
    ppermute x10 -> x11, waiting for transfers between devices: 23.6 us -> 20.4 us  [cross(): return lax.ppermute(value, ('heads', 'seq'), pairs)]
    ppermute x3, starting transfers between devices: 5.77 us -> 2.63 us  [join(): nears[r + 1] = lax.ppermute(following, 'order', flips('order', 0))]
    ppermute x10 -> x11, starting transfers between devices: 12.2 us -> 15.2 us  [cross(): return lax.ppermute(value, ('heads', 'seq'), pairs)]
    ppermute x12 -> x8, waiting for transfers between devices: 23.8 us -> 26.5 us  [hop(): came = lax.ppermute(message, axis, flips(axis, bit))]
  transfers between devices with their start and end apart: 31 -> 28, of which waited for: 17 -> 16; matrix products, arithmetic and copies ran while one was open for 1% -> 1% of each run, Pallas kernels for 14% -> 21%
where the time goes in v4:
time: 136 us; the launch traced here: 135 us
  waiting for transfers between devices  56.4 us (41%)
  starting transfers between devices  38.3 us (28%)
  Pallas kernels  37 us (27%)
  local copies, waits for them, and re-layouts  1.79 us (1%)
    pallas_call x18, Pallas kernels, call(): pl.pallas_call(kernel, out_shape=tuple(outs), grid=(1,), in_specs=in_spec...  37 us
    ppermute x8, waiting for transfers between devices, hop(): came = lax.ppermute(message, axis, flips(axis, bit))  26.5 us
    ppermute x11, waiting for transfers between devices, cross(): return lax.ppermute(value, ('heads', 'seq'), pairs)  20.4 us
    ppermute x11, starting transfers between devices, cross(): return lax.ppermute(value, ('heads', 'seq'), pairs)  15.2 us
    ppermute x8, starting transfers between devices, hop(): came = lax.ppermute(message, axis, flips(axis, bit))  9.56 us
    ppermute x3, waiting for transfers between devices, join(): nears[r + 1] = lax.ppermute(following, 'order', flips('order', 0))  9.46 us
    ppermute x4, starting transfers between devices, join(): incoming[r] = (came, lax.ppermute(joined, 'order', flips('order', 1)))  7.72 us
    ppermute x1, starting transfers between devices, per_device(): lax.ppermute(made[8], 'order', flips('order', 0))  3.09 us
  transfers between devices with their start and end apart: 28, of which 16 were waited for; matrix products, arithmetic and copies ran while one was open for 1% of the time, Pallas kernels for 21%

profile of v4, /device:TPU:0, one launch (start us, length us, event | category | flops | bytes accessed | tf_op | source)
XLA Modules:
  0.0 135.4 jit_solution(10496253983862365915)
XLA Ops:
  1.2 7.0 %order.1 = (bf16[512,1024]{1,0:T(8,128)(2,1)}, bf16[512,1024]{1,0:T(8,128)(2,1)}, f32[512,1024]{1,0:T(8,128)}, bf16[512,256]{1,0:T(8,128)(2,1)}, bf16[512,256]{1...) custom-call(s32[6]{0:T(128)} %stack.27.ids, ...), custom_call_target="tpu_custom_call" | custom-call | flops 16000000000 | bytes 1000 | tf_op jit(solution)/shard_map/order/pallas_call | solution.py:392
  8.2 3.1 %collective-permute-start = (f32[264,256]{1,0:T(8,128)}, f32[264,256]{1,0:T(8,128)S(1)}, u32[]{:S(2)}, u32[]{:S(2)}) collective-permute-start(f32[264,256]{1,0:T(8,128)} %get-tuple-element.105.near), channel_id=1, source_target_pairs={{0,8},{8,0},{16,24},{24,16},{1,9},{9,1},{17,25},{25,17},{2,10},{10... | collective-permute-start | bytes 811016 | tf_op jit(solution)/shard_map/ppermute | solution.py:445
  11.3 8.4 %rest.1 = (bf16[512,256]{1,0:T(8,128)(2,1)}, bf16[512,256]{1,0:T(8,128)(2,1)}, f32[264,256]{1,0:T(8,128)}, bf16[512,256]{1,0:T(8,128)(2,1)}, bf16[512,256]{1,0:T...) custom-call(bf16[512,256]{1,0:T(8,128)(2,1)} %get-tuple-element.98.s, ...), custom_call_target="tpu_custom_call" | custom-call | flops 16000000000 | bytes 1000 | tf_op jit(solution)/shard_map/rest/pallas_call | solution.py:392
  21.5 1.6 %collective-permute-start.4 = (f32[512,1024]{1,0:T(8,128)S(1)}, f32[512,1024]{1,0:T(8,128)S(1)}, u32[]{:S(2)}, u32[]{:S(2)}) collective-permute-start(f32[512,1024]{1,0:T(8,128)S(1)} %copy-done.21), channel_id=1, source_target_pairs={{0,1},{1,0},{2,3},{3,2},{4,6},{5,7},{6,4},{7,5},{8,9},{9,8},{10,11... | collective-permute-start | bytes 6291464 | tf_op jit(solution)/shard_map/ppermute | solution.py:312
  23.0 2.6 %collective-permute-start.2 = (f32[128,256]{1,0:T(8,128)S(1)}, f32[128,256]{1,0:T(8,128)S(1)}, u32[]{:S(2)}, u32[]{:S(2)}) collective-permute-start(f32[128,256]{1,0:T(8,128)S(1)} %join_0.1), channel_id=1, source_target_pairs={{0,16},{8,24},{16,0},{24,8},{1,17},{9,25},{17,1},{25,9},{2,18},{10... | collective-permute-start | bytes 393224 | tf_op jit(solution)/shard_map/ppermute | solution.py:471
  25.6 5.8 %collective-permute-done.1.came = f32[264,256]{1,0:T(8,128)S(1)} collective-permute-done((f32[264,256]{1,0:T(8,128)S(1)}, f32[264,256]{1,0:T(8,128)S(1)}, u32[]{:S(2)}, u32[]{:S(2)}) %collective-permute-start.1) | collective-permute-done | bytes 270368 | tf_op jit(solution)/shard_map/ppermute | solution.py:474
  34.4 2.3 %outputs_0.1 = (bf16[512,256]{1,0:T(8,128)(2,1)S(1)}, f32[512,256]{1,0:T(8,128)S(1)}, bf16[512,256]{1,0:T(8,128)(2,1)S(1)}, f32[512,256]{1,0:T(8,128)S(1)}) custom-call(s32[6]{0:T(128)S(1)} %copy-done, bf16[512,256]{1,0:T(8,128)(2,1)S(1)} %copy-done.12, bf16[512,256]{1,0:T(8,128)(2,1)S(1)} %copy-done.13, bf16[512,256]{1,0:T(8,128)(2,1)S(1)} %copy-done.10, ...), custom_call_target="tpu_custom_call" | custom-call | flops 16000000000 | bytes 1000 | tf_op jit(solution)/shard_map/outputs_0/pallas_call | solution.py:392
  36.7 1.7 %collective-permute-start.6 = (f32[512,256]{1,0:T(8,128)S(1)}, f32[512,256]{1,0:T(8,128)S(1)}, u32[]{:S(2)}, u32[]{:S(2)}) collective-permute-start(f32[512,256]{1,0:T(8,128)S(1)} %get-tuple-element.111), channel_id=1, source_target_pairs={{0,1},{1,0},{2,3},{3,2},{4,6},{5,7},{6,4},{7,5},{8,9},{9,8},{10,11... | collective-permute-start | bytes 1572872 | tf_op jit(solution)/shard_map/ppermute | solution.py:312
  38.4 3.6 %collective-permute-done.3.came = f32[264,256]{1,0:T(8,128)S(1)} collective-permute-done((f32[264,256]{1,0:T(8,128)S(1)}, f32[264,256]{1,0:T(8,128)S(1)}, u32[]{:S(2)}, u32[]{:S(2)}) %collective-permute-start.3) | collective-permute-done | bytes 270368 | tf_op jit(solution)/shard_map/ppermute | solution.py:474
  43.8 1.6 %collective-permute-start.7 = (f32[264,256]{1,0:T(8,128)S(1)}, f32[264,256]{1,0:T(8,128)S(1)}, u32[]{:S(2)}, u32[]{:S(2)}) collective-permute-start(f32[264,256]{1,0:T(8,128)S(1)} %copy-done.3), channel_id=1, source_target_pairs={{0,8},{8,0},{16,24},{24,16},{1,9},{9,1},{17,25},{25,17},{2,10},{10... | collective-permute-start | bytes 811016 | tf_op jit(solution)/shard_map/ppermute | solution.py:474
  45.4 2.2 %collective-permute-done.4.near = f32[512,1024]{1,0:T(8,128)S(1)} collective-permute-done((f32[512,1024]{1,0:T(8,128)S(1)}, f32[512,1024]{1,0:T(8,128)S(1)}, u32[]{:S(2)}, u32[]{:S(2)}) %collective-permute-start.4) | collective-permute-done | bytes 2097184 | tf_op jit(solution)/shard_map/ppermute | solution.py:312
  48.8 2.3 %outputs_1.1 = (bf16[512,256]{1,0:T(8,128)(2,1)S(1)}, f32[512,256]{1,0:T(8,128)S(1)}, bf16[512,256]{1,0:T(8,128)(2,1)S(1)}, f32[512,256]{1,0:T(8,128)S(1)}) custom-call(s32[6]{0:T(128)S(1)} %copy-done, bf16[512,256]{1,0:T(8,128)(2,1)S(1)} %copy-done.18, bf16[512,256]{1,0:T(8,128)(2,1)S(1)} %copy-done.19, bf16[512,256]{1,0:T(8,128)(2,1)S(1)} %copy-done.10, ...), custom_call_target="tpu_custom_call" | custom-call | flops 16000000000 | bytes 1000 | tf_op jit(solution)/shard_map/outputs_1/pallas_call | solution.py:392
  51.1 2.0 %collective-permute-done.6.came = f32[512,256]{1,0:T(8,128)S(1)} collective-permute-done((f32[512,256]{1,0:T(8,128)S(1)}, f32[512,256]{1,0:T(8,128)S(1)}, u32[]{:S(2)}, u32[]{:S(2)}) %collective-permute-start.6) | collective-permute-done | bytes 524320 | tf_op jit(solution)/shard_map/ppermute | solution.py:312
  54.5 2.7 %collective-permute-start.11 = (f32[128,256]{1,0:T(8,128)S(1)}, f32[128,256]{1,0:T(8,128)S(1)}, u32[]{:S(2)}, u32[]{:S(2)}) collective-permute-start(f32[128,256]{1,0:T(8,128)S(1)} %join_3.1), channel_id=1, source_target_pairs={{0,16},{8,24},{16,0},{24,8},{1,17},{9,25},{17,1},{25,9},{2,18},{10... | collective-permute-start | bytes 393224 | tf_op jit(solution)/shard_map/ppermute | solution.py:471
  57.2 1.5 %collective-permute-start.10 = (f32[512,256]{1,0:T(8,128)S(1)}, f32[512,256]{1,0:T(8,128)S(1)}, u32[]{:S(2)}, u32[]{:S(2)}) collective-permute-start(f32[512,256]{1,0:T(8,128)S(1)} %get-tuple-element.123), channel_id=1, source_target_pairs={{0,2},{1,3},{2,0},{3,1},{4,5},{5,4},{6,7},{7,6},{8,10},{9,11},{10,... | collective-permute-start | bytes 1572872 | tf_op jit(solution)/shard_map/ppermute | solution.py:312
  60.2 2.5 %outputs_2.1 = (bf16[512,256]{1,0:T(8,128)(2,1)S(1)}, f32[512,256]{1,0:T(8,128)S(1)}, bf16[512,256]{1,0:T(8,128)(2,1)S(1)}, f32[512,256]{1,0:T(8,128)S(1)}) custom-call(s32[6]{0:T(128)S(1)} %copy-done, bf16[512,256]{1,0:T(8,128)(2,1)S(1)} %copy-done.16, bf16[512,256]{1,0:T(8,128)(2,1)S(1)} %copy-done.17, bf16[512,256]{1,0:T(8,128)(2,1)S(1)} %copy-done.10, ...), custom_call_target="tpu_custom_call" | custom-call | flops 16000000000 | bytes 1000 | tf_op jit(solution)/shard_map/outputs_2/pallas_call | solution.py:392
  63.3 6.1 %collective-permute-done.9.came = f32[512,256]{1,0:T(8,128)S(1)} collective-permute-done((f32[512,256]{1,0:T(8,128)S(1)}, f32[512,256]{1,0:T(8,128)S(1)}, u32[]{:S(2)}, u32[]{:S(2)}) %collective-permute-start.9) | collective-permute-done | bytes 524320 | tf_op jit(solution)/shard_map/ppermute | solution.py:312
  70.1 1.9 %collective-permute-done.10 = f32[512,256]{1,0:T(8,128)S(1)} collective-permute-done((f32[512,256]{1,0:T(8,128)S(1)}, f32[512,256]{1,0:T(8,128)S(1)}, u32[]{:S(2)}, u32[]{:S(2)}) %collective-permute-start.10) | collective-permute-done | bytes 524320 | tf_op jit(solution)/shard_map/ppermute | solution.py:312
  73.5 2.3 %outputs_3.1 = (bf16[512,256]{1,0:T(8,128)(2,1)S(1)}, f32[512,256]{1,0:T(8,128)S(1)}, bf16[512,256]{1,0:T(8,128)(2,1)S(1)}, f32[512,256]{1,0:T(8,128)S(1)}) custom-call(s32[6]{0:T(128)S(1)} %copy-done, bf16[512,256]{1,0:T(8,128)(2,1)S(1)} %copy-done.14, bf16[512,256]{1,0:T(8,128)(2,1)S(1)} %copy-done.15, bf16[512,256]{1,0:T(8,128)(2,1)S(1)} %copy-done.10, ...), custom_call_target="tpu_custom_call" | custom-call | flops 16000000000 | bytes 1000 | tf_op jit(solution)/shard_map/outputs_3/pallas_call | solution.py:392
  75.8 1.6 %collective-permute-start.17 = (f32[512,256]{1,0:T(8,128)S(1)}, f32[512,256]{1,0:T(8,128)S(1)}, u32[]{:S(2)}, u32[]{:S(2)}) collective-permute-start(f32[512,256]{1,0:T(8,128)S(1)} %get-tuple-element.140), channel_id=1, source_target_pairs={{0,1},{1,0},{2,3},{3,2},{4,6},{5,7},{6,4},{7,5},{8,9},{9,8},{10,11... | collective-permute-start | bytes 1572872 | tf_op jit(solution)/shard_map/ppermute | solution.py:312
  77.4 1.5 %collective-permute-start.14 = (f32[512,256]{1,0:T(8,128)S(1)}, f32[512,256]{1,0:T(8,128)S(1)}, u32[]{:S(2)}, u32[]{:S(2)}) collective-permute-start(f32[512,256]{1,0:T(8,128)S(1)} %get-tuple-element.133), channel_id=1, source_target_pairs={{0,2},{1,3},{2,0},{3,1},{4,5},{5,4},{6,7},{7,6},{8,10},{9,11},{10,... | collective-permute-start | bytes 1572872 | tf_op jit(solution)/shard_map/ppermute | solution.py:312
  78.9 2.6 %back.1 = (f32[512,512]{1,0:T(8,128)S(1)}, f32[512,256]{1,0:T(8,128)S(1)}, f32[512,768]{1,0:T(8,128)S(1)}) custom-call(s32[6]{0:T(128)S(1)} %copy-done, bf16[512,256]{1,0:T(8,128)(2,1)S(1)} %get-tuple-element.142.refs_0_, bf16[512,256]{1,0:T(8,128)(2,1)S(1)} %get-tuple-element.143.refs_1_, bf16[512,256]{1,0:T(8,128)(2,1)S(1)} %get-tuple-element.144.refs_2_, ...), custom_call_target="tpu_custom_call" | custom-call | flops 16000000000 | bytes 1000 | tf_op jit(solution)/shard_map/back/pallas_call | solution.py:392
  82.9 4.6 %collective-permute-done.14 = f32[512,256]{1,0:T(8,128)S(1)} collective-permute-done((f32[512,256]{1,0:T(8,128)S(1)}, f32[512,256]{1,0:T(8,128)S(1)}, u32[]{:S(2)}, u32[]{:S(2)}) %collective-permute-start.14) | collective-permute-done | bytes 524320 | tf_op jit(solution)/shard_map/ppermute | solution.py:312
  88.6 1.8 %place.1 = bf16[512,512]{1,0:T(8,128)(2,1)} custom-call(s32[6]{0:T(128)S(1)} %copy-done, s32[1,512]{1,0:T(1,128)S(1)} %copy-done.7, f32[512,512]{1,0:T(8,128)S(1)} %get-tuple-element.161.keep, f32[512,768]{1,0:T(8,128)S(1)} %collective-permute-done.15.came), custom_call_target="tpu_custom_call" | custom-call | flops 16000000000 | bytes 1000 | tf_op jit(solution)/shard_map/place/pallas_call | solution.py:392
  91.4 2.7 %collective-permute-done.18 = f32[256,256]{1,0:T(8,128)S(1)} collective-permute-done((f32[256,256]{1,0:T(8,128)S(1)}, f32[256,256]{1,0:T(8,128)S(1)}, u32[]{:S(2)}, u32[]{:S(2)}) %collective-permute-start.18) | collective-permute-done | bytes 262176 | tf_op jit(solution)/shard_map/ppermute | solution.py:362
  97.3 2.5 %collective-permute-start.19 = (f32[128,256]{1,0:T(8,128)S(1)}, f32[128,256]{1,0:T(8,128)S(1)}, u32[]{:S(2)}, u32[]{:S(2)}) collective-permute-start(f32[128,256]{1,0:T(8,128)S(1)} %slice_add_fusion.9), channel_id=1, source_target_pairs={{0,16},{8,24},{16,0},{24,8},{1,17},{9,25},{17,1},{25,9},{2,18},{10... | collective-permute-start | bytes 393224 | tf_op jit(solution)/shard_map/ppermute | solution.py:362
  99.8 5.9 %collective-permute-done.21 = f32[256,256]{1,0:T(8,128)S(1)} collective-permute-done((f32[256,256]{1,0:T(8,128)S(1)}, f32[256,256]{1,0:T(8,128)S(1)}, u32[]{:S(2)}, u32[]{:S(2)}) %collective-permute-start.21) | collective-permute-done | bytes 262176 | tf_op jit(solution)/shard_map/ppermute | solution.py:362
  106.5 1.8 %collective-permute-start.24 = (f32[384,256]{1,0:T(8,128)S(1)}, f32[384,256]{1,0:T(8,128)S(1)}, u32[]{:S(2)}, u32[]{:S(2)}) collective-permute-start(f32[384,256]{1,0:T(8,128)S(1)} %pad_maximum_fusion.1), channel_id=1, source_target_pairs={{0,8},{8,0},{16,24},{24,16},{1,9},{9,1},{17,25},{25,17},{2,10},{10... | collective-permute-start | bytes 1179656 | tf_op jit(solution)/shard_map/ppermute | solution.py:362
  111.1 8.7 %collective-permute-done.24 = f32[384,256]{1,0:T(8,128)S(1)} collective-permute-done((f32[384,256]{1,0:T(8,128)S(1)}, f32[384,256]{1,0:T(8,128)S(1)}, u32[]{:S(2)}, u32[]{:S(2)}) %collective-permute-start.24) | collective-permute-done | bytes 393248 | tf_op jit(solution)/shard_map/ppermute | solution.py:362
  121.4 7.8 %collective-permute-done.25 = f32[192,256]{1,0:T(8,128)S(1)} collective-permute-done((f32[192,256]{1,0:T(8,128)S(1)}, f32[192,256]{1,0:T(8,128)S(1)}, u32[]{:S(2)}, u32[]{:S(2)}) %collective-permute-start.25) | collective-permute-done | bytes 196640 | tf_op jit(solution)/shard_map/ppermute | solution.py:362
  129.3 1.9 %collective-permute-start.27 = (f32[96,256]{1,0:T(8,128)S(1)}, f32[96,256]{1,0:T(8,128)S(1)}, u32[]{:S(2)}, u32[]{:S(2)}) collective-permute-start(f32[96,256]{1,0:T(8,128)S(1)} %pad_maximum_fusion.4), channel_id=1, source_target_pairs={{0,1},{1,0},{2,3},{3,2},{4,6},{5,7},{6,4},{7,5},{8,9},{9,8},{10,11... | collective-permute-start | bytes 294920 | tf_op jit(solution)/shard_map/ppermute | solution.py:312
  131.2 2.8 %collective-permute-done.27.refs_6_ = f32[96,256]{1,0:T(8,128)S(1)} collective-permute-done((f32[96,256]{1,0:T(8,128)S(1)}, f32[96,256]{1,0:T(8,128)S(1)}, u32[]{:S(2)}, u32[]{:S(2)}) %collective-permute-start.27) | collective-permute-done | bytes 98336 | tf_op jit(solution)/shard_map/ppermute | solution.py:312
  (117 shorter events, 27.0 us)
Async XLA Ops:
  8.2 11.6 %collective-permute-start = (f32[264,256]{1,0:T(8,128)}, f32[264,256]{1,0:T(8,128)S(1)}, u32[]{:S(2)}, u32[]{:S(2)}) collective-permute-start(f32[264,256]{1,0:T(8,128)} %get-tuple-element.105.near), channel_id=1, source_target_pairs={{0,8},{8,0},{16,24},{24,16},{1,9},{9,1},{17,25},{25,17},{2,10},{10... | collective-permute-start | bytes 811016 | tf_op jit(solution)/shard_map/ppermute | solution.py:445
  20.7 10.7 %collective-permute-start.1 = (f32[264,256]{1,0:T(8,128)S(1)}, f32[264,256]{1,0:T(8,128)S(1)}, u32[]{:S(2)}, u32[]{:S(2)}) collective-permute-start(f32[264,256]{1,0:T(8,128)S(1)} %copy-done.5), channel_id=1, source_target_pairs={{0,8},{8,0},{16,24},{24,16},{1,9},{9,1},{17,25},{25,17},{2,10},{10... | collective-permute-start | bytes 811016 | tf_op jit(solution)/shard_map/ppermute | solution.py:474
  21.4 12.9 %copy-start.11 = (bf16[512,256]{1,0:T(8,128)(2,1)S(1)}, bf16[512,256]{1,0:T(8,128)(2,1)}, u32[]{:S(2)}) copy-start(bf16[512,256]{1,0:T(8,128)(2,1)} %get-tuple-element.99.sb) | copy-start | bytes 786436
  21.4 12.9 %copy-start.12 = (bf16[512,256]{1,0:T(8,128)(2,1)S(1)}, bf16[512,256]{1,0:T(8,128)(2,1)}, u32[]{:S(2)}) copy-start(bf16[512,256]{1,0:T(8,128)(2,1)} %get-tuple-element.109.xs) | copy-start | bytes 786436
  21.4 12.9 %copy-start.13 = (bf16[512,256]{1,0:T(8,128)(2,1)S(1)}, bf16[512,256]{1,0:T(8,128)(2,1)}, u32[]{:S(2)}) copy-start(bf16[512,256]{1,0:T(8,128)(2,1)} %get-tuple-element.110.ys) | copy-start | bytes 786436
  21.4 12.9 %copy-start.20 = (f32[16,512]{1,0:T(8,128)S(1)}, f32[16,512]{1,0:T(8,128)}, u32[]{:S(2)}) copy-start(f32[16,512]{1,0:T(8,128)} %get-tuple-element.100.cum) | copy-start | bytes 98308
  21.5 26.1 %collective-permute-start.4 = (f32[512,1024]{1,0:T(8,128)S(1)}, f32[512,1024]{1,0:T(8,128)S(1)}, u32[]{:S(2)}, u32[]{:S(2)}) collective-permute-start(f32[512,1024]{1,0:T(8,128)S(1)} %copy-done.21), channel_id=1, source_target_pairs={{0,1},{1,0},{2,3},{3,2},{4,6},{5,7},{6,4},{7,5},{8,9},{9,8},{10,11... | collective-permute-start | bytes 6291464 | tf_op jit(solution)/shard_map/ppermute | solution.py:312
  23.0 11.3 %collective-permute-start.2 = (f32[128,256]{1,0:T(8,128)S(1)}, f32[128,256]{1,0:T(8,128)S(1)}, u32[]{:S(2)}, u32[]{:S(2)}) collective-permute-start(f32[128,256]{1,0:T(8,128)S(1)} %join_0.1), channel_id=1, source_target_pairs={{0,16},{8,24},{16,0},{24,8},{1,17},{9,25},{17,1},{25,9},{2,18},{10... | collective-permute-start | bytes 393224 | tf_op jit(solution)/shard_map/ppermute | solution.py:471
  32.0 16.8 %collective-permute-start.5 = (f32[128,256]{1,0:T(8,128)S(1)}, f32[128,256]{1,0:T(8,128)S(1)}, u32[]{:S(2)}, u32[]{:S(2)}) collective-permute-start(f32[128,256]{1,0:T(8,128)S(1)} %join_1.1), channel_id=1, source_target_pairs={{0,16},{8,24},{16,0},{24,8},{1,17},{9,25},{17,1},{25,9},{2,18},{10... | collective-permute-start | bytes 393224 | tf_op jit(solution)/shard_map/ppermute | solution.py:471
  33.3 8.7 %collective-permute-start.3 = (f32[264,256]{1,0:T(8,128)S(1)}, f32[264,256]{1,0:T(8,128)S(1)}, u32[]{:S(2)}, u32[]{:S(2)}) collective-permute-start(f32[264,256]{1,0:T(8,128)S(1)} %copy-done.4), channel_id=1, source_target_pairs={{0,8},{8,0},{16,24},{24,16},{1,9},{9,1},{17,25},{25,17},{2,10},{10... | collective-permute-start | bytes 811016 | tf_op jit(solution)/shard_map/ppermute | solution.py:474
  36.7 16.5 %collective-permute-start.6 = (f32[512,256]{1,0:T(8,128)S(1)}, f32[512,256]{1,0:T(8,128)S(1)}, u32[]{:S(2)}, u32[]{:S(2)}) collective-permute-start(f32[512,256]{1,0:T(8,128)S(1)} %get-tuple-element.111), channel_id=1, source_target_pairs={{0,1},{1,0},{2,3},{3,2},{4,6},{5,7},{6,4},{7,5},{8,9},{9,8},{10,11... | collective-permute-start | bytes 1572872 | tf_op jit(solution)/shard_map/ppermute | solution.py:312
  42.6 17.6 %collective-permute-start.8 = (f32[128,256]{1,0:T(8,128)S(1)}, f32[128,256]{1,0:T(8,128)S(1)}, u32[]{:S(2)}, u32[]{:S(2)}) collective-permute-start(f32[128,256]{1,0:T(8,128)S(1)} %join_2.1), channel_id=1, source_target_pairs={{0,16},{8,24},{16,0},{24,8},{1,17},{9,25},{17,1},{25,9},{2,18},{10... | collective-permute-start | bytes 393224 | tf_op jit(solution)/shard_map/ppermute | solution.py:471
  43.8 10.1 %collective-permute-start.7 = (f32[264,256]{1,0:T(8,128)S(1)}, f32[264,256]{1,0:T(8,128)S(1)}, u32[]{:S(2)}, u32[]{:S(2)}) collective-permute-start(f32[264,256]{1,0:T(8,128)S(1)} %copy-done.3), channel_id=1, source_target_pairs={{0,8},{8,0},{16,24},{24,16},{1,9},{9,1},{17,25},{25,17},{2,10},{10... | collective-permute-start | bytes 811016 | tf_op jit(solution)/shard_map/ppermute | solution.py:474
  54.5 19.0 %collective-permute-start.11 = (f32[128,256]{1,0:T(8,128)S(1)}, f32[128,256]{1,0:T(8,128)S(1)}, u32[]{:S(2)}, u32[]{:S(2)}) collective-permute-start(f32[128,256]{1,0:T(8,128)S(1)} %join_3.1), channel_id=1, source_target_pairs={{0,16},{8,24},{16,0},{24,8},{1,17},{9,25},{17,1},{25,9},{2,18},{10... | collective-permute-start | bytes 393224 | tf_op jit(solution)/shard_map/ppermute | solution.py:471
  57.2 14.8 %collective-permute-start.10 = (f32[512,256]{1,0:T(8,128)S(1)}, f32[512,256]{1,0:T(8,128)S(1)}, u32[]{:S(2)}, u32[]{:S(2)}) collective-permute-start(f32[512,256]{1,0:T(8,128)S(1)} %get-tuple-element.123), channel_id=1, source_target_pairs={{0,2},{1,3},{2,0},{3,1},{4,5},{5,4},{6,7},{7,6},{8,10},{9,11},{10,... | collective-permute-start | bytes 1572872 | tf_op jit(solution)/shard_map/ppermute | solution.py:312
  58.7 10.7 %collective-permute-start.9 = (f32[512,256]{1,0:T(8,128)S(1)}, f32[512,256]{1,0:T(8,128)S(1)}, u32[]{:S(2)}, u32[]{:S(2)}) collective-permute-start(f32[512,256]{1,0:T(8,128)S(1)} %get-tuple-element.120), channel_id=1, source_target_pairs={{0,1},{1,0},{2,3},{3,2},{4,6},{5,7},{6,4},{7,5},{8,9},{9,8},{10,11... | collective-permute-start | bytes 1572872 | tf_op jit(solution)/shard_map/ppermute | solution.py:312
  62.7 18.9 %collective-permute-start.12 = (f32[512,256]{1,0:T(8,128)S(1)}, f32[512,256]{1,0:T(8,128)S(1)}, u32[]{:S(2)}, u32[]{:S(2)}) collective-permute-start(f32[512,256]{1,0:T(8,128)S(1)} %get-tuple-element.130), channel_id=1, source_target_pairs={{0,1},{1,0},{2,3},{3,2},{4,6},{5,7},{6,4},{7,5},{8,9},{9,8},{10,11... | collective-permute-start | bytes 1572872 | tf_op jit(solution)/shard_map/ppermute | solution.py:312
  72.1 10.8 %collective-permute-start.13 = (f32[256,256]{1,0:T(8,128)S(1)}, f32[256,256]{1,0:T(8,128)S(1)}, u32[]{:S(2)}, u32[]{:S(2)}) collective-permute-start(f32[256,256]{1,0:T(8,128)S(1)} %get-tuple-element.205), channel_id=1, source_target_pairs={{0,8},{8,0},{16,24},{24,16},{1,9},{9,1},{17,25},{25,17},{2,10},{10... | collective-permute-start | bytes 786440 | tf_op jit(solution)/shard_map/ppermute | solution.py:362
  75.8 14.9 %collective-permute-start.17 = (f32[512,256]{1,0:T(8,128)S(1)}, f32[512,256]{1,0:T(8,128)S(1)}, u32[]{:S(2)}, u32[]{:S(2)}) collective-permute-start(f32[512,256]{1,0:T(8,128)S(1)} %get-tuple-element.140), channel_id=1, source_target_pairs={{0,1},{1,0},{2,3},{3,2},{4,6},{5,7},{6,4},{7,5},{8,9},{9,8},{10,11... | collective-permute-start | bytes 1572872 | tf_op jit(solution)/shard_map/ppermute | solution.py:312
  77.4 10.1 %collective-permute-start.14 = (f32[512,256]{1,0:T(8,128)S(1)}, f32[512,256]{1,0:T(8,128)S(1)}, u32[]{:S(2)}, u32[]{:S(2)}) collective-permute-start(f32[512,256]{1,0:T(8,128)S(1)} %get-tuple-element.133), channel_id=1, source_target_pairs={{0,2},{1,3},{2,0},{3,1},{4,5},{5,4},{6,7},{7,6},{8,10},{9,11},{10,... | collective-permute-start | bytes 1572872 | tf_op jit(solution)/shard_map/ppermute | solution.py:312
  81.5 7.2 %collective-permute-start.15 = (f32[512,768]{1,0:T(8,128)S(1)}, f32[512,768]{1,0:T(8,128)S(1)}, u32[]{:S(2)}, u32[]{:S(2)}) collective-permute-start(f32[512,768]{1,0:T(8,128)S(1)} %get-tuple-element.150), channel_id=1, source_target_pairs={{0,4},{4,0},{1,5},{5,1},{2,6},{6,2},{3,7},{7,3},{8,12},{12,8},{9,1... | collective-permute-start | bytes 4718600 | tf_op jit(solution)/shard_map/ppermute | solution.py:517
  82.3 13.5 %collective-permute-start.20 = (f32[512,256]{1,0:T(8,128)S(1)}, f32[512,256]{1,0:T(8,128)S(1)}, u32[]{:S(2)}, u32[]{:S(2)}) collective-permute-start(f32[512,256]{1,0:T(8,128)S(1)} %get-tuple-element.153), channel_id=1, source_target_pairs={{0,2},{1,3},{2,0},{3,1},{4,5},{5,4},{6,7},{7,6},{8,10},{9,11},{10,... | collective-permute-start | bytes 1572872 | tf_op jit(solution)/shard_map/ppermute | solution.py:312
  87.5 6.6 %collective-permute-start.18 = (f32[256,256]{1,0:T(8,128)S(1)}, f32[256,256]{1,0:T(8,128)S(1)}, u32[]{:S(2)}, u32[]{:S(2)}) collective-permute-start(f32[256,256]{1,0:T(8,128)S(1)} %get-tuple-element.202), channel_id=1, source_target_pairs={{0,8},{8,0},{16,24},{24,16},{1,9},{9,1},{17,25},{25,17},{2,10},{10... | collective-permute-start | bytes 786440 | tf_op jit(solution)/shard_map/ppermute | solution.py:362
  94.2 12.1 %collective-permute-start.23 = (f32[768,256]{1,0:T(8,128)S(1)}, f32[768,256]{1,0:T(8,128)S(1)}, u32[]{:S(2)}, u32[]{:S(2)}) collective-permute-start(f32[768,256]{1,0:T(8,128)S(1)} %pad_maximum_fusion), channel_id=1, source_target_pairs={{0,2},{1,3},{2,0},{3,1},{4,5},{5,4},{6,7},{7,6},{8,10},{9,11},{10,... | collective-permute-start | bytes 2359304 | tf_op jit(solution)/shard_map/ppermute | solution.py:312
  95.8 9.9 %collective-permute-start.21 = (f32[256,256]{1,0:T(8,128)S(1)}, f32[256,256]{1,0:T(8,128)S(1)}, u32[]{:S(2)}, u32[]{:S(2)}) collective-permute-start(f32[256,256]{1,0:T(8,128)S(1)} %get-tuple-element.199), channel_id=1, source_target_pairs={{0,8},{8,0},{16,24},{24,16},{1,9},{9,1},{17,25},{25,17},{2,10},{10... | collective-permute-start | bytes 786440 | tf_op jit(solution)/shard_map/ppermute | solution.py:362
  96.9 11.5 %collective-permute-start.16 = (f32[128,256]{1,0:T(8,128)S(1)}, f32[128,256]{1,0:T(8,128)S(1)}, u32[]{:S(2)}, u32[]{:S(2)}) collective-permute-start(f32[128,256]{1,0:T(8,128)S(1)} %slice_add_fusion.10), channel_id=1, source_target_pairs={{0,16},{8,24},{16,0},{24,8},{1,17},{9,25},{17,1},{25,9},{2,18},{10... | collective-permute-start | bytes 393224 | tf_op jit(solution)/shard_map/ppermute | solution.py:362
  97.3 12.6 %collective-permute-start.19 = (f32[128,256]{1,0:T(8,128)S(1)}, f32[128,256]{1,0:T(8,128)S(1)}, u32[]{:S(2)}, u32[]{:S(2)}) collective-permute-start(f32[128,256]{1,0:T(8,128)S(1)} %slice_add_fusion.9), channel_id=1, source_target_pairs={{0,16},{8,24},{16,0},{24,8},{1,17},{9,25},{17,1},{25,9},{2,18},{10... | collective-permute-start | bytes 393224 | tf_op jit(solution)/shard_map/ppermute | solution.py:362
  106.5 13.2 %collective-permute-start.24 = (f32[384,256]{1,0:T(8,128)S(1)}, f32[384,256]{1,0:T(8,128)S(1)}, u32[]{:S(2)}, u32[]{:S(2)}) collective-permute-start(f32[384,256]{1,0:T(8,128)S(1)} %pad_maximum_fusion.1), channel_id=1, source_target_pairs={{0,8},{8,0},{16,24},{24,16},{1,9},{9,1},{17,25},{25,17},{2,10},{10... | collective-permute-start | bytes 1179656 | tf_op jit(solution)/shard_map/ppermute | solution.py:362
  109.9 10.1 %collective-permute-start.22 = (f32[128,256]{1,0:T(8,128)S(1)}, f32[128,256]{1,0:T(8,128)S(1)}, u32[]{:S(2)}, u32[]{:S(2)}) collective-permute-start(f32[128,256]{1,0:T(8,128)S(1)} %slice_add_fusion.8), channel_id=1, source_target_pairs={{0,16},{8,24},{16,0},{24,8},{1,17},{9,25},{17,1},{25,9},{2,18},{10... | collective-permute-start | bytes 393224 | tf_op jit(solution)/shard_map/ppermute | solution.py:362
  119.9 9.4 %collective-permute-start.25 = (f32[192,256]{1,0:T(8,128)S(1)}, f32[192,256]{1,0:T(8,128)S(1)}, u32[]{:S(2)}, u32[]{:S(2)}) collective-permute-start(f32[192,256]{1,0:T(8,128)S(1)} %pad_maximum_fusion.2), channel_id=1, source_target_pairs={{0,16},{8,24},{16,0},{24,8},{1,17},{9,25},{17,1},{25,9},{2,18},{10... | collective-permute-start | bytes 589832 | tf_op jit(solution)/shard_map/ppermute | solution.py:362
  120.1 11.2 %collective-permute-start.26 = (f32[64,768]{1,0:T(8,128)S(1)}, f32[64,768]{1,0:T(8,128)S(1)}, u32[]{:S(2)}, u32[]{:S(2)}) collective-permute-start(f32[64,768]{1,0:T(8,128)S(1)} %pad_maximum_fusion.3), channel_id=1, source_target_pairs={{0,1},{1,0},{2,3},{3,2},{4,6},{5,7},{6,4},{7,5},{8,9},{9,8},{10,11... | collective-permute-start | bytes 589832 | tf_op jit(solution)/shard_map/ppermute | solution.py:312
  129.3 4.7 %collective-permute-start.27 = (f32[96,256]{1,0:T(8,128)S(1)}, f32[96,256]{1,0:T(8,128)S(1)}, u32[]{:S(2)}, u32[]{:S(2)}) collective-permute-start(f32[96,256]{1,0:T(8,128)S(1)} %pad_maximum_fusion.4), channel_id=1, source_target_pairs={{0,1},{1,0},{2,3},{3,2},{4,6},{5,7},{6,4},{7,5},{8,9},{9,8},{10,11... | collective-permute-start | bytes 294920 | tf_op jit(solution)/shard_map/ppermute | solution.py:312
  (18 other events, 133.4 us)

commit v5 on v4

--- a/solution.py
+++ b/solution.py
@@ -494,13 +494,13 @@
     def gradients(r):
         half = S((width // 2, counts[r] * size), f32)
         keep, send = call(grads_kernel, [half] * 2, [held["left"], line.tie(owns[r]), swapped[r]], f"grads_{r}")
-        line.did(send)
         segments = [[keep]]
         if r == count_rounds - 1:
             whole_state = held["state"]
             middle = whole_state[0].shape[0] // 2
             send = rows_of([send, total_of(whole_state, middle, 2 * middle)])
             segments.append([part[:middle] for part in whole_state])
+        line.did(send)
         came, start = cross(send, sum_bits), 0
         for parts in segments:
             parts.append(came[start:start + parts[0].shape[0]])
@@ -522,19 +522,28 @@
                                [line.tie(ids), node_order, held["keep"], held["came"]], "place")
         line.did(held["tokens"])
 
+    done = {}
+
+    def finish_round(r):
+        halves[r].segments = [list(line.tie(*parts)) for parts in halves[r].segments]
+        done[r], = halves[r].result()
+        line.did(done[r])
+
     def swap_most():
-        held["most"] = [halves[r].result()[0] for r in range(count_rounds - 1)]
+        held["most"] = [done[r] for r in range(count_rounds - 1)]
         message = jnp.concatenate([line.tie(h)[block:] for h in held["most"]], axis=1)
         line.did(message)
         held["swap"] = cross(message, pair_bits)
 
-    steps = [(8.0, turn), (8.5 * count_rounds - 8, back), (8.5 * count_rounds + 1, place_rows)]
+    steps = [(-0.5, turn), (8.5 * count_rounds - 8, back), (8.5 * count_rounds + 1, place_rows)]
     for r in range(count_rounds):
         start = 8.5 * r
-        steps += [(start - 9.5, functools.partial(join, r)), (start, functools.partial(outputs, r)),
+        steps += [(start - (9.5 if r < 2 else 8), functools.partial(join, r)), (start, functools.partial(outputs, r)),
                   (start + 11, functools.partial(gradients, r))]
-        steps += [(start + 23 + 8 * k, lambda r=r: halves[r].hop()) for k in range(order_bits)]
-    steps.append((8.5 * count_rounds + 15 + 8 * order_bits - 7.5, swap_most))
+        steps += [(start + 23 + 10 * k, lambda r=r: halves[r].hop()) for k in range(order_bits)]
+        if r + 1 < count_rounds:
+            steps.append((start + 23 + 10 * order_bits + 2, functools.partial(finish_round, r)))
+    steps.append((8.5 * count_rounds + 15 + 10 * order_bits - 6.5, swap_most))
     for _, step in sorted(steps, key=lambda entry: entry[0]):
         step()
     last, state_sum = halves[count_rounds - 1].result()

time: 136 us -> 128 us (0.941)
  waiting for transfers between devices: 56.4 us -> 45.5 us
  starting transfers between devices: 38.3 us -> 41.6 us
    ppermute x11, waiting for transfers between devices: 20.4 us -> 9.82 us  [cross(): return lax.ppermute(value, ('heads', 'seq'), pairs)]
    ppermute x8, starting transfers between devices: 9.56 us -> 11.5 us  [hop(): came = lax.ppermute(message, axis, flips(axis, bit))]
    ppermute x3, waiting for transfers between devices: 9.46 us -> 7.66 us  [join(): nears[r + 1] = lax.ppermute(following, 'order', flips('order', 0))]
  transfers between devices with their start and end apart: 28 -> 28, of which waited for: 16 -> 13; matrix products, arithmetic and copies ran while one was open for 1% -> 1% of each run, Pallas kernels for 21% -> 22%
where the time goes in v5:
time: 128 us; the launch traced here: 127 us
  waiting for transfers between devices  45.5 us (36%)
  starting transfers between devices  41.6 us (32%)
  Pallas kernels  36.9 us (29%)
    pallas_call x18, Pallas kernels, call(): pl.pallas_call(kernel, out_shape=tuple(outs), grid=(1,), in_specs=in_spec...  36.9 us
    ppermute x8, waiting for transfers between devices, hop(): came = lax.ppermute(message, axis, flips(axis, bit))  26.4 us
    ppermute x11, starting transfers between devices, cross(): return lax.ppermute(value, ('heads', 'seq'), pairs)  15.2 us
    ppermute x8, starting transfers between devices, hop(): came = lax.ppermute(message, axis, flips(axis, bit))  11.5 us
    ppermute x11, waiting for transfers between devices, cross(): return lax.ppermute(value, ('heads', 'seq'), pairs)  9.82 us
    ppermute x4, starting transfers between devices, join(): incoming[r] = (came, lax.ppermute(joined, 'order', flips('order', 1)))  8.98 us
    ppermute x3, waiting for transfers between devices, join(): nears[r + 1] = lax.ppermute(following, 'order', flips('order', 0))  7.66 us
    ppermute x1, starting transfers between devices, per_device(): lax.ppermute(made[8], 'order', flips('order', 0))  3.09 us
  transfers between devices with their start and end apart: 28, of which 13 were waited for; matrix products, arithmetic and copies ran while one was open for 1% of the time, Pallas kernels for 22%

profile of v5, /device:TPU:0, one launch (start us, length us, event | category | flops | bytes accessed | tf_op | source)
XLA Modules:
  0.0 127.3 jit_solution(10931083524347423079)
XLA Ops:
  1.3 7.0 %order.1 = (bf16[512,1024]{1,0:T(8,128)(2,1)}, bf16[512,1024]{1,0:T(8,128)(2,1)}, f32[512,1024]{1,0:T(8,128)}, bf16[512,256]{1,0:T(8,128)(2,1)}, bf16[512,256]{1...) custom-call(s32[6]{0:T(128)} %stack.27.ids, ...), custom_call_target="tpu_custom_call" | custom-call | flops 16000000000 | bytes 1000 | tf_op jit(solution)/shard_map/order/pallas_call | solution.py:392
  8.3 3.1 %collective-permute-start = (f32[264,256]{1,0:T(8,128)}, f32[264,256]{1,0:T(8,128)S(1)}, u32[]{:S(2)}, u32[]{:S(2)}) collective-permute-start(f32[264,256]{1,0:T(8,128)} %get-tuple-element.117.near), channel_id=1, source_target_pairs={{0,8},{8,0},{16,24},{24,16},{1,9},{9,1},{17,25},{25,17},{2,10},{10... | collective-permute-start | bytes 811016 | tf_op jit(solution)/shard_map/ppermute | solution.py:445
  11.4 1.5 %collective-permute-start.2 = (f32[512,1024]{1,0:T(8,128)}, f32[512,1024]{1,0:T(8,128)S(1)}, u32[]{:S(2)}, u32[]{:S(2)}) collective-permute-start(f32[512,1024]{1,0:T(8,128)} %get-tuple-element.121), channel_id=1, source_target_pairs={{0,1},{1,0},{2,3},{3,2},{4,6},{5,7},{6,4},{7,5},{8,9},{9,8},{10,11... | collective-permute-start | bytes 6291464 | tf_op jit(solution)/shard_map/ppermute | solution.py:312
  12.9 8.5 %rest.1 = (bf16[512,256]{1,0:T(8,128)(2,1)}, bf16[512,256]{1,0:T(8,128)(2,1)}, f32[264,256]{1,0:T(8,128)}, bf16[512,256]{1,0:T(8,128)(2,1)}, bf16[512,256]{1,0:T...) custom-call(bf16[512,256]{1,0:T(8,128)(2,1)} %get-tuple-element.110., ...), custom_call_target="tpu_custom_call" | custom-call | flops 16000000000 | bytes 1000 | tf_op jit(solution)/shard_map/rest/pallas_call | solution.py:392
  22.8 2.6 %collective-permute-start.3 = (f32[128,256]{1,0:T(8,128)S(1)}, f32[128,256]{1,0:T(8,128)S(1)}, u32[]{:S(2)}, u32[]{:S(2)}) collective-permute-start(f32[128,256]{1,0:T(8,128)S(1)} %join_0.1), channel_id=1, source_target_pairs={{0,16},{8,24},{16,0},{24,8},{1,17},{9,25},{17,1},{25,9},{2,18},{10... | collective-permute-start | bytes 393224 | tf_op jit(solution)/shard_map/ppermute | solution.py:471
  25.3 7.5 %collective-permute-done.1.came = f32[264,256]{1,0:T(8,128)S(1)} collective-permute-done((f32[264,256]{1,0:T(8,128)S(1)}, f32[264,256]{1,0:T(8,128)S(1)}, u32[]{:S(2)}, u32[]{:S(2)}) %collective-permute-start.1) | collective-permute-done | bytes 270368 | tf_op jit(solution)/shard_map/ppermute | solution.py:474
  34.7 1.9 %collective-permute-start.5 = (f32[264,256]{1,0:T(8,128)S(1)}, f32[264,256]{1,0:T(8,128)S(1)}, u32[]{:S(2)}, u32[]{:S(2)}) collective-permute-start(f32[264,256]{1,0:T(8,128)S(1)} %copy-done.4), channel_id=1, source_target_pairs={{0,8},{8,0},{16,24},{24,16},{1,9},{9,1},{17,25},{25,17},{2,10},{10... | collective-permute-start | bytes 811016 | tf_op jit(solution)/shard_map/ppermute | solution.py:474
  39.0 2.3 %outputs_0.1 = (bf16[512,256]{1,0:T(8,128)(2,1)S(1)}, f32[512,256]{1,0:T(8,128)S(1)}, bf16[512,256]{1,0:T(8,128)(2,1)S(1)}, f32[512,256]{1,0:T(8,128)S(1)}) custom-call(s32[6]{0:T(128)S(1)} %copy-done, bf16[512,256]{1,0:T(8,128)(2,1)S(1)} %copy-done.12, bf16[512,256]{1,0:T(8,128)(2,1)S(1)} %copy-done.13, bf16[512,256]{1,0:T(8,128)(2,1)S(1)} %copy-done.10, ...), custom_call_target="tpu_custom_call" | custom-call | flops 16000000000 | bytes 1000 | tf_op jit(solution)/shard_map/outputs_0/pallas_call | solution.py:392
  41.3 1.6 %collective-permute-start.6 = (f32[512,256]{1,0:T(8,128)S(1)}, f32[512,256]{1,0:T(8,128)S(1)}, u32[]{:S(2)}, u32[]{:S(2)}) collective-permute-start(f32[512,256]{1,0:T(8,128)S(1)} %get-tuple-element.125), channel_id=1, source_target_pairs={{0,1},{1,0},{2,3},{3,2},{4,6},{5,7},{6,4},{7,5},{8,9},{9,8},{10,11... | collective-permute-start | bytes 1572872 | tf_op jit(solution)/shard_map/ppermute | solution.py:312
  42.8 2.3 %outputs_1.1 = (bf16[512,256]{1,0:T(8,128)(2,1)S(1)}, f32[512,256]{1,0:T(8,128)S(1)}, bf16[512,256]{1,0:T(8,128)(2,1)S(1)}, f32[512,256]{1,0:T(8,128)S(1)}) custom-call(s32[6]{0:T(128)S(1)} %copy-done, bf16[512,256]{1,0:T(8,128)(2,1)S(1)} %copy-done.18, bf16[512,256]{1,0:T(8,128)(2,1)S(1)} %copy-done.19, bf16[512,256]{1,0:T(8,128)(2,1)S(1)} %copy-done.10, ...), custom_call_target="tpu_custom_call" | custom-call | flops 16000000000 | bytes 1000 | tf_op jit(solution)/shard_map/outputs_1/pallas_call | solution.py:392
  46.4 2.6 %collective-permute-start.7 = (f32[128,256]{1,0:T(8,128)S(1)}, f32[128,256]{1,0:T(8,128)S(1)}, u32[]{:S(2)}, u32[]{:S(2)}) collective-permute-start(f32[128,256]{1,0:T(8,128)S(1)} %join_2.1), channel_id=1, source_target_pairs={{0,16},{8,24},{16,0},{24,8},{1,17},{9,25},{17,1},{25,9},{2,18},{10... | collective-permute-start | bytes 393224 | tf_op jit(solution)/shard_map/ppermute | solution.py:471
  51.2 1.6 %collective-permute-start.10 = (f32[512,256]{1,0:T(8,128)S(1)}, f32[512,256]{1,0:T(8,128)S(1)}, u32[]{:S(2)}, u32[]{:S(2)}) collective-permute-start(f32[512,256]{1,0:T(8,128)S(1)} %get-tuple-element.135), channel_id=1, source_target_pairs={{0,2},{1,3},{2,0},{3,1},{4,5},{5,4},{6,7},{7,6},{8,10},{9,11},{10,... | collective-permute-start | bytes 1572872 | tf_op jit(solution)/shard_map/ppermute | solution.py:312
  53.6 2.5 %outputs_2.1 = (bf16[512,256]{1,0:T(8,128)(2,1)S(1)}, f32[512,256]{1,0:T(8,128)S(1)}, bf16[512,256]{1,0:T(8,128)(2,1)S(1)}, f32[512,256]{1,0:T(8,128)S(1)}) custom-call(s32[6]{0:T(128)S(1)} %copy-done, bf16[512,256]{1,0:T(8,128)(2,1)S(1)} %copy-done.16, bf16[512,256]{1,0:T(8,128)(2,1)S(1)} %copy-done.17, bf16[512,256]{1,0:T(8,128)(2,1)S(1)} %copy-done.10, ...), custom_call_target="tpu_custom_call" | custom-call | flops 16000000000 | bytes 1000 | tf_op jit(solution)/shard_map/outputs_2/pallas_call | solution.py:392
  56.1 1.6 %collective-permute-start.12 = (f32[512,256]{1,0:T(8,128)S(1)}, f32[512,256]{1,0:T(8,128)S(1)}, u32[]{:S(2)}, u32[]{:S(2)}) collective-permute-start(f32[512,256]{1,0:T(8,128)S(1)} %get-tuple-element.139), channel_id=1, source_target_pairs={{0,1},{1,0},{2,3},{3,2},{4,6},{5,7},{6,4},{7,5},{8,9},{9,8},{10,11... | collective-permute-start | bytes 1572872 | tf_op jit(solution)/shard_map/ppermute | solution.py:312
  58.5 2.6 %collective-permute-start.11 = (f32[128,256]{1,0:T(8,128)S(1)}, f32[128,256]{1,0:T(8,128)S(1)}, u32[]{:S(2)}, u32[]{:S(2)}) collective-permute-start(f32[128,256]{1,0:T(8,128)S(1)} %join_3.1), channel_id=1, source_target_pairs={{0,16},{8,24},{16,0},{24,8},{1,17},{9,25},{17,1},{25,9},{2,18},{10... | collective-permute-start | bytes 393224 | tf_op jit(solution)/shard_map/ppermute | solution.py:471
  61.8 1.6 %collective-permute-start.13 = (f32[512,256]{1,0:T(8,128)S(1)}, f32[512,256]{1,0:T(8,128)S(1)}, u32[]{:S(2)}, u32[]{:S(2)}) collective-permute-start(f32[512,256]{1,0:T(8,128)S(1)} %get-tuple-element.145), channel_id=1, source_target_pairs={{0,2},{1,3},{2,0},{3,1},{4,5},{5,4},{6,7},{7,6},{8,10},{9,11},{10,... | collective-permute-start | bytes 1572872 | tf_op jit(solution)/shard_map/ppermute | solution.py:312
  63.4 1.7 %collective-permute-done.10 = f32[512,256]{1,0:T(8,128)S(1)} collective-permute-done((f32[512,256]{1,0:T(8,128)S(1)}, f32[512,256]{1,0:T(8,128)S(1)}, u32[]{:S(2)}, u32[]{:S(2)}) %collective-permute-start.10) | collective-permute-done | bytes 524320 | tf_op jit(solution)/shard_map/ppermute | solution.py:312
  66.3 2.3 %outputs_3.1 = (bf16[512,256]{1,0:T(8,128)(2,1)S(1)}, f32[512,256]{1,0:T(8,128)S(1)}, bf16[512,256]{1,0:T(8,128)(2,1)S(1)}, f32[512,256]{1,0:T(8,128)S(1)}) custom-call(s32[6]{0:T(128)S(1)} %copy-done, bf16[512,256]{1,0:T(8,128)(2,1)S(1)} %copy-done.14, bf16[512,256]{1,0:T(8,128)(2,1)S(1)} %copy-done.15, bf16[512,256]{1,0:T(8,128)(2,1)S(1)} %copy-done.10, ...), custom_call_target="tpu_custom_call" | custom-call | flops 16000000000 | bytes 1000 | tf_op jit(solution)/shard_map/outputs_3/pallas_call | solution.py:392
  68.6 1.7 %collective-permute-start.16 = (f32[512,256]{1,0:T(8,128)S(1)}, f32[512,256]{1,0:T(8,128)S(1)}, u32[]{:S(2)}, u32[]{:S(2)}) collective-permute-start(f32[512,256]{1,0:T(8,128)S(1)} %get-tuple-element.152), channel_id=1, source_target_pairs={{0,1},{1,0},{2,3},{3,2},{4,6},{5,7},{6,4},{7,5},{8,9},{9,8},{10,11... | collective-permute-start | bytes 1572872 | tf_op jit(solution)/shard_map/ppermute | solution.py:312
  70.3 2.5 %back.1 = (f32[512,512]{1,0:T(8,128)S(1)}, f32[512,256]{1,0:T(8,128)S(1)}, f32[512,768]{1,0:T(8,128)S(1)}) custom-call(s32[6]{0:T(128)S(1)} %copy-done, bf16[512,256]{1,0:T(8,128)(2,1)S(1)} %get-tuple-element.154.refs_0_, bf16[512,256]{1,0:T(8,128)(2,1)S(1)} %get-tuple-element.155.refs_1_, bf16[512,256]{1,0:T(8,128)(2,1)S(1)} %get-tuple-element.156.refs_2_, ...), custom_call_target="tpu_custom_call" | custom-call | flops 16000000000 | bytes 1000 | tf_op jit(solution)/shard_map/back/pallas_call | solution.py:392
  73.6 1.6 %collective-permute-start.17 = (f32[512,256]{1,0:T(8,128)S(1)}, f32[512,256]{1,0:T(8,128)S(1)}, u32[]{:S(2)}, u32[]{:S(2)}) collective-permute-start(f32[512,256]{1,0:T(8,128)S(1)} %get-tuple-element.165), channel_id=1, source_target_pairs={{0,2},{1,3},{2,0},{3,1},{4,5},{5,4},{6,7},{7,6},{8,10},{9,11},{10,... | collective-permute-start | bytes 1572872 | tf_op jit(solution)/shard_map/ppermute | solution.py:312
  76.3 1.8 %place.1 = bf16[512,512]{1,0:T(8,128)(2,1)} custom-call(s32[6]{0:T(128)S(1)} %copy-done, s32[1,512]{1,0:T(1,128)S(1)} %copy-done.7, f32[512,512]{1,0:T(8,128)S(1)} %get-tuple-element.173.keep, f32[512,768]{1,0:T(8,128)S(1)} %collective-permute-done.15.came), custom_call_target="tpu_custom_call" | custom-call | flops 16000000000 | bytes 1000 | tf_op jit(solution)/shard_map/place/pallas_call | solution.py:392
  78.1 2.3 %collective-permute-done.16.came = f32[512,256]{1,0:T(8,128)S(1)} collective-permute-done((f32[512,256]{1,0:T(8,128)S(1)}, f32[512,256]{1,0:T(8,128)S(1)}, u32[]{:S(2)}, u32[]{:S(2)}) %collective-permute-start.16) | collective-permute-done | bytes 524320 | tf_op jit(solution)/shard_map/ppermute | solution.py:312
  81.3 1.6 %collective-permute-start.20 = (f32[768,256]{1,0:T(8,128)S(1)}, f32[768,256]{1,0:T(8,128)S(1)}, u32[]{:S(2)}, u32[]{:S(2)}) collective-permute-start(f32[768,256]{1,0:T(8,128)S(1)} %pad_maximum_fusion), channel_id=1, source_target_pairs={{0,2},{1,3},{2,0},{3,1},{4,5},{5,4},{6,7},{7,6},{8,10},{9,11},{10,... | collective-permute-start | bytes 2359304 | tf_op jit(solution)/shard_map/ppermute | solution.py:312
  82.9 3.1 %collective-permute-start.19 = (f32[128,256]{1,0:T(8,128)S(1)}, f32[128,256]{1,0:T(8,128)S(1)}, u32[]{:S(2)}, u32[]{:S(2)}) collective-permute-start(f32[128,256]{1,0:T(8,128)S(1)} %get-tuple-element.244), channel_id=1, source_target_pairs={{0,16},{8,24},{16,0},{24,8},{1,17},{9,25},{17,1},{25,9},{2,18},{10... | collective-permute-start | bytes 393224 | tf_op jit(solution)/shard_map/ppermute | solution.py:362
  86.1 2.1 %collective-permute-start.21 = (f32[256,256]{1,0:T(8,128)S(1)}, f32[256,256]{1,0:T(8,128)S(1)}, u32[]{:S(2)}, u32[]{:S(2)}) collective-permute-start(f32[256,256]{1,0:T(8,128)S(1)} %get-tuple-element.223), channel_id=1, source_target_pairs={{0,8},{8,0},{16,24},{24,16},{1,9},{9,1},{17,25},{25,17},{2,10},{10... | collective-permute-start | bytes 786440 | tf_op jit(solution)/shard_map/ppermute | solution.py:362
  88.2 6.8 %collective-permute-done.18 = f32[256,256]{1,0:T(8,128)S(1)} collective-permute-done((f32[256,256]{1,0:T(8,128)S(1)}, f32[256,256]{1,0:T(8,128)S(1)}, u32[]{:S(2)}, u32[]{:S(2)}) %collective-permute-start.18) | collective-permute-done | bytes 262176 | tf_op jit(solution)/shard_map/ppermute | solution.py:362
  96.4 2.5 %collective-permute-start.23 = (f32[384,256]{1,0:T(8,128)S(1)}, f32[384,256]{1,0:T(8,128)S(1)}, u32[]{:S(2)}, u32[]{:S(2)}) collective-permute-start(f32[384,256]{1,0:T(8,128)S(1)} %pad_maximum_fusion.1), channel_id=1, source_target_pairs={{0,8},{8,0},{16,24},{24,16},{1,9},{9,1},{17,25},{25,17},{2,10},{10... | collective-permute-start | bytes 1179656 | tf_op jit(solution)/shard_map/ppermute | solution.py:362
  98.9 4.5 %collective-permute-done.21 = f32[256,256]{1,0:T(8,128)S(1)} collective-permute-done((f32[256,256]{1,0:T(8,128)S(1)}, f32[256,256]{1,0:T(8,128)S(1)}, u32[]{:S(2)}, u32[]{:S(2)}) %collective-permute-start.21) | collective-permute-done | bytes 262176 | tf_op jit(solution)/shard_map/ppermute | solution.py:362
  103.6 7.7 %collective-permute-done.23 = f32[384,256]{1,0:T(8,128)S(1)} collective-permute-done((f32[384,256]{1,0:T(8,128)S(1)}, f32[384,256]{1,0:T(8,128)S(1)}, u32[]{:S(2)}, u32[]{:S(2)}) %collective-permute-start.23) | collective-permute-done | bytes 393248 | tf_op jit(solution)/shard_map/ppermute | solution.py:362
  113.7 7.4 %collective-permute-done.25 = f32[192,256]{1,0:T(8,128)S(1)} collective-permute-done((f32[192,256]{1,0:T(8,128)S(1)}, f32[192,256]{1,0:T(8,128)S(1)}, u32[]{:S(2)}, u32[]{:S(2)}) %collective-permute-start.25) | collective-permute-done | bytes 196640 | tf_op jit(solution)/shard_map/ppermute | solution.py:362
  122.3 3.7 %collective-permute-done.27.refs_6_ = f32[96,256]{1,0:T(8,128)S(1)} collective-permute-done((f32[96,256]{1,0:T(8,128)S(1)}, f32[96,256]{1,0:T(8,128)S(1)}, u32[]{:S(2)}, u32[]{:S(2)}) %collective-permute-start.27) | collective-permute-done | bytes 98336 | tf_op jit(solution)/shard_map/ppermute | solution.py:312
  (115 shorter events, 22.3 us)
Async XLA Ops:
  8.3 13.1 %collective-permute-start = (f32[264,256]{1,0:T(8,128)}, f32[264,256]{1,0:T(8,128)S(1)}, u32[]{:S(2)}, u32[]{:S(2)}) collective-permute-start(f32[264,256]{1,0:T(8,128)} %get-tuple-element.117.near), channel_id=1, source_target_pairs={{0,8},{8,0},{16,24},{24,16},{1,9},{9,1},{17,25},{25,17},{2,10},{10... | collective-permute-start | bytes 811016 | tf_op jit(solution)/shard_map/ppermute | solution.py:445
  11.4 26.2 %collective-permute-start.2 = (f32[512,1024]{1,0:T(8,128)}, f32[512,1024]{1,0:T(8,128)S(1)}, u32[]{:S(2)}, u32[]{:S(2)}) collective-permute-start(f32[512,1024]{1,0:T(8,128)} %get-tuple-element.121), channel_id=1, source_target_pairs={{0,1},{1,0},{2,3},{3,2},{4,6},{5,7},{6,4},{7,5},{8,9},{9,8},{10,11... | collective-permute-start | bytes 6291464 | tf_op jit(solution)/shard_map/ppermute | solution.py:312
  12.9 8.5 %copy-start.5 = (f32[264,256]{1,0:T(8,128)S(1)}, f32[264,256]{1,0:T(8,128)}, u32[]{:S(2)}) copy-start(f32[264,256]{1,0:T(8,128)} %get-tuple-element.117.near) | copy-start | bytes 811012
  22.3 12.3 %copy-start.4 = (f32[264,256]{1,0:T(8,128)S(1)}, f32[264,256]{1,0:T(8,128)}, u32[]{:S(2)}) copy-start(f32[264,256]{1,0:T(8,128)} %get-tuple-element.132.near) | copy-start | bytes 811012
  22.3 15.3 %copy-start.8 = (bf16[512,1024]{1,0:T(8,128)(2,1)S(1)}, bf16[512,1024]{1,0:T(8,128)(2,1)}, u32[]{:S(2)}) copy-start(bf16[512,1024]{1,0:T(8,128)(2,1)} %get-tuple-element.113.refs_0_.ordered.refs_10_) | copy-start | bytes 3145732
  22.3 15.3 %copy-start.9 = (bf16[512,1024]{1,0:T(8,128)(2,1)S(1)}, bf16[512,1024]{1,0:T(8,128)(2,1)}, u32[]{:S(2)}) copy-start(bf16[512,1024]{1,0:T(8,128)(2,1)} %get-tuple-element.114.refs_1_.ordered_grad) | copy-start | bytes 3145732
  22.3 10.5 %collective-permute-start.1 = (f32[264,256]{1,0:T(8,128)S(1)}, f32[264,256]{1,0:T(8,128)S(1)}, u32[]{:S(2)}, u32[]{:S(2)}) collective-permute-start(f32[264,256]{1,0:T(8,128)S(1)} %copy-done.6), channel_id=1, source_target_pairs={{0,8},{8,0},{16,24},{24,16},{1,9},{9,1},{17,25},{25,17},{2,10},{10... | collective-permute-start | bytes 811016 | tf_op jit(solution)/shard_map/ppermute | solution.py:474
  22.8 16.1 %collective-permute-start.3 = (f32[128,256]{1,0:T(8,128)S(1)}, f32[128,256]{1,0:T(8,128)S(1)}, u32[]{:S(2)}, u32[]{:S(2)}) collective-permute-start(f32[128,256]{1,0:T(8,128)S(1)} %join_0.1), channel_id=1, source_target_pairs={{0,16},{8,24},{16,0},{24,8},{1,17},{9,25},{17,1},{25,9},{2,18},{10... | collective-permute-start | bytes 393224 | tf_op jit(solution)/shard_map/ppermute | solution.py:471
  33.4 9.4 %collective-permute-start.4 = (f32[128,256]{1,0:T(8,128)S(1)}, f32[128,256]{1,0:T(8,128)S(1)}, u32[]{:S(2)}, u32[]{:S(2)}) collective-permute-start(f32[128,256]{1,0:T(8,128)S(1)} %join_1.1), channel_id=1, source_target_pairs={{0,16},{8,24},{16,0},{24,8},{1,17},{9,25},{17,1},{25,9},{2,18},{10... | collective-permute-start | bytes 393224 | tf_op jit(solution)/shard_map/ppermute | solution.py:471
  34.7 11.2 %collective-permute-start.5 = (f32[264,256]{1,0:T(8,128)S(1)}, f32[264,256]{1,0:T(8,128)S(1)}, u32[]{:S(2)}, u32[]{:S(2)}) collective-permute-start(f32[264,256]{1,0:T(8,128)S(1)} %copy-done.4), channel_id=1, source_target_pairs={{0,8},{8,0},{16,24},{24,16},{1,9},{9,1},{17,25},{25,17},{2,10},{10... | collective-permute-start | bytes 811016 | tf_op jit(solution)/shard_map/ppermute | solution.py:474
  41.3 9.2 %collective-permute-start.6 = (f32[512,256]{1,0:T(8,128)S(1)}, f32[512,256]{1,0:T(8,128)S(1)}, u32[]{:S(2)}, u32[]{:S(2)}) collective-permute-start(f32[512,256]{1,0:T(8,128)S(1)} %get-tuple-element.125), channel_id=1, source_target_pairs={{0,1},{1,0},{2,3},{3,2},{4,6},{5,7},{6,4},{7,5},{8,9},{9,8},{10,11... | collective-permute-start | bytes 1572872 | tf_op jit(solution)/shard_map/ppermute | solution.py:312
  45.2 15.9 %collective-permute-start.9 = (f32[512,256]{1,0:T(8,128)S(1)}, f32[512,256]{1,0:T(8,128)S(1)}, u32[]{:S(2)}, u32[]{:S(2)}) collective-permute-start(f32[512,256]{1,0:T(8,128)S(1)} %get-tuple-element.129), channel_id=1, source_target_pairs={{0,1},{1,0},{2,3},{3,2},{4,6},{5,7},{6,4},{7,5},{8,9},{9,8},{10,11... | collective-permute-start | bytes 1572872 | tf_op jit(solution)/shard_map/ppermute | solution.py:312
  46.4 7.1 %collective-permute-start.7 = (f32[128,256]{1,0:T(8,128)S(1)}, f32[128,256]{1,0:T(8,128)S(1)}, u32[]{:S(2)}, u32[]{:S(2)}) collective-permute-start(f32[128,256]{1,0:T(8,128)S(1)} %join_2.1), channel_id=1, source_target_pairs={{0,16},{8,24},{16,0},{24,8},{1,17},{9,25},{17,1},{25,9},{2,18},{10... | collective-permute-start | bytes 393224 | tf_op jit(solution)/shard_map/ppermute | solution.py:471
  49.0 8.9 %collective-permute-start.8 = (f32[264,256]{1,0:T(8,128)S(1)}, f32[264,256]{1,0:T(8,128)S(1)}, u32[]{:S(2)}, u32[]{:S(2)}) collective-permute-start(f32[264,256]{1,0:T(8,128)S(1)} %copy-done.3), channel_id=1, source_target_pairs={{0,8},{8,0},{16,24},{24,16},{1,9},{9,1},{17,25},{25,17},{2,10},{10... | collective-permute-start | bytes 811016 | tf_op jit(solution)/shard_map/ppermute | solution.py:474
  51.2 13.8 %collective-permute-start.10 = (f32[512,256]{1,0:T(8,128)S(1)}, f32[512,256]{1,0:T(8,128)S(1)}, u32[]{:S(2)}, u32[]{:S(2)}) collective-permute-start(f32[512,256]{1,0:T(8,128)S(1)} %get-tuple-element.135), channel_id=1, source_target_pairs={{0,2},{1,3},{2,0},{3,1},{4,5},{5,4},{6,7},{7,6},{8,10},{9,11},{10,... | collective-permute-start | bytes 1572872 | tf_op jit(solution)/shard_map/ppermute | solution.py:312
  56.1 16.9 %collective-permute-start.12 = (f32[512,256]{1,0:T(8,128)S(1)}, f32[512,256]{1,0:T(8,128)S(1)}, u32[]{:S(2)}, u32[]{:S(2)}) collective-permute-start(f32[512,256]{1,0:T(8,128)S(1)} %get-tuple-element.139), channel_id=1, source_target_pairs={{0,1},{1,0},{2,3},{3,2},{4,6},{5,7},{6,4},{7,5},{8,9},{9,8},{10,11... | collective-permute-start | bytes 1572872 | tf_op jit(solution)/shard_map/ppermute | solution.py:312
  58.5 7.8 %collective-permute-start.11 = (f32[128,256]{1,0:T(8,128)S(1)}, f32[128,256]{1,0:T(8,128)S(1)}, u32[]{:S(2)}, u32[]{:S(2)}) collective-permute-start(f32[128,256]{1,0:T(8,128)S(1)} %join_3.1), channel_id=1, source_target_pairs={{0,16},{8,24},{16,0},{24,8},{1,17},{9,25},{17,1},{25,9},{2,18},{10... | collective-permute-start | bytes 393224 | tf_op jit(solution)/shard_map/ppermute | solution.py:471
  61.8 13.4 %collective-permute-start.13 = (f32[512,256]{1,0:T(8,128)S(1)}, f32[512,256]{1,0:T(8,128)S(1)}, u32[]{:S(2)}, u32[]{:S(2)}) collective-permute-start(f32[512,256]{1,0:T(8,128)S(1)} %get-tuple-element.145), channel_id=1, source_target_pairs={{0,2},{1,3},{2,0},{3,1},{4,5},{5,4},{6,7},{7,6},{8,10},{9,11},{10,... | collective-permute-start | bytes 1572872 | tf_op jit(solution)/shard_map/ppermute | solution.py:312
  65.1 10.2 %collective-permute-start.14 = (f32[256,256]{1,0:T(8,128)S(1)}, f32[256,256]{1,0:T(8,128)S(1)}, u32[]{:S(2)}, u32[]{:S(2)}) collective-permute-start(f32[256,256]{1,0:T(8,128)S(1)} %get-tuple-element.229), channel_id=1, source_target_pairs={{0,8},{8,0},{16,24},{24,16},{1,9},{9,1},{17,25},{25,17},{2,10},{10... | collective-permute-start | bytes 786440 | tf_op jit(solution)/shard_map/ppermute | solution.py:362
  68.6 11.8 %collective-permute-start.16 = (f32[512,256]{1,0:T(8,128)S(1)}, f32[512,256]{1,0:T(8,128)S(1)}, u32[]{:S(2)}, u32[]{:S(2)}) collective-permute-start(f32[512,256]{1,0:T(8,128)S(1)} %get-tuple-element.152), channel_id=1, source_target_pairs={{0,1},{1,0},{2,3},{3,2},{4,6},{5,7},{6,4},{7,5},{8,9},{9,8},{10,11... | collective-permute-start | bytes 1572872 | tf_op jit(solution)/shard_map/ppermute | solution.py:312
  72.8 3.5 %collective-permute-start.15 = (f32[512,768]{1,0:T(8,128)S(1)}, f32[512,768]{1,0:T(8,128)S(1)}, u32[]{:S(2)}, u32[]{:S(2)}) collective-permute-start(f32[512,768]{1,0:T(8,128)S(1)} %get-tuple-element.162), channel_id=1, source_target_pairs={{0,4},{4,0},{1,5},{5,1},{2,6},{6,2},{3,7},{7,3},{8,12},{12,8},{9,1... | collective-permute-start | bytes 4718600 | tf_op jit(solution)/shard_map/ppermute | solution.py:517
  73.6 12.4 %collective-permute-start.17 = (f32[512,256]{1,0:T(8,128)S(1)}, f32[512,256]{1,0:T(8,128)S(1)}, u32[]{:S(2)}, u32[]{:S(2)}) collective-permute-start(f32[512,256]{1,0:T(8,128)S(1)} %get-tuple-element.165), channel_id=1, source_target_pairs={{0,2},{1,3},{2,0},{3,1},{4,5},{5,4},{6,7},{7,6},{8,10},{9,11},{10,... | collective-permute-start | bytes 1572872 | tf_op jit(solution)/shard_map/ppermute | solution.py:312
  81.3 14.8 %collective-permute-start.20 = (f32[768,256]{1,0:T(8,128)S(1)}, f32[768,256]{1,0:T(8,128)S(1)}, u32[]{:S(2)}, u32[]{:S(2)}) collective-permute-start(f32[768,256]{1,0:T(8,128)S(1)} %pad_maximum_fusion), channel_id=1, source_target_pairs={{0,2},{1,3},{2,0},{3,1},{4,5},{5,4},{6,7},{7,6},{8,10},{9,11},{10,... | collective-permute-start | bytes 2359304 | tf_op jit(solution)/shard_map/ppermute | solution.py:312
  82.9 12.1 %collective-permute-start.18 = (f32[256,256]{1,0:T(8,128)S(1)}, f32[256,256]{1,0:T(8,128)S(1)}, u32[]{:S(2)}, u32[]{:S(2)}) collective-permute-start(f32[256,256]{1,0:T(8,128)S(1)} %get-tuple-element.226), channel_id=1, source_target_pairs={{0,8},{8,0},{16,24},{24,16},{1,9},{9,1},{17,25},{25,17},{2,10},{10... | collective-permute-start | bytes 786440 | tf_op jit(solution)/shard_map/ppermute | solution.py:362
  82.9 13.2 %collective-permute-start.19 = (f32[128,256]{1,0:T(8,128)S(1)}, f32[128,256]{1,0:T(8,128)S(1)}, u32[]{:S(2)}, u32[]{:S(2)}) collective-permute-start(f32[128,256]{1,0:T(8,128)S(1)} %get-tuple-element.244), channel_id=1, source_target_pairs={{0,16},{8,24},{16,0},{24,8},{1,17},{9,25},{17,1},{25,9},{2,18},{10... | collective-permute-start | bytes 393224 | tf_op jit(solution)/shard_map/ppermute | solution.py:362
  86.1 17.3 %collective-permute-start.21 = (f32[256,256]{1,0:T(8,128)S(1)}, f32[256,256]{1,0:T(8,128)S(1)}, u32[]{:S(2)}, u32[]{:S(2)}) collective-permute-start(f32[256,256]{1,0:T(8,128)S(1)} %get-tuple-element.223), channel_id=1, source_target_pairs={{0,8},{8,0},{16,24},{24,16},{1,9},{9,1},{17,25},{25,17},{2,10},{10... | collective-permute-start | bytes 786440 | tf_op jit(solution)/shard_map/ppermute | solution.py:362
  95.0 8.5 %collective-permute-start.22 = (f32[128,256]{1,0:T(8,128)S(1)}, f32[128,256]{1,0:T(8,128)S(1)}, u32[]{:S(2)}, u32[]{:S(2)}) collective-permute-start(f32[128,256]{1,0:T(8,128)S(1)} %get-tuple-element.240), channel_id=1, source_target_pairs={{0,16},{8,24},{16,0},{24,8},{1,17},{9,25},{17,1},{25,9},{2,18},{10... | collective-permute-start | bytes 393224 | tf_op jit(solution)/shard_map/ppermute | solution.py:362
  96.4 14.9 %collective-permute-start.23 = (f32[384,256]{1,0:T(8,128)S(1)}, f32[384,256]{1,0:T(8,128)S(1)}, u32[]{:S(2)}, u32[]{:S(2)}) collective-permute-start(f32[384,256]{1,0:T(8,128)S(1)} %pad_maximum_fusion.1), channel_id=1, source_target_pairs={{0,8},{8,0},{16,24},{24,16},{1,9},{9,1},{17,25},{25,17},{2,10},{10... | collective-permute-start | bytes 1179656 | tf_op jit(solution)/shard_map/ppermute | solution.py:362
  103.4 9.4 %collective-permute-start.24 = (f32[128,256]{1,0:T(8,128)S(1)}, f32[128,256]{1,0:T(8,128)S(1)}, u32[]{:S(2)}, u32[]{:S(2)}) collective-permute-start(f32[128,256]{1,0:T(8,128)S(1)} %get-tuple-element.232), channel_id=1, source_target_pairs={{0,16},{8,24},{16,0},{24,8},{1,17},{9,25},{17,1},{25,9},{2,18},{10... | collective-permute-start | bytes 393224 | tf_op jit(solution)/shard_map/ppermute | solution.py:362
  111.4 9.7 %collective-permute-start.25 = (f32[192,256]{1,0:T(8,128)S(1)}, f32[192,256]{1,0:T(8,128)S(1)}, u32[]{:S(2)}, u32[]{:S(2)}) collective-permute-start(f32[192,256]{1,0:T(8,128)S(1)} %pad_maximum_fusion.2), channel_id=1, source_target_pairs={{0,16},{8,24},{16,0},{24,8},{1,17},{9,25},{17,1},{25,9},{2,18},{10... | collective-permute-start | bytes 589832 | tf_op jit(solution)/shard_map/ppermute | solution.py:362
  113.0 9.3 %collective-permute-start.26 = (f32[64,768]{1,0:T(8,128)S(1)}, f32[64,768]{1,0:T(8,128)S(1)}, u32[]{:S(2)}, u32[]{:S(2)}) collective-permute-start(f32[64,768]{1,0:T(8,128)S(1)} %pad_maximum_fusion.3), channel_id=1, source_target_pairs={{0,1},{1,0},{2,3},{3,2},{4,6},{5,7},{6,4},{7,5},{8,9},{9,8},{10,11... | collective-permute-start | bytes 589832 | tf_op jit(solution)/shard_map/ppermute | solution.py:312
  121.3 4.7 %collective-permute-start.27 = (f32[96,256]{1,0:T(8,128)S(1)}, f32[96,256]{1,0:T(8,128)S(1)}, u32[]{:S(2)}, u32[]{:S(2)}) collective-permute-start(f32[96,256]{1,0:T(8,128)S(1)} %pad_maximum_fusion.4), channel_id=1, source_target_pairs={{0,1},{1,0},{2,3},{3,2},{4,6},{5,7},{6,4},{7,5},{8,9},{9,8},{10,11... | collective-permute-start | bytes 294920 | tf_op jit(solution)/shard_map/ppermute | solution.py:312
  (17 other events, 72.6 us)

commit v6 on v5

--- a/solution.py
+++ b/solution.py
@@ -535,7 +535,7 @@
         line.did(message)
         held["swap"] = cross(message, pair_bits)
 
-    steps = [(-0.5, turn), (8.5 * count_rounds - 8, back), (8.5 * count_rounds + 1, place_rows)]
+    steps = [(-0.5, turn), (8.5 * count_rounds - 8, back), (8.5 * count_rounds + 3, place_rows)]
     for r in range(count_rounds):
         start = 8.5 * r
         steps += [(start - (9.5 if r < 2 else 8), functools.partial(join, r)), (start, functools.partial(outputs, r)),

time: 128 us -> 124 us (0.969)
  waiting for transfers between devices: 45.5 us -> 41.2 us
    ppermute x8, waiting for transfers between devices: 26.4 us -> 19.7 us  [hop(): came = lax.ppermute(message, axis, flips(axis, bit))]
    ppermute x11, waiting for transfers between devices: 9.82 us -> 13.1 us  [cross(): return lax.ppermute(value, ('heads', 'seq'), pairs)]
  transfers between devices with their start and end apart: 28 -> 28, of which waited for: 13 -> 13; matrix products, arithmetic and copies ran while one was open for 1% -> 1% of each run, Pallas kernels for 22% -> 23%
where the time goes in v6:
time: 124 us
  starting transfers between devices  42.2 us (34%)
  waiting for transfers between devices  41.2 us (33%)
  Pallas kernels  36.9 us (30%)
    pallas_call x18, Pallas kernels, call(): pl.pallas_call(kernel, out_shape=tuple(outs), grid=(1,), in_specs=in_spec...  36.9 us
    ppermute x8, waiting for transfers between devices, hop(): came = lax.ppermute(message, axis, flips(axis, bit))  19.7 us
    ppermute x11, starting transfers between devices, cross(): return lax.ppermute(value, ('heads', 'seq'), pairs)  16.4 us
    ppermute x11, waiting for transfers between devices, cross(): return lax.ppermute(value, ('heads', 'seq'), pairs)  13.1 us
    ppermute x8, starting transfers between devices, hop(): came = lax.ppermute(message, axis, flips(axis, bit))  10.9 us
    ppermute x4, starting transfers between devices, join(): incoming[r] = (came, lax.ppermute(joined, 'order', flips('order', 1)))  8.97 us
    ppermute x3, waiting for transfers between devices, join(): nears[r + 1] = lax.ppermute(following, 'order', flips('order', 0))  7.67 us
    ppermute x1, starting transfers between devices, per_device(): lax.ppermute(made[8], 'order', flips('order', 0))  3.09 us
  transfers between devices with their start and end apart: 28, of which 13 were waited for; matrix products, arithmetic and copies ran while one was open for 1% of the time, Pallas kernels for 23%

profile of v6, /device:TPU:0, one launch (start us, length us, event | category | flops | bytes accessed | tf_op | source)
XLA Modules:
  0.0 123.6 jit_solution(6225396143528645834)
XLA Ops:
  1.3 7.0 %order.1 = (bf16[512,1024]{1,0:T(8,128)(2,1)}, bf16[512,1024]{1,0:T(8,128)(2,1)}, f32[512,1024]{1,0:T(8,128)}, bf16[512,256]{1,0:T(8,128)(2,1)}, bf16[512,256]{1...) custom-call(s32[6]{0:T(128)} %stack.27.ids, ...), custom_call_target="tpu_custom_call" | custom-call | flops 16000000000 | bytes 1000 | tf_op jit(solution)/shard_map/order/pallas_call | solution.py:392
  8.3 3.1 %collective-permute-start = (f32[264,256]{1,0:T(8,128)}, f32[264,256]{1,0:T(8,128)S(1)}, u32[]{:S(2)}, u32[]{:S(2)}) collective-permute-start(f32[264,256]{1,0:T(8,128)} %get-tuple-element.117.near), channel_id=1, source_target_pairs={{0,8},{8,0},{16,24},{24,16},{1,9},{9,1},{17,25},{25,17},{2,10},{10... | collective-permute-start | bytes 811016 | tf_op jit(solution)/shard_map/ppermute | solution.py:445
  11.4 1.5 %collective-permute-start.2 = (f32[512,1024]{1,0:T(8,128)}, f32[512,1024]{1,0:T(8,128)S(1)}, u32[]{:S(2)}, u32[]{:S(2)}) collective-permute-start(f32[512,1024]{1,0:T(8,128)} %get-tuple-element.121), channel_id=1, source_target_pairs={{0,1},{1,0},{2,3},{3,2},{4,6},{5,7},{6,4},{7,5},{8,9},{9,8},{10,11... | collective-permute-start | bytes 6291464 | tf_op jit(solution)/shard_map/ppermute | solution.py:312
  12.9 8.5 %rest.1 = (bf16[512,256]{1,0:T(8,128)(2,1)}, bf16[512,256]{1,0:T(8,128)(2,1)}, f32[264,256]{1,0:T(8,128)}, bf16[512,256]{1,0:T(8,128)(2,1)}, bf16[512,256]{1,0:T...) custom-call(bf16[512,256]{1,0:T(8,128)(2,1)} %get-tuple-element.110., ...), custom_call_target="tpu_custom_call" | custom-call | flops 16000000000 | bytes 1000 | tf_op jit(solution)/shard_map/rest/pallas_call | solution.py:392
  22.8 2.6 %collective-permute-start.3 = (f32[128,256]{1,0:T(8,128)S(1)}, f32[128,256]{1,0:T(8,128)S(1)}, u32[]{:S(2)}, u32[]{:S(2)}) collective-permute-start(f32[128,256]{1,0:T(8,128)S(1)} %join_0.1), channel_id=1, source_target_pairs={{0,16},{8,24},{16,0},{24,8},{1,17},{9,25},{17,1},{25,9},{2,18},{10... | collective-permute-start | bytes 393224 | tf_op jit(solution)/shard_map/ppermute | solution.py:471
  25.3 7.5 %collective-permute-done.1.came = f32[264,256]{1,0:T(8,128)S(1)} collective-permute-done((f32[264,256]{1,0:T(8,128)S(1)}, f32[264,256]{1,0:T(8,128)S(1)}, u32[]{:S(2)}, u32[]{:S(2)}) %collective-permute-start.1) | collective-permute-done | bytes 270368 | tf_op jit(solution)/shard_map/ppermute | solution.py:474
  34.7 1.9 %collective-permute-start.5 = (f32[264,256]{1,0:T(8,128)S(1)}, f32[264,256]{1,0:T(8,128)S(1)}, u32[]{:S(2)}, u32[]{:S(2)}) collective-permute-start(f32[264,256]{1,0:T(8,128)S(1)} %copy-done.4), channel_id=1, source_target_pairs={{0,8},{8,0},{16,24},{24,16},{1,9},{9,1},{17,25},{25,17},{2,10},{10... | collective-permute-start | bytes 811016 | tf_op jit(solution)/shard_map/ppermute | solution.py:474
  39.0 2.3 %outputs_0.1 = (bf16[512,256]{1,0:T(8,128)(2,1)S(1)}, f32[512,256]{1,0:T(8,128)S(1)}, bf16[512,256]{1,0:T(8,128)(2,1)S(1)}, f32[512,256]{1,0:T(8,128)S(1)}) custom-call(s32[6]{0:T(128)S(1)} %copy-done, bf16[512,256]{1,0:T(8,128)(2,1)S(1)} %copy-done.12, bf16[512,256]{1,0:T(8,128)(2,1)S(1)} %copy-done.13, bf16[512,256]{1,0:T(8,128)(2,1)S(1)} %copy-done.10, ...), custom_call_target="tpu_custom_call" | custom-call | flops 16000000000 | bytes 1000 | tf_op jit(solution)/shard_map/outputs_0/pallas_call | solution.py:392
  41.3 1.6 %collective-permute-start.6 = (f32[512,256]{1,0:T(8,128)S(1)}, f32[512,256]{1,0:T(8,128)S(1)}, u32[]{:S(2)}, u32[]{:S(2)}) collective-permute-start(f32[512,256]{1,0:T(8,128)S(1)} %get-tuple-element.125), channel_id=1, source_target_pairs={{0,1},{1,0},{2,3},{3,2},{4,6},{5,7},{6,4},{7,5},{8,9},{9,8},{10,11... | collective-permute-start | bytes 1572872 | tf_op jit(solution)/shard_map/ppermute | solution.py:312
  42.8 2.3 %outputs_1.1 = (bf16[512,256]{1,0:T(8,128)(2,1)S(1)}, f32[512,256]{1,0:T(8,128)S(1)}, bf16[512,256]{1,0:T(8,128)(2,1)S(1)}, f32[512,256]{1,0:T(8,128)S(1)}) custom-call(s32[6]{0:T(128)S(1)} %copy-done, bf16[512,256]{1,0:T(8,128)(2,1)S(1)} %copy-done.18, bf16[512,256]{1,0:T(8,128)(2,1)S(1)} %copy-done.19, bf16[512,256]{1,0:T(8,128)(2,1)S(1)} %copy-done.10, ...), custom_call_target="tpu_custom_call" | custom-call | flops 16000000000 | bytes 1000 | tf_op jit(solution)/shard_map/outputs_1/pallas_call | solution.py:392
  46.4 2.6 %collective-permute-start.7 = (f32[128,256]{1,0:T(8,128)S(1)}, f32[128,256]{1,0:T(8,128)S(1)}, u32[]{:S(2)}, u32[]{:S(2)}) collective-permute-start(f32[128,256]{1,0:T(8,128)S(1)} %join_2.1), channel_id=1, source_target_pairs={{0,16},{8,24},{16,0},{24,8},{1,17},{9,25},{17,1},{25,9},{2,18},{10... | collective-permute-start | bytes 393224 | tf_op jit(solution)/shard_map/ppermute | solution.py:471
  51.2 1.6 %collective-permute-start.10 = (f32[512,256]{1,0:T(8,128)S(1)}, f32[512,256]{1,0:T(8,128)S(1)}, u32[]{:S(2)}, u32[]{:S(2)}) collective-permute-start(f32[512,256]{1,0:T(8,128)S(1)} %get-tuple-element.135), channel_id=1, source_target_pairs={{0,2},{1,3},{2,0},{3,1},{4,5},{5,4},{6,7},{7,6},{8,10},{9,11},{10,... | collective-permute-start | bytes 1572872 | tf_op jit(solution)/shard_map/ppermute | solution.py:312
  53.6 2.5 %outputs_2.1 = (bf16[512,256]{1,0:T(8,128)(2,1)S(1)}, f32[512,256]{1,0:T(8,128)S(1)}, bf16[512,256]{1,0:T(8,128)(2,1)S(1)}, f32[512,256]{1,0:T(8,128)S(1)}) custom-call(s32[6]{0:T(128)S(1)} %copy-done, bf16[512,256]{1,0:T(8,128)(2,1)S(1)} %copy-done.16, bf16[512,256]{1,0:T(8,128)(2,1)S(1)} %copy-done.17, bf16[512,256]{1,0:T(8,128)(2,1)S(1)} %copy-done.10, ...), custom_call_target="tpu_custom_call" | custom-call | flops 16000000000 | bytes 1000 | tf_op jit(solution)/shard_map/outputs_2/pallas_call | solution.py:392
  56.0 1.6 %collective-permute-start.12 = (f32[512,256]{1,0:T(8,128)S(1)}, f32[512,256]{1,0:T(8,128)S(1)}, u32[]{:S(2)}, u32[]{:S(2)}) collective-permute-start(f32[512,256]{1,0:T(8,128)S(1)} %get-tuple-element.139), channel_id=1, source_target_pairs={{0,1},{1,0},{2,3},{3,2},{4,6},{5,7},{6,4},{7,5},{8,9},{9,8},{10,11... | collective-permute-start | bytes 1572872 | tf_op jit(solution)/shard_map/ppermute | solution.py:312
  58.5 2.6 %collective-permute-start.11 = (f32[128,256]{1,0:T(8,128)S(1)}, f32[128,256]{1,0:T(8,128)S(1)}, u32[]{:S(2)}, u32[]{:S(2)}) collective-permute-start(f32[128,256]{1,0:T(8,128)S(1)} %join_3.1), channel_id=1, source_target_pairs={{0,16},{8,24},{16,0},{24,8},{1,17},{9,25},{17,1},{25,9},{2,18},{10... | collective-permute-start | bytes 393224 | tf_op jit(solution)/shard_map/ppermute | solution.py:471
  61.8 1.6 %collective-permute-start.13 = (f32[512,256]{1,0:T(8,128)S(1)}, f32[512,256]{1,0:T(8,128)S(1)}, u32[]{:S(2)}, u32[]{:S(2)}) collective-permute-start(f32[512,256]{1,0:T(8,128)S(1)} %get-tuple-element.145), channel_id=1, source_target_pairs={{0,2},{1,3},{2,0},{3,1},{4,5},{5,4},{6,7},{7,6},{8,10},{9,11},{10,... | collective-permute-start | bytes 1572872 | tf_op jit(solution)/shard_map/ppermute | solution.py:312
  63.4 1.7 %collective-permute-done.10 = f32[512,256]{1,0:T(8,128)S(1)} collective-permute-done((f32[512,256]{1,0:T(8,128)S(1)}, f32[512,256]{1,0:T(8,128)S(1)}, u32[]{:S(2)}, u32[]{:S(2)}) %collective-permute-start.10) | collective-permute-done | bytes 524320 | tf_op jit(solution)/shard_map/ppermute | solution.py:312
  66.3 2.3 %outputs_3.1 = (bf16[512,256]{1,0:T(8,128)(2,1)S(1)}, f32[512,256]{1,0:T(8,128)S(1)}, bf16[512,256]{1,0:T(8,128)(2,1)S(1)}, f32[512,256]{1,0:T(8,128)S(1)}) custom-call(s32[6]{0:T(128)S(1)} %copy-done, bf16[512,256]{1,0:T(8,128)(2,1)S(1)} %copy-done.14, bf16[512,256]{1,0:T(8,128)(2,1)S(1)} %copy-done.15, bf16[512,256]{1,0:T(8,128)(2,1)S(1)} %copy-done.10, ...), custom_call_target="tpu_custom_call" | custom-call | flops 16000000000 | bytes 1000 | tf_op jit(solution)/shard_map/outputs_3/pallas_call | solution.py:392
  68.6 1.7 %collective-permute-start.15 = (f32[512,256]{1,0:T(8,128)S(1)}, f32[512,256]{1,0:T(8,128)S(1)}, u32[]{:S(2)}, u32[]{:S(2)}) collective-permute-start(f32[512,256]{1,0:T(8,128)S(1)} %get-tuple-element.152), channel_id=1, source_target_pairs={{0,1},{1,0},{2,3},{3,2},{4,6},{5,7},{6,4},{7,5},{8,9},{9,8},{10,11... | collective-permute-start | bytes 1572872 | tf_op jit(solution)/shard_map/ppermute | solution.py:312
  70.3 2.5 %back.1 = (f32[512,512]{1,0:T(8,128)S(1)}, f32[512,256]{1,0:T(8,128)S(1)}, f32[512,768]{1,0:T(8,128)S(1)}) custom-call(s32[6]{0:T(128)S(1)} %copy-done, bf16[512,256]{1,0:T(8,128)(2,1)S(1)} %get-tuple-element.154.refs_0_, bf16[512,256]{1,0:T(8,128)(2,1)S(1)} %get-tuple-element.155.refs_1_, bf16[512,256]{1,0:T(8,128)(2,1)S(1)} %get-tuple-element.156.refs_2_, ...), custom_call_target="tpu_custom_call" | custom-call | flops 16000000000 | bytes 1000 | tf_op jit(solution)/shard_map/back/pallas_call | solution.py:392
  73.6 1.6 %collective-permute-start.17 = (f32[512,256]{1,0:T(8,128)S(1)}, f32[512,256]{1,0:T(8,128)S(1)}, u32[]{:S(2)}, u32[]{:S(2)}) collective-permute-start(f32[512,256]{1,0:T(8,128)S(1)} %get-tuple-element.165), channel_id=1, source_target_pairs={{0,2},{1,3},{2,0},{3,1},{4,5},{5,4},{6,7},{7,6},{8,10},{9,11},{10,... | collective-permute-start | bytes 1572872 | tf_op jit(solution)/shard_map/ppermute | solution.py:312
  76.3 3.3 %collective-permute-start.19 = (f32[128,256]{1,0:T(8,128)S(1)}, f32[128,256]{1,0:T(8,128)S(1)}, u32[]{:S(2)}, u32[]{:S(2)}) collective-permute-start(f32[128,256]{1,0:T(8,128)S(1)} %get-tuple-element.244), channel_id=1, source_target_pairs={{0,16},{8,24},{16,0},{24,8},{1,17},{9,25},{17,1},{25,9},{2,18},{10... | collective-permute-start | bytes 393224 | tf_op jit(solution)/shard_map/ppermute | solution.py:362
  81.3 1.6 %collective-permute-start.20 = (f32[768,256]{1,0:T(8,128)S(1)}, f32[768,256]{1,0:T(8,128)S(1)}, u32[]{:S(2)}, u32[]{:S(2)}) collective-permute-start(f32[768,256]{1,0:T(8,128)S(1)} %pad_maximum_fusion), channel_id=1, source_target_pairs={{0,2},{1,3},{2,0},{3,1},{4,5},{5,4},{6,7},{7,6},{8,10},{9,11},{10,... | collective-permute-start | bytes 2359304 | tf_op jit(solution)/shard_map/ppermute | solution.py:312
  82.9 1.8 %place.1 = bf16[512,512]{1,0:T(8,128)(2,1)} custom-call(s32[6]{0:T(128)S(1)} %copy-done, s32[1,512]{1,0:T(1,128)S(1)} %copy-done.7, f32[512,512]{1,0:T(8,128)S(1)} %get-tuple-element.177.keep, f32[512,768]{1,0:T(8,128)S(1)} %collective-permute-done.16.came), custom_call_target="tpu_custom_call" | custom-call | flops 16000000000 | bytes 1000 | tf_op jit(solution)/shard_map/place/pallas_call | solution.py:392
  85.5 2.6 %collective-permute-start.22 = (f32[128,256]{1,0:T(8,128)S(1)}, f32[128,256]{1,0:T(8,128)S(1)}, u32[]{:S(2)}, u32[]{:S(2)}) collective-permute-start(f32[128,256]{1,0:T(8,128)S(1)} %get-tuple-element.240), channel_id=1, source_target_pairs={{0,16},{8,24},{16,0},{24,8},{1,17},{9,25},{17,1},{25,9},{2,18},{10... | collective-permute-start | bytes 393224 | tf_op jit(solution)/shard_map/ppermute | solution.py:362
  88.2 5.2 %collective-permute-done.20 = f32[768,256]{1,0:T(8,128)S(1)} collective-permute-done((f32[768,256]{1,0:T(8,128)S(1)}, f32[768,256]{1,0:T(8,128)S(1)}, u32[]{:S(2)}, u32[]{:S(2)}) %collective-permute-start.20) | collective-permute-done | bytes 786464 | tf_op jit(solution)/shard_map/ppermute | solution.py:312
  93.7 1.8 %collective-permute-done.21 = f32[256,256]{1,0:T(8,128)S(1)} collective-permute-done((f32[256,256]{1,0:T(8,128)S(1)}, f32[256,256]{1,0:T(8,128)S(1)}, u32[]{:S(2)}, u32[]{:S(2)}) %collective-permute-start.21) | collective-permute-done | bytes 262176 | tf_op jit(solution)/shard_map/ppermute | solution.py:362
  97.0 9.9 %collective-permute-done.23 = f32[384,256]{1,0:T(8,128)S(1)} collective-permute-done((f32[384,256]{1,0:T(8,128)S(1)}, f32[384,256]{1,0:T(8,128)S(1)}, u32[]{:S(2)}, u32[]{:S(2)}) %collective-permute-start.23) | collective-permute-done | bytes 393248 | tf_op jit(solution)/shard_map/ppermute | solution.py:362
  108.4 1.6 %collective-permute-start.26 = (f32[64,768]{1,0:T(8,128)S(1)}, f32[64,768]{1,0:T(8,128)S(1)}, u32[]{:S(2)}, u32[]{:S(2)}) collective-permute-start(f32[64,768]{1,0:T(8,128)S(1)} %pad_maximum_fusion.3), channel_id=1, source_target_pairs={{0,1},{1,0},{2,3},{3,2},{4,6},{5,7},{6,4},{7,5},{8,9},{9,8},{10,11... | collective-permute-start | bytes 589832 | tf_op jit(solution)/shard_map/ppermute | solution.py:312
  109.9 7.5 %collective-permute-done.25 = f32[192,256]{1,0:T(8,128)S(1)} collective-permute-done((f32[192,256]{1,0:T(8,128)S(1)}, f32[192,256]{1,0:T(8,128)S(1)}, u32[]{:S(2)}, u32[]{:S(2)}) %collective-permute-start.25) | collective-permute-done | bytes 196640 | tf_op jit(solution)/shard_map/ppermute | solution.py:362
  117.6 1.5 %collective-permute-start.27 = (f32[96,256]{1,0:T(8,128)S(1)}, f32[96,256]{1,0:T(8,128)S(1)}, u32[]{:S(2)}, u32[]{:S(2)}) collective-permute-start(f32[96,256]{1,0:T(8,128)S(1)} %pad_maximum_fusion.4), channel_id=1, source_target_pairs={{0,1},{1,0},{2,3},{3,2},{4,6},{5,7},{6,4},{7,5},{8,9},{9,8},{10,11... | collective-permute-start | bytes 294920 | tf_op jit(solution)/shard_map/ppermute | solution.py:312
  119.0 3.2 %collective-permute-done.27.refs_6_ = f32[96,256]{1,0:T(8,128)S(1)} collective-permute-done((f32[96,256]{1,0:T(8,128)S(1)}, f32[96,256]{1,0:T(8,128)S(1)}, u32[]{:S(2)}, u32[]{:S(2)}) %collective-permute-start.27) | collective-permute-done | bytes 98336 | tf_op jit(solution)/shard_map/ppermute | solution.py:312
  (115 shorter events, 22.2 us)
Async XLA Ops:
  8.3 13.1 %collective-permute-start = (f32[264,256]{1,0:T(8,128)}, f32[264,256]{1,0:T(8,128)S(1)}, u32[]{:S(2)}, u32[]{:S(2)}) collective-permute-start(f32[264,256]{1,0:T(8,128)} %get-tuple-element.117.near), channel_id=1, source_target_pairs={{0,8},{8,0},{16,24},{24,16},{1,9},{9,1},{17,25},{25,17},{2,10},{10... | collective-permute-start | bytes 811016 | tf_op jit(solution)/shard_map/ppermute | solution.py:445
  11.4 26.2 %collective-permute-start.2 = (f32[512,1024]{1,0:T(8,128)}, f32[512,1024]{1,0:T(8,128)S(1)}, u32[]{:S(2)}, u32[]{:S(2)}) collective-permute-start(f32[512,1024]{1,0:T(8,128)} %get-tuple-element.121), channel_id=1, source_target_pairs={{0,1},{1,0},{2,3},{3,2},{4,6},{5,7},{6,4},{7,5},{8,9},{9,8},{10,11... | collective-permute-start | bytes 6291464 | tf_op jit(solution)/shard_map/ppermute | solution.py:312
  12.9 8.5 %copy-start.5 = (f32[264,256]{1,0:T(8,128)S(1)}, f32[264,256]{1,0:T(8,128)}, u32[]{:S(2)}) copy-start(f32[264,256]{1,0:T(8,128)} %get-tuple-element.117.near) | copy-start | bytes 811012
  22.3 12.3 %copy-start.4 = (f32[264,256]{1,0:T(8,128)S(1)}, f32[264,256]{1,0:T(8,128)}, u32[]{:S(2)}) copy-start(f32[264,256]{1,0:T(8,128)} %get-tuple-element.132.near) | copy-start | bytes 811012
  22.3 15.3 %copy-start.8 = (bf16[512,1024]{1,0:T(8,128)(2,1)S(1)}, bf16[512,1024]{1,0:T(8,128)(2,1)}, u32[]{:S(2)}) copy-start(bf16[512,1024]{1,0:T(8,128)(2,1)} %get-tuple-element.113.refs_0_.ordered.refs_10_) | copy-start | bytes 3145732
  22.3 15.3 %copy-start.9 = (bf16[512,1024]{1,0:T(8,128)(2,1)S(1)}, bf16[512,1024]{1,0:T(8,128)(2,1)}, u32[]{:S(2)}) copy-start(bf16[512,1024]{1,0:T(8,128)(2,1)} %get-tuple-element.114.refs_1_.ordered_grad) | copy-start | bytes 3145732
  22.3 10.5 %collective-permute-start.1 = (f32[264,256]{1,0:T(8,128)S(1)}, f32[264,256]{1,0:T(8,128)S(1)}, u32[]{:S(2)}, u32[]{:S(2)}) collective-permute-start(f32[264,256]{1,0:T(8,128)S(1)} %copy-done.6), channel_id=1, source_target_pairs={{0,8},{8,0},{16,24},{24,16},{1,9},{9,1},{17,25},{25,17},{2,10},{10... | collective-permute-start | bytes 811016 | tf_op jit(solution)/shard_map/ppermute | solution.py:474
  22.8 16.1 %collective-permute-start.3 = (f32[128,256]{1,0:T(8,128)S(1)}, f32[128,256]{1,0:T(8,128)S(1)}, u32[]{:S(2)}, u32[]{:S(2)}) collective-permute-start(f32[128,256]{1,0:T(8,128)S(1)} %join_0.1), channel_id=1, source_target_pairs={{0,16},{8,24},{16,0},{24,8},{1,17},{9,25},{17,1},{25,9},{2,18},{10... | collective-permute-start | bytes 393224 | tf_op jit(solution)/shard_map/ppermute | solution.py:471
  33.4 9.4 %collective-permute-start.4 = (f32[128,256]{1,0:T(8,128)S(1)}, f32[128,256]{1,0:T(8,128)S(1)}, u32[]{:S(2)}, u32[]{:S(2)}) collective-permute-start(f32[128,256]{1,0:T(8,128)S(1)} %join_1.1), channel_id=1, source_target_pairs={{0,16},{8,24},{16,0},{24,8},{1,17},{9,25},{17,1},{25,9},{2,18},{10... | collective-permute-start | bytes 393224 | tf_op jit(solution)/shard_map/ppermute | solution.py:471
  34.7 11.2 %collective-permute-start.5 = (f32[264,256]{1,0:T(8,128)S(1)}, f32[264,256]{1,0:T(8,128)S(1)}, u32[]{:S(2)}, u32[]{:S(2)}) collective-permute-start(f32[264,256]{1,0:T(8,128)S(1)} %copy-done.4), channel_id=1, source_target_pairs={{0,8},{8,0},{16,24},{24,16},{1,9},{9,1},{17,25},{25,17},{2,10},{10... | collective-permute-start | bytes 811016 | tf_op jit(solution)/shard_map/ppermute | solution.py:474
  41.3 9.2 %collective-permute-start.6 = (f32[512,256]{1,0:T(8,128)S(1)}, f32[512,256]{1,0:T(8,128)S(1)}, u32[]{:S(2)}, u32[]{:S(2)}) collective-permute-start(f32[512,256]{1,0:T(8,128)S(1)} %get-tuple-element.125), channel_id=1, source_target_pairs={{0,1},{1,0},{2,3},{3,2},{4,6},{5,7},{6,4},{7,5},{8,9},{9,8},{10,11... | collective-permute-start | bytes 1572872 | tf_op jit(solution)/shard_map/ppermute | solution.py:312
  45.2 15.9 %collective-permute-start.9 = (f32[512,256]{1,0:T(8,128)S(1)}, f32[512,256]{1,0:T(8,128)S(1)}, u32[]{:S(2)}, u32[]{:S(2)}) collective-permute-start(f32[512,256]{1,0:T(8,128)S(1)} %get-tuple-element.129), channel_id=1, source_target_pairs={{0,1},{1,0},{2,3},{3,2},{4,6},{5,7},{6,4},{7,5},{8,9},{9,8},{10,11... | collective-permute-start | bytes 1572872 | tf_op jit(solution)/shard_map/ppermute | solution.py:312
  46.4 7.1 %collective-permute-start.7 = (f32[128,256]{1,0:T(8,128)S(1)}, f32[128,256]{1,0:T(8,128)S(1)}, u32[]{:S(2)}, u32[]{:S(2)}) collective-permute-start(f32[128,256]{1,0:T(8,128)S(1)} %join_2.1), channel_id=1, source_target_pairs={{0,16},{8,24},{16,0},{24,8},{1,17},{9,25},{17,1},{25,9},{2,18},{10... | collective-permute-start | bytes 393224 | tf_op jit(solution)/shard_map/ppermute | solution.py:471
  49.0 8.9 %collective-permute-start.8 = (f32[264,256]{1,0:T(8,128)S(1)}, f32[264,256]{1,0:T(8,128)S(1)}, u32[]{:S(2)}, u32[]{:S(2)}) collective-permute-start(f32[264,256]{1,0:T(8,128)S(1)} %copy-done.3), channel_id=1, source_target_pairs={{0,8},{8,0},{16,24},{24,16},{1,9},{9,1},{17,25},{25,17},{2,10},{10... | collective-permute-start | bytes 811016 | tf_op jit(solution)/shard_map/ppermute | solution.py:474
  51.2 13.8 %collective-permute-start.10 = (f32[512,256]{1,0:T(8,128)S(1)}, f32[512,256]{1,0:T(8,128)S(1)}, u32[]{:S(2)}, u32[]{:S(2)}) collective-permute-start(f32[512,256]{1,0:T(8,128)S(1)} %get-tuple-element.135), channel_id=1, source_target_pairs={{0,2},{1,3},{2,0},{3,1},{4,5},{5,4},{6,7},{7,6},{8,10},{9,11},{10,... | collective-permute-start | bytes 1572872 | tf_op jit(solution)/shard_map/ppermute | solution.py:312
  56.0 16.9 %collective-permute-start.12 = (f32[512,256]{1,0:T(8,128)S(1)}, f32[512,256]{1,0:T(8,128)S(1)}, u32[]{:S(2)}, u32[]{:S(2)}) collective-permute-start(f32[512,256]{1,0:T(8,128)S(1)} %get-tuple-element.139), channel_id=1, source_target_pairs={{0,1},{1,0},{2,3},{3,2},{4,6},{5,7},{6,4},{7,5},{8,9},{9,8},{10,11... | collective-permute-start | bytes 1572872 | tf_op jit(solution)/shard_map/ppermute | solution.py:312
  58.5 7.8 %collective-permute-start.11 = (f32[128,256]{1,0:T(8,128)S(1)}, f32[128,256]{1,0:T(8,128)S(1)}, u32[]{:S(2)}, u32[]{:S(2)}) collective-permute-start(f32[128,256]{1,0:T(8,128)S(1)} %join_3.1), channel_id=1, source_target_pairs={{0,16},{8,24},{16,0},{24,8},{1,17},{9,25},{17,1},{25,9},{2,18},{10... | collective-permute-start | bytes 393224 | tf_op jit(solution)/shard_map/ppermute | solution.py:471
  61.8 13.4 %collective-permute-start.13 = (f32[512,256]{1,0:T(8,128)S(1)}, f32[512,256]{1,0:T(8,128)S(1)}, u32[]{:S(2)}, u32[]{:S(2)}) collective-permute-start(f32[512,256]{1,0:T(8,128)S(1)} %get-tuple-element.145), channel_id=1, source_target_pairs={{0,2},{1,3},{2,0},{3,1},{4,5},{5,4},{6,7},{7,6},{8,10},{9,11},{10,... | collective-permute-start | bytes 1572872 | tf_op jit(solution)/shard_map/ppermute | solution.py:312
  65.1 11.2 %collective-permute-start.14 = (f32[256,256]{1,0:T(8,128)S(1)}, f32[256,256]{1,0:T(8,128)S(1)}, u32[]{:S(2)}, u32[]{:S(2)}) collective-permute-start(f32[256,256]{1,0:T(8,128)S(1)} %get-tuple-element.229), channel_id=1, source_target_pairs={{0,8},{8,0},{16,24},{24,16},{1,9},{9,1},{17,25},{25,17},{2,10},{10... | collective-permute-start | bytes 786440 | tf_op jit(solution)/shard_map/ppermute | solution.py:362
  68.6 11.9 %collective-permute-start.15 = (f32[512,256]{1,0:T(8,128)S(1)}, f32[512,256]{1,0:T(8,128)S(1)}, u32[]{:S(2)}, u32[]{:S(2)}) collective-permute-start(f32[512,256]{1,0:T(8,128)S(1)} %get-tuple-element.152), channel_id=1, source_target_pairs={{0,1},{1,0},{2,3},{3,2},{4,6},{5,7},{6,4},{7,5},{8,9},{9,8},{10,11... | collective-permute-start | bytes 1572872 | tf_op jit(solution)/shard_map/ppermute | solution.py:312
  72.8 8.4 %collective-permute-start.16 = (f32[512,768]{1,0:T(8,128)S(1)}, f32[512,768]{1,0:T(8,128)S(1)}, u32[]{:S(2)}, u32[]{:S(2)}) collective-permute-start(f32[512,768]{1,0:T(8,128)S(1)} %get-tuple-element.162), channel_id=1, source_target_pairs={{0,4},{4,0},{1,5},{5,1},{2,6},{6,2},{3,7},{7,3},{8,12},{12,8},{9,1... | collective-permute-start | bytes 4718600 | tf_op jit(solution)/shard_map/ppermute | solution.py:517
  73.6 11.1 %collective-permute-start.17 = (f32[512,256]{1,0:T(8,128)S(1)}, f32[512,256]{1,0:T(8,128)S(1)}, u32[]{:S(2)}, u32[]{:S(2)}) collective-permute-start(f32[512,256]{1,0:T(8,128)S(1)} %get-tuple-element.165), channel_id=1, source_target_pairs={{0,2},{1,3},{2,0},{3,1},{4,5},{5,4},{6,7},{7,6},{8,10},{9,11},{10,... | collective-permute-start | bytes 1572872 | tf_op jit(solution)/shard_map/ppermute | solution.py:312
  75.3 10.2 %collective-permute-start.18 = (f32[256,256]{1,0:T(8,128)S(1)}, f32[256,256]{1,0:T(8,128)S(1)}, u32[]{:S(2)}, u32[]{:S(2)}) collective-permute-start(f32[256,256]{1,0:T(8,128)S(1)} %get-tuple-element.226), channel_id=1, source_target_pairs={{0,8},{8,0},{16,24},{24,16},{1,9},{9,1},{17,25},{25,17},{2,10},{10... | collective-permute-start | bytes 786440 | tf_op jit(solution)/shard_map/ppermute | solution.py:362
  76.3 11.8 %collective-permute-start.19 = (f32[128,256]{1,0:T(8,128)S(1)}, f32[128,256]{1,0:T(8,128)S(1)}, u32[]{:S(2)}, u32[]{:S(2)}) collective-permute-start(f32[128,256]{1,0:T(8,128)S(1)} %get-tuple-element.244), channel_id=1, source_target_pairs={{0,16},{8,24},{16,0},{24,8},{1,17},{9,25},{17,1},{25,9},{2,18},{10... | collective-permute-start | bytes 393224 | tf_op jit(solution)/shard_map/ppermute | solution.py:362
  81.3 12.1 %collective-permute-start.20 = (f32[768,256]{1,0:T(8,128)S(1)}, f32[768,256]{1,0:T(8,128)S(1)}, u32[]{:S(2)}, u32[]{:S(2)}) collective-permute-start(f32[768,256]{1,0:T(8,128)S(1)} %pad_maximum_fusion), channel_id=1, source_target_pairs={{0,2},{1,3},{2,0},{3,1},{4,5},{5,4},{6,7},{7,6},{8,10},{9,11},{10,... | collective-permute-start | bytes 2359304 | tf_op jit(solution)/shard_map/ppermute | solution.py:312
  84.8 10.7 %collective-permute-start.21 = (f32[256,256]{1,0:T(8,128)S(1)}, f32[256,256]{1,0:T(8,128)S(1)}, u32[]{:S(2)}, u32[]{:S(2)}) collective-permute-start(f32[256,256]{1,0:T(8,128)S(1)} %get-tuple-element.223), channel_id=1, source_target_pairs={{0,8},{8,0},{16,24},{24,16},{1,9},{9,1},{17,25},{25,17},{2,10},{10... | collective-permute-start | bytes 786440 | tf_op jit(solution)/shard_map/ppermute | solution.py:362
  85.5 11.5 %collective-permute-start.22 = (f32[128,256]{1,0:T(8,128)S(1)}, f32[128,256]{1,0:T(8,128)S(1)}, u32[]{:S(2)}, u32[]{:S(2)}) collective-permute-start(f32[128,256]{1,0:T(8,128)S(1)} %get-tuple-element.240), channel_id=1, source_target_pairs={{0,16},{8,24},{16,0},{24,8},{1,17},{9,25},{17,1},{25,9},{2,18},{10... | collective-permute-start | bytes 393224 | tf_op jit(solution)/shard_map/ppermute | solution.py:362
  93.6 13.3 %collective-permute-start.23 = (f32[384,256]{1,0:T(8,128)S(1)}, f32[384,256]{1,0:T(8,128)S(1)}, u32[]{:S(2)}, u32[]{:S(2)}) collective-permute-start(f32[384,256]{1,0:T(8,128)S(1)} %pad_maximum_fusion.1), channel_id=1, source_target_pairs={{0,8},{8,0},{16,24},{24,16},{1,9},{9,1},{17,25},{25,17},{2,10},{10... | collective-permute-start | bytes 1179656 | tf_op jit(solution)/shard_map/ppermute | solution.py:362
  95.6 12.7 %collective-permute-start.24 = (f32[128,256]{1,0:T(8,128)S(1)}, f32[128,256]{1,0:T(8,128)S(1)}, u32[]{:S(2)}, u32[]{:S(2)}) collective-permute-start(f32[128,256]{1,0:T(8,128)S(1)} %get-tuple-element.232), channel_id=1, source_target_pairs={{0,16},{8,24},{16,0},{24,8},{1,17},{9,25},{17,1},{25,9},{2,18},{10... | collective-permute-start | bytes 393224 | tf_op jit(solution)/shard_map/ppermute | solution.py:362
  107.0 10.4 %collective-permute-start.25 = (f32[192,256]{1,0:T(8,128)S(1)}, f32[192,256]{1,0:T(8,128)S(1)}, u32[]{:S(2)}, u32[]{:S(2)}) collective-permute-start(f32[192,256]{1,0:T(8,128)S(1)} %pad_maximum_fusion.2), channel_id=1, source_target_pairs={{0,16},{8,24},{16,0},{24,8},{1,17},{9,25},{17,1},{25,9},{2,18},{10... | collective-permute-start | bytes 589832 | tf_op jit(solution)/shard_map/ppermute | solution.py:362
  108.4 10.7 %collective-permute-start.26 = (f32[64,768]{1,0:T(8,128)S(1)}, f32[64,768]{1,0:T(8,128)S(1)}, u32[]{:S(2)}, u32[]{:S(2)}) collective-permute-start(f32[64,768]{1,0:T(8,128)S(1)} %pad_maximum_fusion.3), channel_id=1, source_target_pairs={{0,1},{1,0},{2,3},{3,2},{4,6},{5,7},{6,4},{7,5},{8,9},{9,8},{10,11... | collective-permute-start | bytes 589832 | tf_op jit(solution)/shard_map/ppermute | solution.py:312
  117.6 4.7 %collective-permute-start.27 = (f32[96,256]{1,0:T(8,128)S(1)}, f32[96,256]{1,0:T(8,128)S(1)}, u32[]{:S(2)}, u32[]{:S(2)}) collective-permute-start(f32[96,256]{1,0:T(8,128)S(1)} %pad_maximum_fusion.4), channel_id=1, source_target_pairs={{0,1},{1,0},{2,3},{3,2},{4,6},{5,7},{6,4},{7,5},{8,9},{9,8},{10,11... | collective-permute-start | bytes 294920 | tf_op jit(solution)/shard_map/ppermute | solution.py:312
  (17 other events, 71.6 us)
